TPU v7x, 32 devices: a whole 2x2x4 slice. The times are simulated.
32 devices in a mesh: tm: 8 (over y, x, core), space: 4 (over z).
Axes of the slice: x: 2, y: 2, z: 4, core: 2. Of those that a mesh axis runs over, the one named last changes fastest.
Arguments:
- q_spatial: bfloat16 [8, 512, 1152], P('tm', 'space'), may hold values from -6 to 6
- k_spatial: bfloat16 [8, 512, 1152], P('tm', 'space'), may hold values from -6 to 6
- v_spatial: bfloat16 [8, 512, 1152], P('tm', 'space'), may hold values from -6 to 6
- grad_spatial: bfloat16 [8, 512, 1152], P('tm', 'space'), may hold values from -192 to 192
- q_temporal: bfloat16 [8, 512, 1152], P('tm', 'space'), may hold values from -6 to 6
- k_temporal: bfloat16 [8, 512, 1152], P('tm', 'space'), may hold values from -6 to 6
- v_temporal: bfloat16 [8, 512, 1152], P('tm', 'space'), may hold values from -6 to 6
- grad_temporal: bfloat16 [8, 512, 1152], P('tm', 'space'), may hold values from -24 to 24
Outputs:
- dq_spatial: bfloat16 [8, 512, 1152], P('tm', 'space')
- dk_spatial: bfloat16 [8, 512, 1152], P('tm', 'space')
- dv_spatial: bfloat16 [8, 512, 1152], P('tm', 'space')
- dq_temporal: bfloat16 [8, 512, 1152], P('tm', 'space')
- dk_temporal: bfloat16 [8, 512, 1152], P('tm', 'space')
- dv_temporal: bfloat16 [8, 512, 1152], P('tm', 'space')
All inputs are finite; a program needn't handle non-finite values.
Results may differ from a plain program's by a relative error of at most 0.012.
The roundings to bfloat16 on the way count: a program that leaves them out, or rounds other values in their place, can miss the bound.
Values may be sent and summed in bfloat16 or wider, within the bound.
No kernel may reach another device: no remote copies, remote signals or barrier semaphores. Data moves between devices by JAX's collectives and lax.ppermute only.
A program may use at most 64 MiB of HBM per device.

v0:
```python
import functools
import math

import jax
import jax.numpy as jnp
from jax import lax
from jax.experimental import pallas as pl
from jax.experimental.pallas import tpu as pltpu
from jax.sharding import PartitionSpec as P

HEAD_DIM = 72
SCALE = 1.0 / math.sqrt(HEAD_DIM)
EXP2_SCALE = SCALE * math.log2(math.e)
LANES = 128
CHUNKS = 1

NT = (((1,), (1,)), ((), ()))
TN = (((0,), (0,)), ((), ()))
VMEM_LIMIT = 48 * 1024 * 1024


def call(kernel, out_shape, *, flops=0, moved=0, exps=0, scratch=()):
    return pl.pallas_call(
        kernel,
        out_shape=out_shape,
        scratch_shapes=list(scratch),
        compiler_params=pltpu.CompilerParams(vmem_limit_bytes=VMEM_LIMIT),
        cost_estimate=pl.CostEstimate(flops=flops, bytes_accessed=moved, transcendentals=exps),
    )


def bf16(*shape):
    return jax.ShapeDtypeStruct(shape, jnp.bfloat16)


def swap(array, axis, distance):
    size = lax.axis_size(axis)
    return lax.ppermute(array, axis, [(i, i ^ distance) for i in range(size)])


def spatial_pack_kernel(group, chunks, *refs):
    sources, outs, scratch = refs[:4], refs[4:-1], refs[-1]
    share = scratch.shape[2]
    for a in range(4):
        turned = sources[a][...].T
        for d in range(group):
            scratch[a, d] = turned[d * share : (d + 1) * share]
    me = lax.axis_index("space")
    rows = share // chunks
    for k in range(group):
        to = me ^ k
        for a in range(4):
            block = scratch[a, to]
            for c in range(chunks):
                outs[k * chunks + c][a * rows : (a + 1) * rows] = block[c * rows : (c + 1) * rows]


def spatial_core_kernel(heads, *refs):
    group = (len(refs)) // 2
    messages, outs = refs[:group], refs[group:]
    whole = jnp.concatenate([m[...] for m in messages], axis=1)
    length = whole.shape[1]
    block = min(512, length)
    per = LANES
    for h in range(heads):
        qs, ks, vs, gs = (
            whole[(a * heads + h) * HEAD_DIM : (a * heads + h + 1) * HEAD_DIM] for a in range(4)
        )
        k_rows, v_rows = ks.T, vs.T
        dk = jnp.zeros((HEAD_DIM, length), jnp.float32)
        dv = jnp.zeros((HEAD_DIM, length), jnp.float32)
        dqs = []
        for b in range(length // block):
            q = qs[:, b * block : (b + 1) * block]
            g = gs[:, b * block : (b + 1) * block]
            s = jnp.dot(k_rows, q, preferred_element_type=jnp.float32)
            e = jnp.exp2((s - jnp.max(s, axis=0, keepdims=True)) * EXP2_SCALE)
            p = e * (1.0 / jnp.sum(e, axis=0, keepdims=True))
            w = p.astype(jnp.bfloat16)
            dp = jnp.dot(v_rows, g, preferred_element_type=jnp.float32)
            delta = jnp.sum(w.astype(jnp.float32) * dp, axis=0, keepdims=True)
            ds = (p * (dp - delta)).astype(jnp.bfloat16)
            dqs.append(jnp.dot(ks, ds, preferred_element_type=jnp.float32))
            dk += lax.dot_general(q, ds, NT, preferred_element_type=jnp.float32)
            dv += lax.dot_general(g, w, NT, preferred_element_type=jnp.float32)
        dq = jnp.concatenate(dqs, axis=1)
        for i, result in enumerate((dq * SCALE, dk * SCALE, dv)):
            low = result.astype(jnp.bfloat16)
            row = (i * heads + h) * HEAD_DIM
            for k in range(group):
                outs[k][row : row + HEAD_DIM] = low[:, k * per : (k + 1) * per]


def spatial_unpack_kernel(group, chunks, *refs):
    messages, outs, scratch = refs[: group * chunks], refs[group * chunks : -1], refs[-1]
    share = scratch.shape[2]
    rows = share // chunks
    me = lax.axis_index("space")
    for k in range(group):
        of = me ^ k
        parts = [messages[k * chunks + c][...] for c in range(chunks)]
        for i in range(3):
            scratch[i, of] = jnp.concatenate([p[i * rows : (i + 1) * rows] for p in parts], axis=0)
    for i in range(3):
        outs[i][...] = scratch[i].reshape(group * share, LANES).T


def spatial(q, k, v, g):
    tokens, width = q.shape
    group = lax.axis_size("space")
    share = width // group
    heads_here = share // HEAD_DIM
    chunks = math.gcd(CHUNKS, heads_here)
    heads = heads_here // chunks
    nbytes = 4 * tokens * width * 2
    packed = call(
        functools.partial(spatial_pack_kernel, group, chunks),
        [bf16(4 * heads * HEAD_DIM, tokens)] * (group * chunks),
        moved=2 * nbytes,
        scratch=[pltpu.VMEM((4, group, share, tokens), jnp.bfloat16)],
    )(q, k, v, g)
    length = group * tokens
    back = [[None] * chunks for _ in range(group)]
    for c in range(chunks):
        arrived = [
            packed[d * chunks + c] if d == 0 else swap(packed[d * chunks + c], "space", d)
            for d in range(group)
        ]
        results = call(
            functools.partial(spatial_core_kernel, heads),
            [bf16(3 * heads * HEAD_DIM, tokens)] * group,
            flops=2 * 5 * heads * length * length * HEAD_DIM,
            exps=heads * length * length,
            moved=7 * heads * HEAD_DIM * length * 2,
        )(*arrived)
        for d in range(group):
            back[d][c] = results[d] if d == 0 else swap(results[d], "space", d)
    return call(
        functools.partial(spatial_unpack_kernel, group, chunks),
        [bf16(tokens, width)] * 3,
        moved=2 * nbytes * 3 // 4,
        scratch=[pltpu.VMEM((3, group, share, tokens), jnp.bfloat16)],
    )(*[m for row in back for m in row])


def temporal_pack_kernel(group, *refs):
    sources, outs = refs[:4], refs[4:]
    me = lax.axis_index("tm")
    rows = outs[0].shape[1]
    for k in range(group):
        start = pl.multiple_of((me ^ k) * rows, rows)
        for a in range(4):
            outs[k][a] = sources[a][pl.ds(start, rows)]


def temporal_core_kernel(*refs):
    group = len(refs) // 2
    messages, outs = refs[:group], refs[group:]
    tok = messages[0].shape[1]
    width = messages[0].shape[2]
    total = group * tok
    arrays = [jnp.concatenate([m[a] for m in messages], axis=0) for a in range(4)]
    row = lax.broadcasted_iota(jnp.int32, (total, total), 0)
    col = lax.broadcasted_iota(jnp.int32, (total, total), 1)
    same = lax.rem(row, tok) == lax.rem(col, tok)
    lane = lax.broadcasted_iota(jnp.int32, (total, LANES), 1)
    tiles = width // LANES
    sums = [[[] for _ in range(tiles)] for _ in range(3)]

    def flush(t):
        for i in range(3):
            left = [x for x, _ in sums[i][t]]
            right = jnp.concatenate([y for _, y in sums[i][t]], axis=0)
            if i == 0:
                lhs = jnp.concatenate(left, axis=0)
                value = lax.dot_general(lhs, right, TN, preferred_element_type=jnp.float32)
            else:
                lhs = jnp.concatenate(left, axis=1)
                value = jnp.dot(lhs, right, preferred_element_type=jnp.float32)
            if i < 2:
                value = value * SCALE
            low = value.astype(jnp.bfloat16)
            for k in range(group):
                outs[k][i, :, t * LANES : (t + 1) * LANES] = low[k * tok : (k + 1) * tok]

    for h in range(width // HEAD_DIM):
        first, last = h * HEAD_DIM, (h + 1) * HEAD_DIM - 1
        span = range(first // LANES, last // LANES + 1)

        def part(a, t, masked=True):
            block = arrays[a][:, t * LANES : (t + 1) * LANES]
            if not masked:
                return block
            lo, hi = first - t * LANES, last - t * LANES
            keep = (lane >= lo) & (lane <= hi)
            return jnp.where(keep, block, jnp.zeros_like(block))

        qm = [part(0, t) for t in span]
        km = [part(1, t) for t in span]
        gm = [part(3, t) for t in span]
        s = lax.dot_general(
            jnp.concatenate(km, axis=1), jnp.concatenate(qm, axis=1), NT, preferred_element_type=jnp.float32
        )
        dp = lax.dot_general(
            jnp.concatenate([part(2, t, False) for t in span], axis=1),
            jnp.concatenate(gm, axis=1),
            NT,
            preferred_element_type=jnp.float32,
        )
        s = jnp.where(same, s, -1e30)
        e = jnp.exp2((s - jnp.max(s, axis=0, keepdims=True)) * EXP2_SCALE)
        p = e * (1.0 / jnp.sum(e, axis=0, keepdims=True))
        w = p.astype(jnp.bfloat16)
        delta = jnp.sum(w.astype(jnp.float32) * dp, axis=0, keepdims=True)
        ds = (p * (dp - delta)).astype(jnp.bfloat16)
        for j, t in enumerate(span):
            sums[0][t].append((ds, km[j]))
            sums[1][t].append((ds, qm[j]))
            sums[2][t].append((w, gm[j]))
            if (t + 1) * LANES <= last + 1:
                flush(t)


def temporal_unpack_kernel(*refs):
    group = len(refs) - 3
    messages, outs = refs[:group], refs[group:]
    me = lax.axis_index("tm")
    rows = messages[0].shape[1]
    for k in range(group):
        start = pl.multiple_of((me ^ k) * rows, rows)
        for i in range(3):
            outs[i][pl.ds(start, rows)] = messages[k][i]


def temporal(q, k, v, g):
    tokens, width = q.shape
    group = lax.axis_size("tm")
    rows = tokens // group
    aligned = rows % 16 == 0
    nbytes = 4 * tokens * width * 2
    partner = lax.axis_index("tm") ^ jnp.arange(group)
    if aligned:
        packed = call(
            functools.partial(temporal_pack_kernel, group),
            [bf16(4, rows, width)] * group,
            moved=2 * nbytes,
        )(q, k, v, g)
    else:
        stacked = jnp.stack([x.reshape(group, rows, width) for x in (q, k, v, g)], axis=1)
        packed = [
            lax.dynamic_index_in_dim(stacked, partner[d], 0, keepdims=False) for d in range(group)
        ]
    arrived = [packed[d] if d == 0 else swap(packed[d], "tm", d) for d in range(group)]
    results = call(
        temporal_core_kernel,
        [bf16(3, rows, width)] * group,
        flops=2 * 5 * 2 * tokens * tokens * width,
        exps=tokens * tokens * width // HEAD_DIM,
        moved=nbytes * 7 // 4,
    )(*arrived)
    back = [results[d] if d == 0 else swap(results[d], "tm", d) for d in range(group)]
    if aligned:
        return call(
            temporal_unpack_kernel, [bf16(tokens, width)] * 3, moved=2 * nbytes * 3 // 4
        )(*back)
    stacked = jnp.take(jnp.stack(back), partner, axis=0)
    return [stacked[:, i].reshape(tokens, width) for i in range(3)]


def shards(*arrays):
    local = [array[0] for array in arrays]
    results = list(spatial(*local[:4])) + list(temporal(*local[4:]))
    return tuple(result[None] for result in results)


def solution(mesh):
    placed = P("tm", "space", None)
    return jax.shard_map(
        shards,
        mesh=mesh,
        in_specs=(placed,) * 8,
        out_specs=(placed,) * 6,
        check_vma=False,
    )
```

profile of v0, /device:TPU:19, one launch (start us, length us, event | category | flops | bytes accessed | tf_op | source)
XLA Modules:
  0.0 69.5 jit_solution(8515514132984465152)
XLA Ops:
  1.6 1.0 %copy-done.1 = bf16[1,128,1152]{2,1,0:T(8,128)(2,1)S(1)} copy-done((bf16[1,128,1152]{2,1,0:T(8,128)(2,1)S(1)}, bf16[1,128,1152]{2,1,0:T(8,128)(2,1)}, u32[]{:S(2)}) %copy-start.1) | copy-done | bytes 294936
  2.6 1.0 %copy-done.2 = bf16[1,128,1152]{2,1,0:T(8,128)(2,1)S(1)} copy-done((bf16[1,128,1152]{2,1,0:T(8,128)(2,1)S(1)}, bf16[1,128,1152]{2,1,0:T(8,128)(2,1)}, u32[]{:S(2)}) %copy-start.2) | copy-done | bytes 294936
  3.5 1.0 %copy-done.3 = bf16[1,128,1152]{2,1,0:T(8,128)(2,1)S(1)} copy-done((bf16[1,128,1152]{2,1,0:T(8,128)(2,1)S(1)}, bf16[1,128,1152]{2,1,0:T(8,128)(2,1)}, u32[]{:S(2)}) %copy-start.3) | copy-done | bytes 294936
  5.6 1.4 %collective-permute-start.8 = (bf16[4,16,1152]{2,1,0:T(8,128)(2,1)S(1)}, bf16[4,16,1152]{2,1,0:T(8,128)(2,1)S(1)}, u32[]{:S(2)}, u32[]{:S(2)}) collective-permute-start(bf16[4,16,1152]{2,1,0:T(8,128)(2,1)S(1)} %get-tuple-element.50), channel_id=1, source_target_pairs={{0,12},{4,8},{8,4},{12,0},{16,28},{20,24},{24,20},{28,16},{1,13},{... | collective-permute-start | bytes 442376 | tf_op jit(solution)/shard_map/ppermute | solution.py:38
  7.1 1.2 %collective-permute-start.9 = (bf16[4,16,1152]{2,1,0:T(8,128)(2,1)S(1)}, bf16[4,16,1152]{2,1,0:T(8,128)(2,1)S(1)}, u32[]{:S(2)}, u32[]{:S(2)}) collective-permute-start(bf16[4,16,1152]{2,1,0:T(8,128)(2,1)S(1)} %get-tuple-element.51), channel_id=1, source_target_pairs={{0,16},{4,20},{8,24},{12,28},{16,0},{20,4},{24,8},{28,12},{1,17},{... | collective-permute-start | bytes 442376 | tf_op jit(solution)/shard_map/ppermute | solution.py:38
  9.4 1.4 %collective-permute-start = (bf16[1152,128]{1,0:T(8,128)(2,1)S(1)}, bf16[1152,128]{1,0:T(8,128)(2,1)S(1)}, u32[]{:S(2)}, u32[]{:S(2)}) collective-permute-start(bf16[1152,128]{1,0:T(8,128)(2,1)S(1)} %get-tuple-element.37), channel_id=1, source_target_pairs={{0,1},{1,0},{2,3},{3,2},{4,5},{5,4},{6,7},{7,6},{8,9},{9,8},{10,11... | collective-permute-start | bytes 884744 | tf_op jit(solution)/shard_map/ppermute | solution.py:38
  10.8 3.6 %collective-permute-done.8.refs_3_ = bf16[4,16,1152]{2,1,0:T(8,128)(2,1)S(1)} collective-permute-done((bf16[4,16,1152]{2,1,0:T(8,128)(2,1)S(1)}, bf16[4,16,1152]{2,1,0:T(8,128)(2,1)S(1)}, u32[]{:S(2)}, u32[]{:S(2)}) %collective-permute-start.8) | collective-permute-done | bytes 147488 | tf_op jit(solution)/shard_map/ppermute | solution.py:38
  14.6 1.2 %collective-permute-start.11 = (bf16[4,16,1152]{2,1,0:T(8,128)(2,1)S(1)}, bf16[4,16,1152]{2,1,0:T(8,128)(2,1)S(1)}, u32[]{:S(2)}, u32[]{:S(2)}) collective-permute-start(bf16[4,16,1152]{2,1,0:T(8,128)(2,1)S(1)} %get-tuple-element.53), channel_id=1, source_target_pairs={{0,24},{4,28},{8,16},{12,20},{16,8},{20,12},{24,0},{28,4},{1,25},{... | collective-permute-start | bytes 442376 | tf_op jit(solution)/shard_map/ppermute | solution.py:38
  16.1 1.6 %collective-permute-start.12 = (bf16[4,16,1152]{2,1,0:T(8,128)(2,1)S(1)}, bf16[4,16,1152]{2,1,0:T(8,128)(2,1)S(1)}, u32[]{:S(2)}, u32[]{:S(2)}) collective-permute-start(bf16[4,16,1152]{2,1,0:T(8,128)(2,1)S(1)} %get-tuple-element.54), channel_id=1, source_target_pairs={{0,28},{4,24},{8,20},{12,16},{16,12},{20,8},{24,4},{28,0},{1,29},{... | collective-permute-start | bytes 442376 | tf_op jit(solution)/shard_map/ppermute | solution.py:38
  17.7 2.7 %collective-permute-done.11.refs_6_ = bf16[4,16,1152]{2,1,0:T(8,128)(2,1)S(1)} collective-permute-done((bf16[4,16,1152]{2,1,0:T(8,128)(2,1)S(1)}, bf16[4,16,1152]{2,1,0:T(8,128)(2,1)S(1)}, u32[]{:S(2)}, u32[]{:S(2)}) %collective-permute-start.11) | collective-permute-done | bytes 147488 | tf_op jit(solution)/shard_map/ppermute | solution.py:38
  20.3 4.2 %collective-permute-done.12.refs_7_ = bf16[4,16,1152]{2,1,0:T(8,128)(2,1)S(1)} collective-permute-done((bf16[4,16,1152]{2,1,0:T(8,128)(2,1)S(1)}, bf16[4,16,1152]{2,1,0:T(8,128)(2,1)S(1)}, u32[]{:S(2)}, u32[]{:S(2)}) %collective-permute-start.12) | collective-permute-done | bytes 147488 | tf_op jit(solution)/shard_map/ppermute | solution.py:38
  24.5 3.4 %shard_map.131 = (bf16[3,16,1152]{2,1,0:T(8,128)(2,1)S(1)}, bf16[3,16,1152]{2,1,0:T(8,128)(2,1)S(1)}, bf16[3,16,1152]{2,1,0:T(8,128)(2,1)S(1)}, bf16[3,16,1152]{...) custom-call(bf16[4,16,1152]{2,1,0:T(8,128)(2,1)S(1)} %get-tuple-elem, ...), custom_call_target="tpu_custom_call" | custom-call | flops 377487360 | bytes 2064384 | tf_op jit(solution)/shard_map/pallas_call | solution.py:254
  28.4 1.7 %collective-permute-start.15 = (bf16[3,16,1152]{2,1,0:T(8,128)(2,1)S(1)}, bf16[3,16,1152]{2,1,0:T(8,128)(2,1)S(1)}, u32[]{:S(2)}, u32[]{:S(2)}) collective-permute-start(bf16[3,16,1152]{2,1,0:T(8,128)(2,1)S(1)} %get-tuple-element.58), channel_id=1, source_target_pairs={{0,12},{4,8},{8,4},{12,0},{16,28},{20,24},{24,20},{28,16},{1,13},{... | collective-permute-start | bytes 331784 | tf_op jit(solution)/shard_map/ppermute | solution.py:38
  30.1 1.2 %collective-permute-start.16 = (bf16[3,16,1152]{2,1,0:T(8,128)(2,1)S(1)}, bf16[3,16,1152]{2,1,0:T(8,128)(2,1)S(1)}, u32[]{:S(2)}, u32[]{:S(2)}) collective-permute-start(bf16[3,16,1152]{2,1,0:T(8,128)(2,1)S(1)} %get-tuple-element.59), channel_id=1, source_target_pairs={{0,16},{4,20},{8,24},{12,28},{16,0},{20,4},{24,8},{28,12},{1,17},{... | collective-permute-start | bytes 331784 | tf_op jit(solution)/shard_map/ppermute | solution.py:38
  31.4 6.7 %collective-permute-done.2.refs_3_ = bf16[1152,128]{1,0:T(8,128)(2,1)S(1)} collective-permute-done((bf16[1152,128]{1,0:T(8,128)(2,1)S(1)}, bf16[1152,128]{1,0:T(8,128)(2,1)S(1)}, u32[]{:S(2)}, u32[]{:S(2)}) %collective-permute-start.2) | collective-permute-done | bytes 294944 | tf_op jit(solution)/shard_map/ppermute | solution.py:38
  38.0 3.3 %collective-permute-start.17 = (bf16[3,16,1152]{2,1,0:T(8,128)(2,1)S(1)}, bf16[3,16,1152]{2,1,0:T(8,128)(2,1)S(1)}, u32[]{:S(2)}, u32[]{:S(2)}) collective-permute-start(bf16[3,16,1152]{2,1,0:T(8,128)(2,1)S(1)} %get-tuple-element.60), channel_id=1, source_target_pairs={{0,20},{4,16},{8,28},{12,24},{16,4},{20,0},{24,12},{28,8},{1,21},{... | collective-permute-start | bytes 331784 | tf_op jit(solution)/shard_map/ppermute | solution.py:38
  41.3 4.8 %shard_map.128 = (bf16[864,128]{1,0:T(8,128)(2,1)S(1)}, bf16[864,128]{1,0:T(8,128)(2,1)S(1)}, bf16[864,128]{1,0:T(8,128)(2,1)S(1)}, bf16[864,128]{1,0:T(8,128)(2,1)S(1)}) custom-call(bf16[1152,128]{1,0:T(8,128)(2,1)S(1)} %get-tuple-element.36.refs_0_, bf16[1152,128]{1,0:T(8,128)(2,1)S(1)} %collective-permute-done.refs_1_, ...), custom_call_target="tpu_custom_call" | custom-call | flops 754974720 | bytes 2064384 | tf_op jit(solution)/shard_map/pallas_call | solution.py:129
  46.6 2.2 %collective-permute-start.5 = (bf16[864,128]{1,0:T(8,128)(2,1)S(1)}, bf16[864,128]{1,0:T(8,128)(2,1)S(1)}, u32[]{:S(2)}, u32[]{:S(2)}) collective-permute-start(bf16[864,128]{1,0:T(8,128)(2,1)S(1)} %get-tuple-element.43), channel_id=1, source_target_pairs={{0,3},{1,2},{2,1},{3,0},{4,7},{5,6},{6,5},{7,4},{8,11},{9,10},{10,... | collective-permute-start | bytes 663560 | tf_op jit(solution)/shard_map/ppermute | solution.py:38
  49.0 2.1 %collective-permute-start.19 = (bf16[3,16,1152]{2,1,0:T(8,128)(2,1)S(1)}, bf16[3,16,1152]{2,1,0:T(8,128)(2,1)S(1)}, u32[]{:S(2)}, u32[]{:S(2)}) collective-permute-start(bf16[3,16,1152]{2,1,0:T(8,128)(2,1)S(1)} %get-tuple-element.62), channel_id=1, source_target_pairs={{0,28},{4,24},{8,20},{12,16},{16,12},{20,8},{24,4},{28,0},{1,29},{... | collective-permute-start | bytes 331784 | tf_op jit(solution)/shard_map/ppermute | solution.py:38
  51.1 3.5 %collective-permute-done.18.refs_6_ = bf16[3,16,1152]{2,1,0:T(8,128)(2,1)S(1)} collective-permute-done((bf16[3,16,1152]{2,1,0:T(8,128)(2,1)S(1)}, bf16[3,16,1152]{2,1,0:T(8,128)(2,1)S(1)}, u32[]{:S(2)}, u32[]{:S(2)}) %collective-permute-start.18) | collective-permute-done | bytes 110624 | tf_op jit(solution)/shard_map/ppermute | solution.py:38
  54.6 2.4 %collective-permute-done.19.refs_7_ = bf16[3,16,1152]{2,1,0:T(8,128)(2,1)S(1)} collective-permute-done((bf16[3,16,1152]{2,1,0:T(8,128)(2,1)S(1)}, bf16[3,16,1152]{2,1,0:T(8,128)(2,1)S(1)}, u32[]{:S(2)}, u32[]{:S(2)}) %collective-permute-start.19) | collective-permute-done | bytes 110624 | tf_op jit(solution)/shard_map/ppermute | solution.py:38
  57.0 1.0 %shard_map.132 = (bf16[128,1152]{1,0:T(8,128)(2,1)}, bf16[128,1152]{1,0:T(8,128)(2,1)}, bf16[128,1152]{1,0:T(8,128)(2,1)}) custom-call(bf16[3,16,1152]{2,1,0:T(8,128)(2,1)S(1)} %get-tuple-element.55.refs_0_, bf16[3,16,1152]{2,1,0:T(8,128)(2,1)S(1)} %collective-permute-done.13.refs_1_, bf16[3,16,1152]{2,1,0:T(8,128)(2,1)S(1)} %collective-permute-done.14.refs_2_, ...), custom_call_target="tpu_custom_call" | custom-call | bytes 1769472 | tf_op jit(solution)/shard_map/pallas_call | solution.py:263
  58.0 10.4 %collective-permute-done.5.refs_3_ = bf16[864,128]{1,0:T(8,128)(2,1)S(1)} collective-permute-done((bf16[864,128]{1,0:T(8,128)(2,1)S(1)}, bf16[864,128]{1,0:T(8,128)(2,1)S(1)}, u32[]{:S(2)}, u32[]{:S(2)}) %collective-permute-start.5) | collective-permute-done | bytes 221216 | tf_op jit(solution)/shard_map/ppermute | solution.py:38
  68.4 1.1 %shard_map.129 = (bf16[128,1152]{1,0:T(8,128)(2,1)}, bf16[128,1152]{1,0:T(8,128)(2,1)}, bf16[128,1152]{1,0:T(8,128)(2,1)}) custom-call(bf16[864,128]{1,0:T(8,128)(2,1)S(1)} %get-tuple-element.40.refs_0_, bf16[864,128]{1,0:T(8,128)(2,1)S(1)} %collective-permute-done.3.refs_1_, bf16[864,128]{1,0:T(8,128)(2,1)S(1)} %collective-permute-done.4.refs_2_, ...), custom_call_target="tpu_custom_call" | custom-call | bytes 1769472 | tf_op jit(solution)/shard_map/pallas_call | solution.py:138
  (38 shorter events, 4.9 us)
Async XLA Ops:
  4.5 4.4 %copy-start.4 = (bf16[1,128,1152]{2,1,0:T(8,128)(2,1)S(1)}, bf16[1,128,1152]{2,1,0:T(8,128)(2,1)}, u32[]{:S(2)}) copy-start(bf16[1,128,1152]{2,1,0:T(8,128)(2,1)} %param.8) | copy-start | bytes 884740
  4.5 4.4 %copy-start.5 = (bf16[1,128,1152]{2,1,0:T(8,128)(2,1)S(1)}, bf16[1,128,1152]{2,1,0:T(8,128)(2,1)}, u32[]{:S(2)}) copy-start(bf16[1,128,1152]{2,1,0:T(8,128)(2,1)} %param.9) | copy-start | bytes 884740
  4.5 4.4 %copy-start.6 = (bf16[1,128,1152]{2,1,0:T(8,128)(2,1)S(1)}, bf16[1,128,1152]{2,1,0:T(8,128)(2,1)}, u32[]{:S(2)}) copy-start(bf16[1,128,1152]{2,1,0:T(8,128)(2,1)} %param.10) | copy-start | bytes 884740
  4.5 4.4 %copy-start.7 = (bf16[1,128,1152]{2,1,0:T(8,128)(2,1)S(1)}, bf16[1,128,1152]{2,1,0:T(8,128)(2,1)}, u32[]{:S(2)}) copy-start(bf16[1,128,1152]{2,1,0:T(8,128)(2,1)} %param.11) | copy-start | bytes 884740
  4.6 4.8 %collective-permute-start.6 = (bf16[4,16,1152]{2,1,0:T(8,128)(2,1)S(1)}, bf16[4,16,1152]{2,1,0:T(8,128)(2,1)S(1)}, u32[]{:S(2)}, u32[]{:S(2)}) collective-permute-start(bf16[4,16,1152]{2,1,0:T(8,128)(2,1)S(1)} %get-tuple-element.48), channel_id=1, source_target_pairs={{0,4},{4,0},{8,12},{12,8},{16,20},{20,16},{24,28},{28,24},{1,5},{5... | collective-permute-start | bytes 442376 | tf_op jit(solution)/shard_map/ppermute | solution.py:38
  5.3 5.4 %collective-permute-start.7 = (bf16[4,16,1152]{2,1,0:T(8,128)(2,1)S(1)}, bf16[4,16,1152]{2,1,0:T(8,128)(2,1)S(1)}, u32[]{:S(2)}, u32[]{:S(2)}) collective-permute-start(bf16[4,16,1152]{2,1,0:T(8,128)(2,1)S(1)} %get-tuple-element.49), channel_id=1, source_target_pairs={{0,8},{4,12},{8,0},{12,4},{16,24},{20,28},{24,16},{28,20},{1,9},{5... | collective-permute-start | bytes 442376 | tf_op jit(solution)/shard_map/ppermute | solution.py:38
  5.6 8.8 %collective-permute-start.8 = (bf16[4,16,1152]{2,1,0:T(8,128)(2,1)S(1)}, bf16[4,16,1152]{2,1,0:T(8,128)(2,1)S(1)}, u32[]{:S(2)}, u32[]{:S(2)}) collective-permute-start(bf16[4,16,1152]{2,1,0:T(8,128)(2,1)S(1)} %get-tuple-element.50), channel_id=1, source_target_pairs={{0,12},{4,8},{8,4},{12,0},{16,28},{20,24},{24,20},{28,16},{1,13},{... | collective-permute-start | bytes 442376 | tf_op jit(solution)/shard_map/ppermute | solution.py:38
  7.1 7.5 %collective-permute-start.9 = (bf16[4,16,1152]{2,1,0:T(8,128)(2,1)S(1)}, bf16[4,16,1152]{2,1,0:T(8,128)(2,1)S(1)}, u32[]{:S(2)}, u32[]{:S(2)}) collective-permute-start(bf16[4,16,1152]{2,1,0:T(8,128)(2,1)S(1)} %get-tuple-element.51), channel_id=1, source_target_pairs={{0,16},{4,20},{8,24},{12,28},{16,0},{20,4},{24,8},{28,12},{1,17},{... | collective-permute-start | bytes 442376 | tf_op jit(solution)/shard_map/ppermute | solution.py:38
  8.3 7.8 %collective-permute-start.10 = (bf16[4,16,1152]{2,1,0:T(8,128)(2,1)S(1)}, bf16[4,16,1152]{2,1,0:T(8,128)(2,1)S(1)}, u32[]{:S(2)}, u32[]{:S(2)}) collective-permute-start(bf16[4,16,1152]{2,1,0:T(8,128)(2,1)S(1)} %get-tuple-element.52), channel_id=1, source_target_pairs={{0,20},{4,16},{8,28},{12,24},{16,4},{20,0},{24,12},{28,8},{1,21},{... | collective-permute-start | bytes 442376 | tf_op jit(solution)/shard_map/ppermute | solution.py:38
  9.4 19.0 %collective-permute-start = (bf16[1152,128]{1,0:T(8,128)(2,1)S(1)}, bf16[1152,128]{1,0:T(8,128)(2,1)S(1)}, u32[]{:S(2)}, u32[]{:S(2)}) collective-permute-start(bf16[1152,128]{1,0:T(8,128)(2,1)S(1)} %get-tuple-element.37), channel_id=1, source_target_pairs={{0,1},{1,0},{2,3},{3,2},{4,5},{5,4},{6,7},{7,6},{8,9},{9,8},{10,11... | collective-permute-start | bytes 884744 | tf_op jit(solution)/shard_map/ppermute | solution.py:38
  10.8 19.4 %collective-permute-start.1 = (bf16[1152,128]{1,0:T(8,128)(2,1)S(1)}, bf16[1152,128]{1,0:T(8,128)(2,1)S(1)}, u32[]{:S(2)}, u32[]{:S(2)}) collective-permute-start(bf16[1152,128]{1,0:T(8,128)(2,1)S(1)} %get-tuple-element.38), channel_id=1, source_target_pairs={{0,2},{1,3},{2,0},{3,1},{4,6},{5,7},{6,4},{7,5},{8,10},{9,11},{10,... | collective-permute-start | bytes 884744 | tf_op jit(solution)/shard_map/ppermute | solution.py:38
  14.4 23.6 %collective-permute-start.2 = (bf16[1152,128]{1,0:T(8,128)(2,1)S(1)}, bf16[1152,128]{1,0:T(8,128)(2,1)S(1)}, u32[]{:S(2)}, u32[]{:S(2)}) collective-permute-start(bf16[1152,128]{1,0:T(8,128)(2,1)S(1)} %get-tuple-element.39), channel_id=1, source_target_pairs={{0,3},{1,2},{2,1},{3,0},{4,7},{5,6},{6,5},{7,4},{8,11},{9,10},{10,... | collective-permute-start | bytes 884744 | tf_op jit(solution)/shard_map/ppermute | solution.py:38
  14.6 5.7 %collective-permute-start.11 = (bf16[4,16,1152]{2,1,0:T(8,128)(2,1)S(1)}, bf16[4,16,1152]{2,1,0:T(8,128)(2,1)S(1)}, u32[]{:S(2)}, u32[]{:S(2)}) collective-permute-start(bf16[4,16,1152]{2,1,0:T(8,128)(2,1)S(1)} %get-tuple-element.53), channel_id=1, source_target_pairs={{0,24},{4,28},{8,16},{12,20},{16,8},{20,12},{24,0},{28,4},{1,25},{... | collective-permute-start | bytes 442376 | tf_op jit(solution)/shard_map/ppermute | solution.py:38
  16.1 8.4 %collective-permute-start.12 = (bf16[4,16,1152]{2,1,0:T(8,128)(2,1)S(1)}, bf16[4,16,1152]{2,1,0:T(8,128)(2,1)S(1)}, u32[]{:S(2)}, u32[]{:S(2)}) collective-permute-start(bf16[4,16,1152]{2,1,0:T(8,128)(2,1)S(1)} %get-tuple-element.54), channel_id=1, source_target_pairs={{0,28},{4,24},{8,20},{12,16},{16,12},{20,8},{24,4},{28,0},{1,29},{... | collective-permute-start | bytes 442376 | tf_op jit(solution)/shard_map/ppermute | solution.py:38
  27.9 18.2 %collective-permute-start.13 = (bf16[3,16,1152]{2,1,0:T(8,128)(2,1)S(1)}, bf16[3,16,1152]{2,1,0:T(8,128)(2,1)S(1)}, u32[]{:S(2)}, u32[]{:S(2)}) collective-permute-start(bf16[3,16,1152]{2,1,0:T(8,128)(2,1)S(1)} %get-tuple-element.56), channel_id=1, source_target_pairs={{0,4},{4,0},{8,12},{12,8},{16,20},{20,16},{24,28},{28,24},{1,5},{5... | collective-permute-start | bytes 331784 | tf_op jit(solution)/shard_map/ppermute | solution.py:38
  28.0 18.2 %collective-permute-start.14 = (bf16[3,16,1152]{2,1,0:T(8,128)(2,1)S(1)}, bf16[3,16,1152]{2,1,0:T(8,128)(2,1)S(1)}, u32[]{:S(2)}, u32[]{:S(2)}) collective-permute-start(bf16[3,16,1152]{2,1,0:T(8,128)(2,1)S(1)} %get-tuple-element.57), channel_id=1, source_target_pairs={{0,8},{4,12},{8,0},{12,4},{16,24},{20,28},{24,16},{28,20},{1,9},{5... | collective-permute-start | bytes 331784 | tf_op jit(solution)/shard_map/ppermute | solution.py:38
  28.4 18.2 %collective-permute-start.15 = (bf16[3,16,1152]{2,1,0:T(8,128)(2,1)S(1)}, bf16[3,16,1152]{2,1,0:T(8,128)(2,1)S(1)}, u32[]{:S(2)}, u32[]{:S(2)}) collective-permute-start(bf16[3,16,1152]{2,1,0:T(8,128)(2,1)S(1)} %get-tuple-element.58), channel_id=1, source_target_pairs={{0,12},{4,8},{8,4},{12,0},{16,28},{20,24},{24,20},{28,16},{1,13},{... | collective-permute-start | bytes 331784 | tf_op jit(solution)/shard_map/ppermute | solution.py:38
  30.1 18.7 %collective-permute-start.16 = (bf16[3,16,1152]{2,1,0:T(8,128)(2,1)S(1)}, bf16[3,16,1152]{2,1,0:T(8,128)(2,1)S(1)}, u32[]{:S(2)}, u32[]{:S(2)}) collective-permute-start(bf16[3,16,1152]{2,1,0:T(8,128)(2,1)S(1)} %get-tuple-element.59), channel_id=1, source_target_pairs={{0,16},{4,20},{8,24},{12,28},{16,0},{20,4},{24,8},{28,12},{1,17},{... | collective-permute-start | bytes 331784 | tf_op jit(solution)/shard_map/ppermute | solution.py:38
  38.0 11.0 %collective-permute-start.17 = (bf16[3,16,1152]{2,1,0:T(8,128)(2,1)S(1)}, bf16[3,16,1152]{2,1,0:T(8,128)(2,1)S(1)}, u32[]{:S(2)}, u32[]{:S(2)}) collective-permute-start(bf16[3,16,1152]{2,1,0:T(8,128)(2,1)S(1)} %get-tuple-element.60), channel_id=1, source_target_pairs={{0,20},{4,16},{8,28},{12,24},{16,4},{20,0},{24,12},{28,8},{1,21},{... | collective-permute-start | bytes 331784 | tf_op jit(solution)/shard_map/ppermute | solution.py:38
  46.1 11.9 %collective-permute-start.3 = (bf16[864,128]{1,0:T(8,128)(2,1)S(1)}, bf16[864,128]{1,0:T(8,128)(2,1)S(1)}, u32[]{:S(2)}, u32[]{:S(2)}) collective-permute-start(bf16[864,128]{1,0:T(8,128)(2,1)S(1)} %get-tuple-element.41), channel_id=1, source_target_pairs={{0,1},{1,0},{2,3},{3,2},{4,5},{5,4},{6,7},{7,6},{8,9},{9,8},{10,11... | collective-permute-start | bytes 663560 | tf_op jit(solution)/shard_map/ppermute | solution.py:38
  46.2 11.8 %collective-permute-start.4 = (bf16[864,128]{1,0:T(8,128)(2,1)S(1)}, bf16[864,128]{1,0:T(8,128)(2,1)S(1)}, u32[]{:S(2)}, u32[]{:S(2)}) collective-permute-start(bf16[864,128]{1,0:T(8,128)(2,1)S(1)} %get-tuple-element.42), channel_id=1, source_target_pairs={{0,2},{1,3},{2,0},{3,1},{4,6},{5,7},{6,4},{7,5},{8,10},{9,11},{10,... | collective-permute-start | bytes 663560 | tf_op jit(solution)/shard_map/ppermute | solution.py:38
  46.6 21.8 %collective-permute-start.5 = (bf16[864,128]{1,0:T(8,128)(2,1)S(1)}, bf16[864,128]{1,0:T(8,128)(2,1)S(1)}, u32[]{:S(2)}, u32[]{:S(2)}) collective-permute-start(bf16[864,128]{1,0:T(8,128)(2,1)S(1)} %get-tuple-element.43), channel_id=1, source_target_pairs={{0,3},{1,2},{2,1},{3,0},{4,7},{5,6},{6,5},{7,4},{8,11},{9,10},{10,... | collective-permute-start | bytes 663560 | tf_op jit(solution)/shard_map/ppermute | solution.py:38
  48.8 5.8 %collective-permute-start.18 = (bf16[3,16,1152]{2,1,0:T(8,128)(2,1)S(1)}, bf16[3,16,1152]{2,1,0:T(8,128)(2,1)S(1)}, u32[]{:S(2)}, u32[]{:S(2)}) collective-permute-start(bf16[3,16,1152]{2,1,0:T(8,128)(2,1)S(1)} %get-tuple-element.61), channel_id=1, source_target_pairs={{0,24},{4,28},{8,16},{12,20},{16,8},{20,12},{24,0},{28,4},{1,25},{... | collective-permute-start | bytes 331784 | tf_op jit(solution)/shard_map/ppermute | solution.py:38
  49.0 8.0 %collective-permute-start.19 = (bf16[3,16,1152]{2,1,0:T(8,128)(2,1)S(1)}, bf16[3,16,1152]{2,1,0:T(8,128)(2,1)S(1)}, u32[]{:S(2)}, u32[]{:S(2)}) collective-permute-start(bf16[3,16,1152]{2,1,0:T(8,128)(2,1)S(1)} %get-tuple-element.62), channel_id=1, source_target_pairs={{0,28},{4,24},{8,20},{12,16},{16,12},{20,8},{24,4},{28,0},{1,29},{... | collective-permute-start | bytes 331784 | tf_op jit(solution)/shard_map/ppermute | solution.py:38
  (4 other events, 3.8 us)
where the time goes:
time: 69.8 us; the launch traced here: 69.5 us
  waiting for transfers between devices  33.7 us (48%)
  starting transfers between devices  20.3 us (29%)
  Pallas kernels  10.9 us (16%)
  local copies, waits for them, and re-layouts  3.85 us (6%)
  between operations  0.74 us (1%)
    ppermute x20, waiting for transfers between devices, swap(): return lax.ppermute(array, axis, [(i, i ^ distance) for i in range(size)])  33.7 us
    ppermute x20, starting transfers between devices, swap(): return lax.ppermute(array, axis, [(i, i ^ distance) for i in range(size)])  20.3 us
    pallas_call x1, Pallas kernels, spatial(): call(functools.partial(spatial_core_kernel, heads), [bf16(3 * heads * HEA...  4.76 us
    unnamed x16, local copies, waits for them, and re-layouts  3.85 us
    pallas_call x1, Pallas kernels, temporal(): call(temporal_core_kernel, [bf16(3, rows, width)] * group, flops=2 * 5 *...  3.41 us
  transfers between devices with their start and end apart: 20, of which 8 were waited for; matrix products, arithmetic and copies ran while one was open for 0% of the time, Pallas kernels for 14%

commit v1 on v0

v1 whole, which is shorter than its diff:
```python
import functools
import math

import jax
import jax.numpy as jnp
from jax import lax
from jax.experimental import pallas as pl
from jax.experimental.pallas import tpu as pltpu
from jax.sharding import PartitionSpec as P

HEAD_DIM = 72
SCALE = 1.0 / math.sqrt(HEAD_DIM)
EXP2_SCALE = SCALE * math.log2(math.e)
LANES = 128
CHUNKS = 2
HOLD = False
HEAD_GROUP = 8
IN_ORDER = "desc"
OUT_ORDER = "desc"
COST = {"core_spatial0": 20, "core_spatial1": 10, "core_temporal": 3, "unpack_spatial": 3, "pack_temporal": 5}
AFTER = 1
LAST = ""
VM = {"pack_spatial": 63}

NT = (((1,), (1,)), ((), ()))
TN = (((0,), (0,)), ((), ()))
VMEM_LIMIT = 48 * 1024 * 1024


def call(name, kernel, out_shape, *, us=1.0, scratch=(), **specs):
    return pl.pallas_call(
        kernel,
        out_shape=out_shape,
        scratch_shapes=list(scratch),
        **specs,
        name=name,
        compiler_params=pltpu.CompilerParams(vmem_limit_bytes=VM.get(name, 48) * 1024 * 1024),
        cost_estimate=pl.CostEstimate(
            flops=int(COST.get(name, us) * 1e9), bytes_accessed=1024, transcendentals=0
        ),
    )


def bf16(*shape):
    return jax.ShapeDtypeStruct(shape, jnp.bfloat16)


def swap(array, axis, distance):
    size = lax.axis_size(axis)
    return lax.ppermute(array, axis, [(i, i ^ distance) for i in range(size)])


def spatial_pack_kernel(group, chunks, *refs):
    sources, outs, token = refs[:4], refs[4:-4], refs[-4]
    scratch, staged, sems = refs[-3:]
    share = scratch.shape[2]
    copies = [
        pltpu.make_async_copy(sources[a].at[0], staged.at[a], sems.at[a]) for a in range(4)
    ]
    for copy in copies:
        copy.start()
    token[...] = jnp.zeros_like(token)
    for a in range(4):
        copies[a].wait()
        turned = staged[a].T
        for d in range(group):
            scratch[a, d] = turned[d * share : (d + 1) * share]
    me = lax.axis_index("space")
    rows = share // chunks
    for k in range(group):
        to = me ^ k
        for a in range(4):
            block = scratch[a, to]
            for c in range(chunks):
                outs[k * chunks + c][a * rows : (a + 1) * rows] = block[c * rows : (c + 1) * rows]


def spatial_core_kernel(heads, *refs):
    group = (len(refs)) // 2
    messages, outs = refs[:group], refs[group:]
    whole = jnp.concatenate([m[...] for m in messages], axis=1)
    length = whole.shape[1]
    block = min(512, length)
    per = length // group
    every = range(heads)

    def mm(x, y):
        return jnp.dot(x, y, preferred_element_type=jnp.float32)

    def nt(x, y):
        return lax.dot_general(x, y, NT, preferred_element_type=jnp.float32)

    qs, ks, vs, gs = (
        [whole[(a * heads + h) * HEAD_DIM : (a * heads + h + 1) * HEAD_DIM] for h in every]
        for a in range(4)
    )
    k_rows = [x.T for x in ks]
    v_rows = [x.T for x in vs]
    dk = [jnp.zeros((HEAD_DIM, length), jnp.float32)] * heads
    dv = [jnp.zeros((HEAD_DIM, length), jnp.float32)] * heads
    dqs = [[] for h in every]
    for b in range(length // block):
        q = [x[:, b * block : (b + 1) * block] for x in qs]
        g = [x[:, b * block : (b + 1) * block] for x in gs]
        s = [mm(x, y) for x, y in zip(k_rows, q)]
        dp = [mm(x, y) for x, y in zip(v_rows, g)]
        for h in every:
            e = jnp.exp2((s[h] - jnp.max(s[h], axis=0, keepdims=True)) * EXP2_SCALE)
            p = e * (1.0 / jnp.sum(e, axis=0, keepdims=True))
            w = p.astype(jnp.bfloat16)
            delta = jnp.sum(w.astype(jnp.float32) * dp[h], axis=0, keepdims=True)
            ds = (p * (dp[h] - delta)).astype(jnp.bfloat16)
            dqs[h].append(mm(ks[h], ds))
            dk[h] += nt(q[h], ds)
            dv[h] += nt(g[h], w)
    for h in every:
        dq = jnp.concatenate(dqs[h], axis=1)
        for i, result in enumerate((dq * SCALE, dk[h] * SCALE, dv[h])):
            low = result.astype(jnp.bfloat16)
            row = (i * heads + h) * HEAD_DIM
            for k in range(group):
                outs[k][row : row + HEAD_DIM] = low[:, k * per : (k + 1) * per]


def spatial_unpack_kernel(places, chunks, *refs):
    group = len(places)
    messages, outs, scratch = refs[: group * chunks], refs[group * chunks : -1], refs[-1]
    share = scratch.shape[2]
    rows = share // chunks
    me = lax.axis_index("space")
    for k, d in enumerate(places):
        of = me ^ d
        parts = [messages[c * group + k][...] for c in range(chunks)]
        for i in range(3):
            scratch[i, of] = jnp.concatenate([p[i * rows : (i + 1) * rows] for p in parts], axis=0)
    for i in range(3):
        outs[i][...] = scratch[i].reshape(group * share, LANES).T


def spatial_send(q, k, v, g):
    _, tokens, width = q.shape
    group = lax.axis_size("space")
    share = width // group
    heads_here = share // HEAD_DIM
    chunks = math.gcd(CHUNKS, heads_here)
    heads = heads_here // chunks
    *packed, token = call(
        "pack_spatial",
        functools.partial(spatial_pack_kernel, group, chunks),
        [bf16(4 * heads * HEAD_DIM, tokens)] * (group * chunks) + [bf16(16, LANES)],
        in_specs=[pl.BlockSpec(memory_space=pltpu.HBM)] * 4,
        scratch=[
            pltpu.VMEM((4, group, share, tokens), jnp.bfloat16),
            pltpu.VMEM((4, tokens, width), jnp.bfloat16),
            pltpu.SemaphoreType.DMA((4,)),
        ],
    )(q, k, v, g)
    arrived = []
    for c in range(chunks):
        far = [swap(packed[d * chunks + c], "space", d) for d in range(group - 1, 0, -1)]
        arrived.append([packed[c]] + far[::-1])
    return arrived, token


def order(kind, group):
    far = list(range(1, group))
    if kind == "desc":
        far = far[::-1]
    elif kind != "asc" and len(kind) == group - 1:
        far = [int(c) for c in kind]
    return [0] + far


def spatial_core(arrived, first):
    if not arrived:
        return []
    group = len(arrived[0])
    places = order(IN_ORDER, group)
    rows, tokens = arrived[0][0].shape
    heads = rows // (4 * HEAD_DIM)
    length = group * tokens
    results = []
    for c, messages in enumerate(arrived):
        results.append(
            call(
            f"core_spatial{first + c}",
            functools.partial(spatial_core_kernel, heads),
            [bf16(3 * heads * HEAD_DIM, tokens)] * group,
            us=1.2 * heads * (length / 512) ** 2,
        )(*[messages[d] for d in places])
        )
    return [[chunk[places.index(d)] for d in range(group)] for chunk in results]


def spatial_return(results, width):
    chunks, group = len(results), len(results[0])
    tokens = results[0][0].shape[1]
    places = order(OUT_ORDER, group)
    back = []
    for mine in results:
        far = [swap(mine[d], "space", d) for d in range(group - 1, 0, -1)]
        back.append([mine[0]] + far[::-1])
    return call(
        "unpack_spatial",
        functools.partial(spatial_unpack_kernel, places, chunks),
        [bf16(tokens, width)] * 3,
        scratch=[pltpu.VMEM((3, group, width // group, tokens), jnp.bfloat16)],
    )(*[back[c][d] for c in range(chunks) for d in places]), back


def temporal_pack_kernel(q, k, v, g, token, out):
    group, _, rows, _ = out.shape
    for t in range(group):
        for a, source in enumerate((q, k, v, g)):
            out[t, a] = source[0, t * rows : (t + 1) * rows]


def temporal_core_kernel(messages, token, out):
    group, _, tok, width = messages.shape
    total = group * tok
    arrays = [
        jnp.concatenate([messages[t, a] for t in range(group)], axis=0) for a in range(4)
    ]
    row = lax.broadcasted_iota(jnp.int32, (total, total), 0)
    col = lax.broadcasted_iota(jnp.int32, (total, total), 1)
    same = lax.rem(row, tok) == lax.rem(col, tok)
    lane = lax.broadcasted_iota(jnp.int32, (total, LANES), 1)
    tiles = width // LANES
    sums = [[[] for _ in range(tiles)] for _ in range(3)]

    def flush(t):
        for i in range(3):
            left = [x for x, _ in sums[i][t]]
            right = jnp.concatenate([y for _, y in sums[i][t]], axis=0)
            if i == 0:
                lhs = jnp.concatenate(left, axis=0)
                value = lax.dot_general(lhs, right, TN, preferred_element_type=jnp.float32)
            else:
                lhs = jnp.concatenate(left, axis=1)
                value = jnp.dot(lhs, right, preferred_element_type=jnp.float32)
            if i < 2:
                value = value * SCALE
            low = value.astype(jnp.bfloat16)
            for k in range(group):
                out[k, i, :, t * LANES : (t + 1) * LANES] = low[k * tok : (k + 1) * tok]

    def part(a, h, t, masked=True):
        block = arrays[a][:, t * LANES : (t + 1) * LANES]
        if not masked:
            return block
        low = h * HEAD_DIM - t * LANES
        keep = (lane >= low) & (lane < low + HEAD_DIM)
        return jnp.where(keep, block, jnp.zeros_like(block))

    def wide(parts):
        return jnp.concatenate(parts, axis=1)

    heads = width // HEAD_DIM
    for start in range(0, heads, HEAD_GROUP):
        batch = range(start, min(start + HEAD_GROUP, heads))
        spans = [range(h * HEAD_DIM // LANES, ((h + 1) * HEAD_DIM - 1) // LANES + 1) for h in batch]
        qm = [[part(0, h, t) for t in span] for h, span in zip(batch, spans)]
        km = [[part(1, h, t) for t in span] for h, span in zip(batch, spans)]
        gm = [[part(3, h, t) for t in span] for h, span in zip(batch, spans)]
        vs = [[part(2, h, t, False) for t in span] for h, span in zip(batch, spans)]
        s = [
            lax.dot_general(wide(x), wide(y), NT, preferred_element_type=jnp.float32)
            for x, y in zip(km, qm)
        ]
        dp = [
            lax.dot_general(wide(x), wide(y), NT, preferred_element_type=jnp.float32)
            for x, y in zip(vs, gm)
        ]
        s = [jnp.where(same, x, -1e30) for x in s]
        e = [jnp.exp2((x - jnp.max(x, axis=0, keepdims=True)) * EXP2_SCALE) for x in s]
        p = [x * (1.0 / jnp.sum(x, axis=0, keepdims=True)) for x in e]
        w = [x.astype(jnp.bfloat16) for x in p]
        delta = [
            jnp.sum(x.astype(jnp.float32) * y, axis=0, keepdims=True) for x, y in zip(w, dp)
        ]
        ds = [(x * (y - z)).astype(jnp.bfloat16) for x, y, z in zip(p, dp, delta)]
        for n, h in enumerate(batch):
            for j, t in enumerate(spans[n]):
                sums[0][t].append((ds[n], km[n][j]))
                sums[1][t].append((ds[n], qm[n][j]))
                sums[2][t].append((w[n], gm[n][j]))
                if (t + 1) * LANES <= (h + 1) * HEAD_DIM:
                    flush(t)


def temporal_unpack_kernel(*refs):
    messages, outs, sems = refs[0], refs[-4:-1], refs[-1]
    group, _, rows, _ = messages.shape
    copies = [
        pltpu.make_async_copy(
            messages.at[t, i], outs[i].at[0, t * rows : (t + 1) * rows], sems.at[t, i]
        )
        for i in range(3)
        for t in range(group)
    ]
    for copy in copies:
        copy.start()
    for copy in copies:
        copy.wait()


def temporal_send(q, k, v, g, token):
    _, tokens, width = q.shape
    group = lax.axis_size("tm")
    rows = tokens // group
    if rows % 16 == 0:
        packed = call(
            "pack_temporal",
            temporal_pack_kernel,
            bf16(group, 4, rows, width),
            in_specs=[pl.BlockSpec(memory_space=pltpu.VMEM)] * 4
            + [pl.BlockSpec(memory_space=pl.ANY)],
        )(q, k, v, g, token)
    else:
        packed = jnp.stack([x.reshape(group, rows, width) for x in (q, k, v, g)], axis=1)
    return lax.all_to_all(packed, "tm", 0, 0, tiled=True)


def temporal_core(arrived, token):
    group, _, rows, width = arrived.shape
    return call(
        "core_temporal",
        temporal_core_kernel,
        bf16(group, 3, rows, width),
        us=3.4,
        in_specs=[pl.BlockSpec(memory_space=pltpu.VMEM), pl.BlockSpec(memory_space=pl.ANY)],
    )(arrived, token)


def temporal_return(results, last):
    group, _, rows, width = results.shape
    arrived = lax.all_to_all(results, "tm", 0, 0, tiled=True)
    if rows % 16 == 0:
        return call(
            "unpack_temporal",
            temporal_unpack_kernel,
            [bf16(1, group * rows, width)] * 3,
            in_specs=[pl.BlockSpec(memory_space=pl.ANY)] * (1 + len(last)),
            out_specs=[pl.BlockSpec(memory_space=pltpu.HBM)] * 3,
            scratch=[pltpu.SemaphoreType.DMA((group, 3))],
        )(arrived, *last)
    return [arrived[:, i].reshape(1, group * rows, width) for i in range(3)]


def shards(*arrays):
    width = arrays[0].shape[2]
    spatial_in, token = spatial_send(*arrays[:4])
    temporal_in = temporal_send(*arrays[4:], token)
    cut = len(spatial_in) if AFTER is None else min(AFTER, len(spatial_in))
    spatial_out = spatial_core(spatial_in[:cut], 0)
    temporal_out = temporal_core(temporal_in, spatial_out[-1][0] if cut else token)
    if cut < len(spatial_in):
        if HOLD:
            spatial_in[cut][0], _ = lax.optimization_barrier((spatial_in[cut][0], temporal_out))
        spatial_out += spatial_core(spatial_in[cut:], cut)
    spatial_grads, zback = spatial_return(spatial_out, width)
    last = {"uz": spatial_grads[:1], "z1": zback[0][1:2], "z12": zback[0][1:3], "z13": zback[0][1:4:2], "": []}[LAST]
    temporal_grads = temporal_return(temporal_out, last)
    return tuple(x[None] for x in spatial_grads) + tuple(temporal_grads)


def solution(mesh):
    placed = P("tm", "space", None)
    return jax.shard_map(
        shards,
        mesh=mesh,
        in_specs=(placed,) * 8,
        out_specs=(placed,) * 6,
        check_vma=False,
    )
```

time: 69.8 us -> 61.1 us (0.88)
  the two profiles are of different devices: /device:TPU:19 before, /device:TPU:0 now
where the time goes in v1:
time: 61.1 us; the launch traced here: 60.8 us
  starting transfers between devices  25.9 us (42%)
  waiting for transfers between devices  19.5 us (32%)
  Pallas kernels  13 us (21%)
  local copies, waits for them, and re-layouts  1.66 us (3%)
  between operations  0.73 us (1%)
    ppermute x12, starting transfers between devices, swap(): return lax.ppermute(array, axis, [(i, i ^ distance) for i in range(size)])  18.3 us
    ppermute x12, waiting for transfers between devices, swap(): return lax.ppermute(array, axis, [(i, i ^ distance) for i in range(size)])  16.6 us
    pallas_call x2, Pallas kernels, spatial_core(): call(f'core_spatial{first + c}', functools.partial(spatial_core_kernel, h...  4.34 us
    all_to_all x1, starting transfers between devices, temporal_send(): return lax.all_to_all(packed, 'tm', 0, 0, tiled=True)  3.85 us
    all_to_all x1, starting transfers between devices, temporal_return(): arrived = lax.all_to_all(results, 'tm', 0, 0, tiled=True)  3.68 us
    all_to_all x1, waiting for transfers between devices, temporal_send(): return lax.all_to_all(packed, 'tm', 0, 0, tiled=True)  2.96 us
    pallas_call x1, Pallas kernels, spatial_send(): call('pack_spatial', functools.partial(spatial_pack_kernel, group, chunks...  2.64 us
    pallas_call x1, Pallas kernels, temporal_core(): call('core_temporal', temporal_core_kernel, bf16(group, 3, rows, width),...  2.53 us
  transfers between devices with their start and end apart: 14, of which 4 were waited for; matrix products, arithmetic and copies ran while one was open for 0% of the time, Pallas kernels for 15%

profile of v1, /device:TPU:0, one launch (start us, length us, event | category | flops | bytes accessed | tf_op | source)
XLA Modules:
  0.0 60.8 jit_solution(12552166804094341566)
XLA Ops:
  0.7 2.6 %pack_spatial.1 = (bf16[576,128]{1,0:T(8,128)(2,1)}, bf16[576,128]{1,0:T(8,128)(2,1)}, bf16[576,128]{1,0:T(8,128)(2,1)}, bf16[576,128]{1,0:T(8,128)(2,1)}, bf16[...) custom-call(bf16[1,128,1152]{2,1,0:T(8,128)(2,1)} %refs_0_.1, ...), custom_call_target="tpu_custom_call" | custom-call | flops 1000000000 | bytes 1024 | tf_op jit(solution)/shard_map/pack_spatial/pallas_call | solution.py:147
  3.3 5.1 %collective-permute-start = (bf16[576,128]{1,0:T(8,128)(2,1)}, bf16[576,128]{1,0:T(8,128)(2,1)S(1)}, u32[]{:S(2)}, u32[]{:S(2)}) collective-permute-start(bf16[576,128]{1,0:T(8,128)(2,1)} %get-tuple-element.30), channel_id=1, source_target_pairs={{0,3},{1,2},{2,1},{3,0},{4,7},{5,6},{6,5},{7,4},{8,11},{9,10},{10,... | collective-permute-start | bytes 442376 | tf_op jit(solution)/shard_map/ppermute | solution.py:50
  8.4 0.6 %collective-permute-start.2 = (bf16[576,128]{1,0:T(8,128)(2,1)}, bf16[576,128]{1,0:T(8,128)(2,1)S(1)}, u32[]{:S(2)}, u32[]{:S(2)}) collective-permute-start(bf16[576,128]{1,0:T(8,128)(2,1)} %get-tuple-element.32), channel_id=1, source_target_pairs={{0,1},{1,0},{2,3},{3,2},{4,5},{5,4},{6,7},{7,6},{8,9},{9,8},{10,11... | collective-permute-start | bytes 442376 | tf_op jit(solution)/shard_map/ppermute | solution.py:50
  9.1 3.7 %collective-permute-start.6 = (bf16[576,128]{1,0:T(8,128)(2,1)}, bf16[576,128]{1,0:T(8,128)(2,1)S(1)}, u32[]{:S(2)}, u32[]{:S(2)}) collective-permute-start(bf16[576,128]{1,0:T(8,128)(2,1)} %get-tuple-element.38), channel_id=1, source_target_pairs={{0,3},{1,2},{2,1},{3,0},{4,7},{5,6},{6,5},{7,4},{8,11},{9,10},{10,... | collective-permute-start | bytes 442376 | tf_op jit(solution)/shard_map/ppermute | solution.py:50
  12.8 0.0 copy-start.3
  12.9 1.0 %copy-done.3 = bf16[1,128,1152]{2,1,0:T(8,128)(2,1)S(1)} copy-done((bf16[1,128,1152]{2,1,0:T(8,128)(2,1)S(1)}, bf16[1,128,1152]{2,1,0:T(8,128)(2,1)}, u32[]{:S(2)}) %copy-start.3) | copy-done | bytes 294936
  13.8 0.7 %copy-done.6 = bf16[16,128]{1,0:T(8,128)(2,1)S(1)} copy-done((bf16[16,128]{1,0:T(8,128)(2,1)S(1)}, bf16[16,128]{1,0:T(8,128)(2,1)}, u32[]{:S(2)}) %copy-start.6) | copy-done | bytes 4120
  14.5 1.1 %pack_temporal.1 = bf16[8,4,16,1152]{3,2,1,0:T(8,128)(2,1)} custom-call(bf16[1,128,1152]{2,1,0:T(8,128)(2,1)S(1)} %copy-done, bf16[1,128,1152]{2,1,0:T(8,128)(2,1)S(1)} %copy-done.1, bf16[1,128,1152]{2,1,0:T(8,128)(2,1)S(1)} %copy-done.2, bf16[1,128,1152]{2,1,0:T(8,128)(2,1)S(1)} %copy-done.3, bf16[16,128]{1,0:T(8,128)(2,1)S(1)} %copy-done.6), custom_call_target="tpu_custom_call" | custom-call | flops 5000000000 | bytes 1024 | tf_op jit(solution)/shard_map/pack_temporal/pallas_call | solution.py:312
  15.6 3.9 %all-to-all-start = ((bf16[8,4,16,1152]{3,2,1,0:T(8,128)(2,1)}), bf16[8,4,16,1152]{3,2,1,0:T(8,128)(2,1)S(1)}, u32[]{:S(2)}, u32[]{:S(2)}) async-start(bf16[8,4,16,1152]{3,2,1,0:T(8,128)(2,1)} %pack_temporal.1), calls=%async_computation | async-start | bytes 2359296 | tf_op jit(solution)/shard_map/all_to_all | solution.py:321
  19.5 0.8 %collective-permute-start.8 = (bf16[576,128]{1,0:T(8,128)(2,1)S(1)}, bf16[576,128]{1,0:T(8,128)(2,1)S(1)}, u32[]{:S(2)}, u32[]{:S(2)}) collective-permute-start(bf16[576,128]{1,0:T(8,128)(2,1)S(1)} %copy-done.7), channel_id=1, source_target_pairs={{0,1},{1,0},{2,3},{3,2},{4,5},{5,4},{6,7},{7,6},{8,9},{9,8},{10,11... | collective-permute-start | bytes 442376 | tf_op jit(solution)/shard_map/ppermute | solution.py:50
  20.3 8.1 %collective-permute-done.1.refs_2_ = bf16[576,128]{1,0:T(8,128)(2,1)S(1)} collective-permute-done((bf16[576,128]{1,0:T(8,128)(2,1)}, bf16[576,128]{1,0:T(8,128)(2,1)S(1)}, u32[]{:S(2)}, u32[]{:S(2)}) %collective-permute-start.1) | collective-permute-done | bytes 147488 | tf_op jit(solution)/shard_map/ppermute | solution.py:50
  28.5 2.2 %core_spatial0.1 = (bf16[432,128]{1,0:T(8,128)(2,1)S(1)}, bf16[432,128]{1,0:T(8,128)(2,1)S(1)}, bf16[432,128]{1,0:T(8,128)(2,1)S(1)}, bf16[432,128]{1,0:T(8,128)(2,1)S(1)}) custom-call(bf16[576,128]{1,0:T(8,128)(2,1)S(1)} %copy-done.5, bf16[576,128]{1,0:T(8,128)(2,1)S(1)} %collective-permute-done.refs_1_, ...), custom_call_target="tpu_custom_call" | custom-call | flops 20000000000 | bytes 1024 | tf_op jit(solution)/shard_map/core_spatial0/pallas_call | solution.py:185
  30.6 2.7 %collective-permute-start.3 = (bf16[432,128]{1,0:T(8,128)(2,1)S(1)}, bf16[432,128]{1,0:T(8,128)(2,1)S(1)}, u32[]{:S(2)}, u32[]{:S(2)}) collective-permute-start(bf16[432,128]{1,0:T(8,128)(2,1)S(1)} %get-tuple-element.34), channel_id=1, source_target_pairs={{0,3},{1,2},{2,1},{3,0},{4,7},{5,6},{6,5},{7,4},{8,11},{9,10},{10,... | collective-permute-start | bytes 331784 | tf_op jit(solution)/shard_map/ppermute | solution.py:50
  33.3 3.0 %all-to-all-done.messages = bf16[8,4,16,1152]{3,2,1,0:T(8,128)(2,1)S(1)} async-done(((bf16[8,4,16,1152]{3,2,1,0:T(8,128)(2,1)}), bf16[8,4,16,1152]{3,2,1,0:T(8,128)(2,1)S(1)}, u32[]{:S(2)}, u32[]{:S(2)}) %all-to-all-start) | async-done | bytes 1179680 | tf_op jit(solution)/shard_map/all_to_all | solution.py:321
  36.3 2.5 %core_temporal.1 = bf16[8,3,16,1152]{3,2,1,0:T(8,128)(2,1)} custom-call(bf16[8,4,16,1152]{3,2,1,0:T(8,128)(2,1)S(1)} %all-to-all-done.messages, bf16[432,128]{1,0:T(8,128)(2,1)S(1)} %get-tuple-element.33.refs_0_.token), custom_call_target="tpu_custom_call" | custom-call | flops 3000000000 | bytes 1024 | tf_op jit(solution)/shard_map/core_temporal/pallas_call | solution.py:326
  38.8 3.7 %all-to-all-start.1 = ((bf16[8,3,16,1152]{3,2,1,0:T(8,128)(2,1)}), bf16[8,3,16,1152]{3,2,1,0:T(8,128)(2,1)S(1)}, u32[]{:S(2)}, u32[]{:S(2)}) async-start(bf16[8,3,16,1152]{3,2,1,0:T(8,128)(2,1)} %core_temporal.1), calls=%async_computation.1 | async-start | bytes 1769472 | tf_op jit(solution)/shard_map/all_to_all | solution.py:337
  42.5 0.8 %collective-permute-start.5 = (bf16[432,128]{1,0:T(8,128)(2,1)S(1)}, bf16[432,128]{1,0:T(8,128)(2,1)S(1)}, u32[]{:S(2)}, u32[]{:S(2)}) collective-permute-start(bf16[432,128]{1,0:T(8,128)(2,1)S(1)} %get-tuple-element.36), channel_id=1, source_target_pairs={{0,1},{1,0},{2,3},{3,2},{4,5},{5,4},{6,7},{7,6},{8,9},{9,8},{10,11... | collective-permute-start | bytes 331784 | tf_op jit(solution)/shard_map/ppermute | solution.py:50
  43.4 2.2 %core_spatial1.1 = (bf16[432,128]{1,0:T(8,128)(2,1)S(1)}, bf16[432,128]{1,0:T(8,128)(2,1)S(1)}, bf16[432,128]{1,0:T(8,128)(2,1)S(1)}, bf16[432,128]{1,0:T(8,128)(2,1)S(1)}) custom-call(bf16[576,128]{1,0:T(8,128)(2,1)S(1)} %copy-done.4, bf16[576,128]{1,0:T(8,128)(2,1)S(1)} %collective-permute-done.6.refs_1_, ...), custom_call_target="tpu_custom_call" | custom-call | flops 10000000000 | bytes 1024 | tf_op jit(solution)/shard_map/core_spatial1/pallas_call | solution.py:185
  45.6 3.7 %collective-permute-start.9 = (bf16[432,128]{1,0:T(8,128)(2,1)S(1)}, bf16[432,128]{1,0:T(8,128)(2,1)S(1)}, u32[]{:S(2)}, u32[]{:S(2)}) collective-permute-start(bf16[432,128]{1,0:T(8,128)(2,1)S(1)} %get-tuple-element.42), channel_id=1, source_target_pairs={{0,3},{1,2},{2,1},{3,0},{4,7},{5,6},{6,5},{7,4},{8,11},{9,10},{10,... | collective-permute-start | bytes 331784 | tf_op jit(solution)/shard_map/ppermute | solution.py:50
  49.2 0.8 %collective-permute-start.11 = (bf16[432,128]{1,0:T(8,128)(2,1)S(1)}, bf16[432,128]{1,0:T(8,128)(2,1)S(1)}, u32[]{:S(2)}, u32[]{:S(2)}) collective-permute-start(bf16[432,128]{1,0:T(8,128)(2,1)S(1)} %get-tuple-element.44), channel_id=1, source_target_pairs={{0,1},{1,0},{2,3},{3,2},{4,5},{5,4},{6,7},{7,6},{8,9},{9,8},{10,11... | collective-permute-start | bytes 331784 | tf_op jit(solution)/shard_map/ppermute | solution.py:50
  50.0 3.4 %collective-permute-done.9.refs_5_ = bf16[432,128]{1,0:T(8,128)(2,1)S(1)} collective-permute-done((bf16[432,128]{1,0:T(8,128)(2,1)S(1)}, bf16[432,128]{1,0:T(8,128)(2,1)S(1)}, u32[]{:S(2)}, u32[]{:S(2)}) %collective-permute-start.9) | collective-permute-done | bytes 110624 | tf_op jit(solution)/shard_map/ppermute | solution.py:50
  53.4 5.0 %collective-permute-done.10.refs_6_ = bf16[432,128]{1,0:T(8,128)(2,1)S(1)} collective-permute-done((bf16[432,128]{1,0:T(8,128)(2,1)S(1)}, bf16[432,128]{1,0:T(8,128)(2,1)S(1)}, u32[]{:S(2)}, u32[]{:S(2)}) %collective-permute-start.10) | collective-permute-done | bytes 110624 | tf_op jit(solution)/shard_map/ppermute | solution.py:50
  58.5 1.2 %unpack_spatial.1 = (bf16[128,1152]{1,0:T(8,128)(2,1)}, bf16[128,1152]{1,0:T(8,128)(2,1)}, bf16[128,1152]{1,0:T(8,128)(2,1)}) custom-call(bf16[432,128]{1,0:T(8,128)(2,1)S(1)} %get-tuple-element.33.refs_0_.token, bf16[432,128]{1,0:T(8,128)(2,1)S(1)} %collective-permute-done.3.refs_1_, bf16[432,128]{1,0:T(8,128)(2,1)S(1)} %collective-permute-done.4.refs_2_, ...), custom_call_target="tpu_custom_call" | custom-call | flops 3000000000 | bytes 1024 | tf_op jit(solution)/shard_map/unpack_spatial/pallas_call | solution.py:203
  59.7 1.1 %unpack_temporal.1 = (bf16[1,128,1152]{2,1,0:T(8,128)(2,1)}, bf16[1,128,1152]{2,1,0:T(8,128)(2,1)}, bf16[1,128,1152]{2,1,0:T(8,128)(2,1)}) custom-call(bf16[8,3,16,1152]{3,2,1,0:T(8,128)(2,1)S(1)} %all-to-all-done.1.refs_0_), custom_call_target="tpu_custom_call" | custom-call | flops 1000000000 | bytes 1024 | tf_op jit(solution)/shard_map/unpack_temporal/pallas_call | solution.py:339
  (27 shorter events, 0.1 us)
Async XLA Ops:
  0.6 12.2 %copy-start.2 = (bf16[1,128,1152]{2,1,0:T(8,128)(2,1)S(1)}, bf16[1,128,1152]{2,1,0:T(8,128)(2,1)}, u32[]{:S(2)}) copy-start(bf16[1,128,1152]{2,1,0:T(8,128)(2,1)} %v.1) | copy-start | bytes 884740
  0.6 12.2 %copy-start.1 = (bf16[1,128,1152]{2,1,0:T(8,128)(2,1)S(1)}, bf16[1,128,1152]{2,1,0:T(8,128)(2,1)}, u32[]{:S(2)}) copy-start(bf16[1,128,1152]{2,1,0:T(8,128)(2,1)} %k.1) | copy-start | bytes 884740
  0.7 12.2 %copy-start = (bf16[1,128,1152]{2,1,0:T(8,128)(2,1)S(1)}, bf16[1,128,1152]{2,1,0:T(8,128)(2,1)}, u32[]{:S(2)}) copy-start(bf16[1,128,1152]{2,1,0:T(8,128)(2,1)} %q.1) | copy-start | bytes 884740
  3.3 16.2 %collective-permute-start = (bf16[576,128]{1,0:T(8,128)(2,1)}, bf16[576,128]{1,0:T(8,128)(2,1)S(1)}, u32[]{:S(2)}, u32[]{:S(2)}) collective-permute-start(bf16[576,128]{1,0:T(8,128)(2,1)} %get-tuple-element.30), channel_id=1, source_target_pairs={{0,3},{1,2},{2,1},{3,0},{4,7},{5,6},{6,5},{7,4},{8,11},{9,10},{10,... | collective-permute-start | bytes 442376 | tf_op jit(solution)/shard_map/ppermute | solution.py:50
  8.4 20.0 %collective-permute-start.1 = (bf16[576,128]{1,0:T(8,128)(2,1)}, bf16[576,128]{1,0:T(8,128)(2,1)S(1)}, u32[]{:S(2)}, u32[]{:S(2)}) collective-permute-start(bf16[576,128]{1,0:T(8,128)(2,1)} %get-tuple-element.31), channel_id=1, source_target_pairs={{0,2},{1,3},{2,0},{3,1},{4,6},{5,7},{6,4},{7,5},{8,10},{9,11},{10,... | collective-permute-start | bytes 442376 | tf_op jit(solution)/shard_map/ppermute | solution.py:50
  8.4 20.0 %collective-permute-start.2 = (bf16[576,128]{1,0:T(8,128)(2,1)}, bf16[576,128]{1,0:T(8,128)(2,1)S(1)}, u32[]{:S(2)}, u32[]{:S(2)}) collective-permute-start(bf16[576,128]{1,0:T(8,128)(2,1)} %get-tuple-element.32), channel_id=1, source_target_pairs={{0,1},{1,0},{2,3},{3,2},{4,5},{5,4},{6,7},{7,6},{8,9},{9,8},{10,11... | collective-permute-start | bytes 442376 | tf_op jit(solution)/shard_map/ppermute | solution.py:50
  9.1 33.4 %collective-permute-start.6 = (bf16[576,128]{1,0:T(8,128)(2,1)}, bf16[576,128]{1,0:T(8,128)(2,1)S(1)}, u32[]{:S(2)}, u32[]{:S(2)}) collective-permute-start(bf16[576,128]{1,0:T(8,128)(2,1)} %get-tuple-element.38), channel_id=1, source_target_pairs={{0,3},{1,2},{2,1},{3,0},{4,7},{5,6},{6,5},{7,4},{8,11},{9,10},{10,... | collective-permute-start | bytes 442376 | tf_op jit(solution)/shard_map/ppermute | solution.py:50
  12.8 30.5 %collective-permute-start.7 = (bf16[576,128]{1,0:T(8,128)(2,1)}, bf16[576,128]{1,0:T(8,128)(2,1)S(1)}, u32[]{:S(2)}, u32[]{:S(2)}) collective-permute-start(bf16[576,128]{1,0:T(8,128)(2,1)} %get-tuple-element.39), channel_id=1, source_target_pairs={{0,2},{1,3},{2,0},{3,1},{4,6},{5,7},{6,4},{7,5},{8,10},{9,11},{10,... | collective-permute-start | bytes 442376 | tf_op jit(solution)/shard_map/ppermute | solution.py:50
  12.8 1.0 %copy-start.3 = (bf16[1,128,1152]{2,1,0:T(8,128)(2,1)S(1)}, bf16[1,128,1152]{2,1,0:T(8,128)(2,1)}, u32[]{:S(2)}) copy-start(bf16[1,128,1152]{2,1,0:T(8,128)(2,1)} %g.1) | copy-start | bytes 884740
  13.8 0.7 %copy-start.6 = (bf16[16,128]{1,0:T(8,128)(2,1)S(1)}, bf16[16,128]{1,0:T(8,128)(2,1)}, u32[]{:S(2)}) copy-start(bf16[16,128]{1,0:T(8,128)(2,1)} %get-tuple-element.48.token) | copy-start | bytes 12292
  15.6 3.9 %copy-start.7 = (bf16[576,128]{1,0:T(8,128)(2,1)S(1)}, bf16[576,128]{1,0:T(8,128)(2,1)}, u32[]{:S(2)}) copy-start(bf16[576,128]{1,0:T(8,128)(2,1)} %get-tuple-element.40) | copy-start | bytes 442372
  15.6 12.8 %copy-start.5 = (bf16[576,128]{1,0:T(8,128)(2,1)S(1)}, bf16[576,128]{1,0:T(8,128)(2,1)}, u32[]{:S(2)}) copy-start(bf16[576,128]{1,0:T(8,128)(2,1)} %get-tuple-element.29.refs_0_) | copy-start | bytes 442372
  15.6 20.7 %all-to-all-start = ((bf16[8,4,16,1152]{3,2,1,0:T(8,128)(2,1)}), bf16[8,4,16,1152]{3,2,1,0:T(8,128)(2,1)S(1)}, u32[]{:S(2)}, u32[]{:S(2)}) async-start(bf16[8,4,16,1152]{3,2,1,0:T(8,128)(2,1)} %pack_temporal.1), calls=%async_computation | async-start | bytes 2359296 | tf_op jit(solution)/shard_map/all_to_all | solution.py:321
  19.5 23.9 %collective-permute-start.8 = (bf16[576,128]{1,0:T(8,128)(2,1)S(1)}, bf16[576,128]{1,0:T(8,128)(2,1)S(1)}, u32[]{:S(2)}, u32[]{:S(2)}) collective-permute-start(bf16[576,128]{1,0:T(8,128)(2,1)S(1)} %copy-done.7), channel_id=1, source_target_pairs={{0,1},{1,0},{2,3},{3,2},{4,5},{5,4},{6,7},{7,6},{8,9},{9,8},{10,11... | collective-permute-start | bytes 442376 | tf_op jit(solution)/shard_map/ppermute | solution.py:50
  30.6 18.6 %collective-permute-start.3 = (bf16[432,128]{1,0:T(8,128)(2,1)S(1)}, bf16[432,128]{1,0:T(8,128)(2,1)S(1)}, u32[]{:S(2)}, u32[]{:S(2)}) collective-permute-start(bf16[432,128]{1,0:T(8,128)(2,1)S(1)} %get-tuple-element.34), channel_id=1, source_target_pairs={{0,3},{1,2},{2,1},{3,0},{4,7},{5,6},{6,5},{7,4},{8,11},{9,10},{10,... | collective-permute-start | bytes 331784 | tf_op jit(solution)/shard_map/ppermute | solution.py:50
  33.3 16.7 %collective-permute-start.4 = (bf16[432,128]{1,0:T(8,128)(2,1)S(1)}, bf16[432,128]{1,0:T(8,128)(2,1)S(1)}, u32[]{:S(2)}, u32[]{:S(2)}) collective-permute-start(bf16[432,128]{1,0:T(8,128)(2,1)S(1)} %get-tuple-element.35), channel_id=1, source_target_pairs={{0,2},{1,3},{2,0},{3,1},{4,6},{5,7},{6,4},{7,5},{8,10},{9,11},{10,... | collective-permute-start | bytes 331784 | tf_op jit(solution)/shard_map/ppermute | solution.py:50
  38.8 4.5 %copy-start.4 = (bf16[576,128]{1,0:T(8,128)(2,1)S(1)}, bf16[576,128]{1,0:T(8,128)(2,1)}, u32[]{:S(2)}) copy-start(bf16[576,128]{1,0:T(8,128)(2,1)} %get-tuple-element.37.refs_0_) | copy-start | bytes 442372
  38.8 20.8 %all-to-all-start.1 = ((bf16[8,3,16,1152]{3,2,1,0:T(8,128)(2,1)}), bf16[8,3,16,1152]{3,2,1,0:T(8,128)(2,1)S(1)}, u32[]{:S(2)}, u32[]{:S(2)}) async-start(bf16[8,3,16,1152]{3,2,1,0:T(8,128)(2,1)} %core_temporal.1), calls=%async_computation.1 | async-start | bytes 1769472 | tf_op jit(solution)/shard_map/all_to_all | solution.py:337
  42.5 7.5 %collective-permute-start.5 = (bf16[432,128]{1,0:T(8,128)(2,1)S(1)}, bf16[432,128]{1,0:T(8,128)(2,1)S(1)}, u32[]{:S(2)}, u32[]{:S(2)}) collective-permute-start(bf16[432,128]{1,0:T(8,128)(2,1)S(1)} %get-tuple-element.36), channel_id=1, source_target_pairs={{0,1},{1,0},{2,3},{3,2},{4,5},{5,4},{6,7},{7,6},{8,9},{9,8},{10,11... | collective-permute-start | bytes 331784 | tf_op jit(solution)/shard_map/ppermute | solution.py:50
  45.6 7.9 %collective-permute-start.9 = (bf16[432,128]{1,0:T(8,128)(2,1)S(1)}, bf16[432,128]{1,0:T(8,128)(2,1)S(1)}, u32[]{:S(2)}, u32[]{:S(2)}) collective-permute-start(bf16[432,128]{1,0:T(8,128)(2,1)S(1)} %get-tuple-element.42), channel_id=1, source_target_pairs={{0,3},{1,2},{2,1},{3,0},{4,7},{5,6},{6,5},{7,4},{8,11},{9,10},{10,... | collective-permute-start | bytes 331784 | tf_op jit(solution)/shard_map/ppermute | solution.py:50
  49.2 9.2 %collective-permute-start.10 = (bf16[432,128]{1,0:T(8,128)(2,1)S(1)}, bf16[432,128]{1,0:T(8,128)(2,1)S(1)}, u32[]{:S(2)}, u32[]{:S(2)}) collective-permute-start(bf16[432,128]{1,0:T(8,128)(2,1)S(1)} %get-tuple-element.43), channel_id=1, source_target_pairs={{0,2},{1,3},{2,0},{3,1},{4,6},{5,7},{6,4},{7,5},{8,10},{9,11},{10,... | collective-permute-start | bytes 331784 | tf_op jit(solution)/shard_map/ppermute | solution.py:50
  49.2 9.2 %collective-permute-start.11 = (bf16[432,128]{1,0:T(8,128)(2,1)S(1)}, bf16[432,128]{1,0:T(8,128)(2,1)S(1)}, u32[]{:S(2)}, u32[]{:S(2)}) collective-permute-start(bf16[432,128]{1,0:T(8,128)(2,1)S(1)} %get-tuple-element.44), channel_id=1, source_target_pairs={{0,1},{1,0},{2,3},{3,2},{4,5},{5,4},{6,7},{7,6},{8,9},{9,8},{10,11... | collective-permute-start | bytes 331784 | tf_op jit(solution)/shard_map/ppermute | solution.py:50

commit v2 on v1

--- a/solution.py
+++ b/solution.py
@@ -13,14 +13,15 @@
 EXP2_SCALE = SCALE * math.log2(math.e)
 LANES = 128
 CHUNKS = 2
-HOLD = False
+REST_AFTER = True
+HOLD = True
 HEAD_GROUP = 8
-IN_ORDER = "desc"
-OUT_ORDER = "desc"
-COST = {"core_spatial0": 20, "core_spatial1": 10, "core_temporal": 3, "unpack_spatial": 3, "pack_temporal": 5}
+IN_ORDER = "213"
+OUT_ORDER = "231"
+SEND_ORDER = "desc"
+COST = {"core_spatial0": 40, "core_spatial1": 15, "core_temporal": 3, "unpack": 3}
 AFTER = 1
-LAST = ""
-VM = {"pack_spatial": 63}
+VM = {"pack_spatial": 62}
 
 NT = (((1,), (1,)), ((), ()))
 TN = (((0,), (0,)), ((), ()))
@@ -50,29 +51,42 @@
     return lax.ppermute(array, axis, [(i, i ^ distance) for i in range(size)])
 
 
+def cut_messages(turned, outs, group, chunks, wanted):
+    me = lax.axis_index("space")
+    rows = turned.shape[2] // chunks
+    for n, c in enumerate(wanted):
+        for d in range(group):
+            for a in range(4):
+                block = turned[a, me ^ d]
+                outs[n * group + d][a * rows : (a + 1) * rows] = block[c * rows : (c + 1) * rows]
+
+
 def spatial_pack_kernel(group, chunks, *refs):
-    sources, outs, token = refs[:4], refs[4:-4], refs[-4]
-    scratch, staged, sems = refs[-3:]
-    share = scratch.shape[2]
+    sources, outs, turned = refs[:4], refs[4 : 4 + group], refs[-3]
+    staged, sems = refs[-2:]
+    share = turned.shape[2]
     copies = [
         pltpu.make_async_copy(sources[a].at[0], staged.at[a], sems.at[a]) for a in range(4)
     ]
     for copy in copies:
         copy.start()
-    token[...] = jnp.zeros_like(token)
     for a in range(4):
         copies[a].wait()
-        turned = staged[a].T
+        block = staged[a].T
         for d in range(group):
-            scratch[a, d] = turned[d * share : (d + 1) * share]
-    me = lax.axis_index("space")
-    rows = share // chunks
-    for k in range(group):
-        to = me ^ k
-        for a in range(4):
-            block = scratch[a, to]
-            for c in range(chunks):
-                outs[k * chunks + c][a * rows : (a + 1) * rows] = block[c * rows : (c + 1) * rows]
+            turned[a, d] = block[d * share : (d + 1) * share]
+    cut_messages(turned, outs, group, chunks, [0])
+
+
+def spatial_pack_rest_kernel(group, chunks, turned, token, *outs):
+    cut_messages(turned, outs, group, chunks, range(1, chunks))
+
+
+def temporal_pack_kernel(q, k, v, g, token, out):
+    group, _, rows, _ = out.shape
+    for t in range(group):
+        for a, source in enumerate((q, k, v, g)):
+            out[t, a] = source[0, t * rows : (t + 1) * rows]
 
 
 def spatial_core_kernel(heads, *refs):
@@ -122,44 +136,81 @@
                 outs[k][row : row + HEAD_DIM] = low[:, k * per : (k + 1) * per]
 
 
-def spatial_unpack_kernel(places, chunks, *refs):
+def unpack_kernel(places, chunks, *refs):
     group = len(places)
-    messages, outs, scratch = refs[: group * chunks], refs[group * chunks : -1], refs[-1]
-    share = scratch.shape[2]
+    messages, others = refs[: group * chunks], refs[group * chunks : -4]
+    scratch, turned, sems, other_sems = refs[-4:]
+    outs, slices = others[-3:], []
+    if len(others) > 3:
+        arrived, outs = others[0], others[1:4]
+        parts, _, rows, _ = arrived.shape
+        slices = [
+            pltpu.make_async_copy(
+                arrived.at[t, i], others[4 + i].at[0, t * rows : (t + 1) * rows], other_sems.at[t, i]
+            )
+            for i in range(3)
+            for t in range(parts)
+        ]
+    for copy in slices:
+        copy.start()
+    share, tokens = scratch.shape[2:]
     rows = share // chunks
     me = lax.axis_index("space")
-    for k, d in enumerate(places):
-        of = me ^ d
-        parts = [messages[c * group + k][...] for c in range(chunks)]
-        for i in range(3):
-            scratch[i, of] = jnp.concatenate([p[i * rows : (i + 1) * rows] for p in parts], axis=0)
+    copies = []
     for i in range(3):
-        outs[i][...] = scratch[i].reshape(group * share, LANES).T
-
-
-def spatial_send(q, k, v, g):
-    _, tokens, width = q.shape
-    group = lax.axis_size("space")
+        for k, d in enumerate(places):
+            parts = [
+                messages[c * group + k][i * rows : (i + 1) * rows] for c in range(chunks)
+            ]
+            scratch[i, me ^ d] = jnp.concatenate(parts, axis=0)
+        turned[i] = scratch[i].reshape(group * share, tokens).T
+        copies.append(pltpu.make_async_copy(turned.at[i], outs[i].at[0], sems.at[i]))
+        copies[i].start()
+    for copy in copies + slices:
+        copy.wait()
+
+
+def send(arrays):
+    _, tokens, width = arrays[0].shape
+    group, parts = lax.axis_size("space"), lax.axis_size("tm")
     share = width // group
     heads_here = share // HEAD_DIM
     chunks = math.gcd(CHUNKS, heads_here)
-    heads = heads_here // chunks
-    *packed, token = call(
+    rows = tokens // parts
+    hbm, vmem = pl.BlockSpec(memory_space=pltpu.HBM), pl.BlockSpec(memory_space=pltpu.VMEM)
+    message = bf16(4 * share // chunks, tokens)
+    *messages, turned = call(
         "pack_spatial",
         functools.partial(spatial_pack_kernel, group, chunks),
-        [bf16(4 * heads * HEAD_DIM, tokens)] * (group * chunks) + [bf16(16, LANES)],
-        in_specs=[pl.BlockSpec(memory_space=pltpu.HBM)] * 4,
+        [message] * group + [bf16(4, group, share, tokens)],
+        in_specs=[hbm] * 4,
         scratch=[
-            pltpu.VMEM((4, group, share, tokens), jnp.bfloat16),
             pltpu.VMEM((4, tokens, width), jnp.bfloat16),
             pltpu.SemaphoreType.DMA((4,)),
         ],
-    )(q, k, v, g)
-    arrived = []
+    )(*arrays[:4])
+    if rows % 16 == 0:
+        slices = call(
+            "pack_temporal",
+            temporal_pack_kernel,
+            bf16(parts, 4, rows, width),
+            in_specs=[vmem] * 4 + [pl.BlockSpec(memory_space=pl.ANY)],
+        )(*arrays[4:], messages[0])
+    else:
+        slices = jnp.stack([x.reshape(parts, rows, width) for x in arrays[4:]], axis=1)
+    if chunks > 1:
+        messages += call(
+            "pack_rest",
+            functools.partial(spatial_pack_rest_kernel, group, chunks),
+            [message] * (group * (chunks - 1)),
+            in_specs=[vmem, pl.BlockSpec(memory_space=pl.ANY)],
+        )(turned, slices if REST_AFTER else messages[0])
+    spatial = []
     for c in range(chunks):
-        far = [swap(packed[d * chunks + c], "space", d) for d in range(group - 1, 0, -1)]
-        arrived.append([packed[c]] + far[::-1])
-    return arrived, token
+        mine = messages[c * group : (c + 1) * group]
+        far = {d: swap(mine[d], "space", d) for d in order(SEND_ORDER, group)[1:]}
+        spatial.append([mine[0]] + [far[d] for d in range(1, group)])
+    return spatial, lax.all_to_all(slices, "tm", 0, 0, tiled=True)
 
 
 def order(kind, group):
@@ -192,27 +243,33 @@
     return [[chunk[places.index(d)] for d in range(group)] for chunk in results]
 
 
-def spatial_return(results, width):
-    chunks, group = len(results), len(results[0])
-    tokens = results[0][0].shape[1]
+def give_back(spatial, temporal, width):
+    chunks, group = len(spatial), len(spatial[0])
+    tokens = spatial[0][0].shape[1]
+    parts, _, rows, _ = temporal.shape
+    aligned = rows % 16 == 0
     places = order(OUT_ORDER, group)
-    back = []
-    for mine in results:
-        far = [swap(mine[d], "space", d) for d in range(group - 1, 0, -1)]
-        back.append([mine[0]] + far[::-1])
-    return call(
-        "unpack_spatial",
-        functools.partial(spatial_unpack_kernel, places, chunks),
-        [bf16(tokens, width)] * 3,
-        scratch=[pltpu.VMEM((3, group, width // group, tokens), jnp.bfloat16)],
-    )(*[back[c][d] for c in range(chunks) for d in places]), back
-
-
-def temporal_pack_kernel(q, k, v, g, token, out):
-    group, _, rows, _ = out.shape
-    for t in range(group):
-        for a, source in enumerate((q, k, v, g)):
-            out[t, a] = source[0, t * rows : (t + 1) * rows]
+    messages = [
+        mine[d] if d == 0 else swap(mine[d], "space", d) for mine in spatial for d in places
+    ]
+    arrived = lax.all_to_all(temporal, "tm", 0, 0, tiled=True)
+    hbm, vmem = pl.BlockSpec(memory_space=pltpu.HBM), pl.BlockSpec(memory_space=pltpu.VMEM)
+    outs = call(
+        "unpack",
+        functools.partial(unpack_kernel, places, chunks),
+        [bf16(1, tokens, width)] * (6 if aligned else 3),
+        in_specs=[vmem] * len(messages) + [pl.BlockSpec(memory_space=pl.ANY)] * aligned,
+        out_specs=[hbm] * (6 if aligned else 3),
+        scratch=[
+            pltpu.VMEM((3, group, width // group, tokens), jnp.bfloat16),
+            pltpu.VMEM((3, tokens, width), jnp.bfloat16),
+            pltpu.SemaphoreType.DMA((3,)),
+            pltpu.SemaphoreType.DMA((parts, 3)),
+        ],
+    )(*messages, *[arrived] * aligned)
+    if aligned:
+        return outs
+    return list(outs) + [arrived[:, i].reshape(1, tokens, width) for i in range(3)]
 
 
 def temporal_core_kernel(messages, token, out):
@@ -288,39 +345,6 @@
                     flush(t)
 
 
-def temporal_unpack_kernel(*refs):
-    messages, outs, sems = refs[0], refs[-4:-1], refs[-1]
-    group, _, rows, _ = messages.shape
-    copies = [
-        pltpu.make_async_copy(
-            messages.at[t, i], outs[i].at[0, t * rows : (t + 1) * rows], sems.at[t, i]
-        )
-        for i in range(3)
-        for t in range(group)
-    ]
-    for copy in copies:
-        copy.start()
-    for copy in copies:
-        copy.wait()
-
-
-def temporal_send(q, k, v, g, token):
-    _, tokens, width = q.shape
-    group = lax.axis_size("tm")
-    rows = tokens // group
-    if rows % 16 == 0:
-        packed = call(
-            "pack_temporal",
-            temporal_pack_kernel,
-            bf16(group, 4, rows, width),
-            in_specs=[pl.BlockSpec(memory_space=pltpu.VMEM)] * 4
-            + [pl.BlockSpec(memory_space=pl.ANY)],
-        )(q, k, v, g, token)
-    else:
-        packed = jnp.stack([x.reshape(group, rows, width) for x in (q, k, v, g)], axis=1)
-    return lax.all_to_all(packed, "tm", 0, 0, tiled=True)
-
-
 def temporal_core(arrived, token):
     group, _, rows, width = arrived.shape
     return call(
@@ -332,36 +356,17 @@
     )(arrived, token)
 
 
-def temporal_return(results, last):
-    group, _, rows, width = results.shape
-    arrived = lax.all_to_all(results, "tm", 0, 0, tiled=True)
-    if rows % 16 == 0:
-        return call(
-            "unpack_temporal",
-            temporal_unpack_kernel,
-            [bf16(1, group * rows, width)] * 3,
-            in_specs=[pl.BlockSpec(memory_space=pl.ANY)] * (1 + len(last)),
-            out_specs=[pl.BlockSpec(memory_space=pltpu.HBM)] * 3,
-            scratch=[pltpu.SemaphoreType.DMA((group, 3))],
-        )(arrived, *last)
-    return [arrived[:, i].reshape(1, group * rows, width) for i in range(3)]
-
-
 def shards(*arrays):
     width = arrays[0].shape[2]
-    spatial_in, token = spatial_send(*arrays[:4])
-    temporal_in = temporal_send(*arrays[4:], token)
-    cut = len(spatial_in) if AFTER is None else min(AFTER, len(spatial_in))
-    spatial_out = spatial_core(spatial_in[:cut], 0)
-    temporal_out = temporal_core(temporal_in, spatial_out[-1][0] if cut else token)
-    if cut < len(spatial_in):
+    spatial, temporal = send(arrays)
+    cut = min(AFTER, len(spatial))
+    done = spatial_core(spatial[:cut], 0)
+    results = temporal_core(temporal, done[-1][0])
+    if cut < len(spatial):
         if HOLD:
-            spatial_in[cut][0], _ = lax.optimization_barrier((spatial_in[cut][0], temporal_out))
-        spatial_out += spatial_core(spatial_in[cut:], cut)
-    spatial_grads, zback = spatial_return(spatial_out, width)
-    last = {"uz": spatial_grads[:1], "z1": zback[0][1:2], "z12": zback[0][1:3], "z13": zback[0][1:4:2], "": []}[LAST]
-    temporal_grads = temporal_return(temporal_out, last)
-    return tuple(x[None] for x in spatial_grads) + tuple(temporal_grads)
+            spatial[cut][0], _ = lax.optimization_barrier((spatial[cut][0], results))
+        done += spatial_core(spatial[cut:], cut)
+    return tuple(give_back(done, results, width))
 
 
 def solution(mesh):

time: 61.1 us -> 56 us (0.917)
  waiting for transfers between devices: 19.5 us -> 10.8 us
  starting transfers between devices: 25.9 us -> 29.4 us
    ppermute x12, waiting for transfers between devices: 16.6 us -> 8.75 us  [swap(): return lax.ppermute(array, axis, [(i, i ^ distance) for i in range(size)])]
    ppermute x12, starting transfers between devices: 18.3 us -> 21.9 us  [swap(): return lax.ppermute(array, axis, [(i, i ^ distance) for i in range(size)])]
    all_to_all x2, waiting for transfers between devices: 2.96 us -> 2.04 us  [the longest x1 2.03 us: send(): return (spatial, lax.all_to_all(slices, 'tm', 0, 0, tiled=True))]
    unnamed x16 -> x14, local copies, waits for them, and re-layouts: 1.66 us -> 2.19 us
  transfers between devices with their start and end apart: 14 -> 14, of which waited for: 4 -> 3; matrix products, arithmetic and copies ran while one was open for 0% -> 0% of each run, Pallas kernels for 15% -> 14%
where the time goes in v2:
time: 56 us; the launch traced here: 55.7 us
  starting transfers between devices  29.4 us (52%)
  Pallas kernels  12.6 us (22%)
  waiting for transfers between devices  10.8 us (19%)
  local copies, waits for them, and re-layouts  2.19 us (4%)
  between operations  0.74 us (1%)
    ppermute x12, starting transfers between devices, swap(): return lax.ppermute(array, axis, [(i, i ^ distance) for i in range(size)])  21.9 us
    ppermute x12, waiting for transfers between devices, swap(): return lax.ppermute(array, axis, [(i, i ^ distance) for i in range(size)])  8.75 us
    pallas_call x2, Pallas kernels, spatial_core(): call(f'core_spatial{first + c}', functools.partial(spatial_core_kernel, h...  4.34 us
    all_to_all x1, starting transfers between devices, send(): return (spatial, lax.all_to_all(slices, 'tm', 0, 0, tiled=True))  3.92 us
    all_to_all x1, starting transfers between devices, give_back(): arrived = lax.all_to_all(temporal, 'tm', 0, 0, tiled=True)  3.55 us
    pallas_call x1, Pallas kernels, send(): call('pack_spatial', functools.partial(spatial_pack_kernel, group, chunks...  2.85 us
    pallas_call x1, Pallas kernels, temporal_core(): call('core_temporal', temporal_core_kernel, bf16(group, 3, rows, width),...  2.53 us
    unnamed x14, local copies, waits for them, and re-layouts  2.19 us
  transfers between devices with their start and end apart: 14, of which 3 were waited for; matrix products, arithmetic and copies ran while one was open for 0% of the time, Pallas kernels for 14%

profile of v2, /device:TPU:0, one launch (start us, length us, event | category | flops | bytes accessed | tf_op | source)
XLA Modules:
  0.0 55.7 jit_solution(15028384677899214437)
XLA Ops:
  0.7 2.9 %pack_spatial.1 = (bf16[576,128]{1,0:T(8,128)(2,1)}, bf16[576,128]{1,0:T(8,128)(2,1)}, bf16[576,128]{1,0:T(8,128)(2,1)}, bf16[576,128]{1,0:T(8,128)(2,1)}, bf16[4,4,288,128]{3,2,1,0:T(8,128)(2,1)}) custom-call(bf16[1,128,1152]{2,1,0:T(8,128)(2,1)} %refs_0_.1, bf16[1,128,1152]{2,1,0:T(8,128)(2,1)} %refs_1_.1, bf16[1,128,1152]{2,1,0:T(8,128)(2,1)} %refs_2_.1, ...), custom_call_target="tpu_custom_call" | custom-call | flops 1000000000 | bytes 1024 | tf_op jit(solution)/shard_map/pack_spatial/pallas_call | solution.py:182
  3.5 4.1 %collective-permute-start = (bf16[576,128]{1,0:T(8,128)(2,1)}, bf16[576,128]{1,0:T(8,128)(2,1)S(1)}, u32[]{:S(2)}, u32[]{:S(2)}) collective-permute-start(bf16[576,128]{1,0:T(8,128)(2,1)} %get-tuple-element.25), channel_id=1, source_target_pairs={{0,2},{1,3},{2,0},{3,1},{4,6},{5,7},{6,4},{7,5},{8,10},{9,11},{10,... | collective-permute-start | bytes 442376 | tf_op jit(solution)/shard_map/ppermute | solution.py:51
  7.6 1.6 %collective-permute-start.1 = (bf16[576,128]{1,0:T(8,128)(2,1)}, bf16[576,128]{1,0:T(8,128)(2,1)S(1)}, u32[]{:S(2)}, u32[]{:S(2)}) collective-permute-start(bf16[576,128]{1,0:T(8,128)(2,1)} %get-tuple-element.26), channel_id=1, source_target_pairs={{0,1},{1,0},{2,3},{3,2},{4,5},{5,4},{6,7},{7,6},{8,9},{9,8},{10,11... | collective-permute-start | bytes 442376 | tf_op jit(solution)/shard_map/ppermute | solution.py:51
  9.3 0.9 %copy-done.5 = bf16[576,128]{1,0:T(8,128)(2,1)S(1)} copy-done((bf16[576,128]{1,0:T(8,128)(2,1)S(1)}, bf16[576,128]{1,0:T(8,128)(2,1)}, u32[]{:S(2)}) %copy-start.5) | copy-done | bytes 147480
  10.2 1.1 %pack_temporal.1.token = bf16[8,4,16,1152]{3,2,1,0:T(8,128)(2,1)} custom-call(bf16[1,128,1152]{2,1,0:T(8,128)(2,1)S(1)} %copy-done, bf16[1,128,1152]{2,1,0:T(8,128)(2,1)S(1)} %copy-done.1, bf16[1,128,1152]{2,1,0:T(8,128)(2,1)S(1)} %copy-done.2, bf16[1,128,1152]{2,1,0:T(8,128)(2,1)S(1)} %copy-done.3, bf16[576,128]{1,0:T(8,128)(2,1)S(1)} %copy-done.5), custom_call_target="tpu_custom_call" | custom-call | flops 1000000000 | bytes 1024 | tf_op jit(solution)/shard_map/pack_temporal/pallas_call | solution.py:193
  11.3 3.9 %all-to-all-start = ((bf16[8,4,16,1152]{3,2,1,0:T(8,128)(2,1)}), bf16[8,4,16,1152]{3,2,1,0:T(8,128)(2,1)S(1)}, u32[]{:S(2)}, u32[]{:S(2)}) async-start(bf16[8,4,16,1152]{3,2,1,0:T(8,128)(2,1)} %pack_temporal.1.token), calls=%async_computation | async-start | bytes 2359296 | tf_op jit(solution)/shard_map/all_to_all | solution.py:213
  15.2 1.3 %copy-done.4 = bf16[4,4,288,128]{3,2,1,0:T(8,128)(2,1)S(1)} copy-done((bf16[4,4,288,128]{3,2,1,0:T(8,128)(2,1)S(1)}, bf16[4,4,288,128]{3,2,1,0:T(8,128)(2,1)}, u32[]{:S(2)}) %copy-start.4) | copy-done | bytes 1179672
  16.5 1.8 %collective-permute-start.6 = (bf16[576,128]{1,0:T(8,128)(2,1)S(1)}, bf16[576,128]{1,0:T(8,128)(2,1)S(1)}, u32[]{:S(2)}, u32[]{:S(2)}) collective-permute-start(bf16[576,128]{1,0:T(8,128)(2,1)S(1)} %get-tuple-element.35), channel_id=1, source_target_pairs={{0,2},{1,3},{2,0},{3,1},{4,6},{5,7},{6,4},{7,5},{8,10},{9,11},{10,... | collective-permute-start | bytes 442376 | tf_op jit(solution)/shard_map/ppermute | solution.py:51
  18.3 2.5 %collective-permute-start.7 = (bf16[576,128]{1,0:T(8,128)(2,1)S(1)}, bf16[576,128]{1,0:T(8,128)(2,1)S(1)}, u32[]{:S(2)}, u32[]{:S(2)}) collective-permute-start(bf16[576,128]{1,0:T(8,128)(2,1)S(1)} %get-tuple-element.36), channel_id=1, source_target_pairs={{0,1},{1,0},{2,3},{3,2},{4,5},{5,4},{6,7},{7,6},{8,9},{9,8},{10,11... | collective-permute-start | bytes 442376 | tf_op jit(solution)/shard_map/ppermute | solution.py:51
  20.7 0.2 collective-permute-start.8
  21.0 2.2 %core_spatial0.1 = (bf16[432,128]{1,0:T(8,128)(2,1)S(1)}, bf16[432,128]{1,0:T(8,128)(2,1)S(1)}, bf16[432,128]{1,0:T(8,128)(2,1)S(1)}, bf16[432,128]{1,0:T(8,128)(2,1)S(1)}) custom-call(bf16[576,128]{1,0:T(8,128)(2,1)S(1)} %copy-done.6, bf16[576,128]{1,0:T(8,128)(2,1)S(1)} %collective-permute-done.refs_1_, ...), custom_call_target="tpu_custom_call" | custom-call | flops 40000000000 | bytes 1024 | tf_op jit(solution)/shard_map/core_spatial0/pallas_call | solution.py:236
  23.2 6.1 %collective-permute-start.3 = (bf16[432,128]{1,0:T(8,128)(2,1)S(1)}, bf16[432,128]{1,0:T(8,128)(2,1)S(1)}, u32[]{:S(2)}, u32[]{:S(2)}) collective-permute-start(bf16[432,128]{1,0:T(8,128)(2,1)S(1)} %get-tuple-element.29), channel_id=1, source_target_pairs={{0,2},{1,3},{2,0},{3,1},{4,6},{5,7},{6,4},{7,5},{8,10},{9,11},{10,... | collective-permute-start | bytes 331784 | tf_op jit(solution)/shard_map/ppermute | solution.py:51
  29.3 0.7 %collective-permute-start.4 = (bf16[432,128]{1,0:T(8,128)(2,1)S(1)}, bf16[432,128]{1,0:T(8,128)(2,1)S(1)}, u32[]{:S(2)}, u32[]{:S(2)}) collective-permute-start(bf16[432,128]{1,0:T(8,128)(2,1)S(1)} %get-tuple-element.30), channel_id=1, source_target_pairs={{0,3},{1,2},{2,1},{3,0},{4,7},{5,6},{6,5},{7,4},{8,11},{9,10},{10,... | collective-permute-start | bytes 331784 | tf_op jit(solution)/shard_map/ppermute | solution.py:51
  30.0 2.0 %all-to-all-done.messages = bf16[8,4,16,1152]{3,2,1,0:T(8,128)(2,1)S(1)} async-done(((bf16[8,4,16,1152]{3,2,1,0:T(8,128)(2,1)}), bf16[8,4,16,1152]{3,2,1,0:T(8,128)(2,1)S(1)}, u32[]{:S(2)}, u32[]{:S(2)}) %all-to-all-start) | async-done | bytes 1179680 | tf_op jit(solution)/shard_map/all_to_all | solution.py:213
  32.0 2.5 %core_temporal.1 = bf16[8,3,16,1152]{3,2,1,0:T(8,128)(2,1)} custom-call(bf16[8,4,16,1152]{3,2,1,0:T(8,128)(2,1)S(1)} %all-to-all-done.messages, bf16[432,128]{1,0:T(8,128)(2,1)S(1)} %get-tuple-element.28.token.refs_0_), custom_call_target="tpu_custom_call" | custom-call | flops 3000000000 | bytes 1024 | tf_op jit(solution)/shard_map/core_temporal/pallas_call | solution.py:350
  34.5 3.5 %all-to-all-start.1 = ((bf16[8,3,16,1152]{3,2,1,0:T(8,128)(2,1)}), bf16[8,3,16,1152]{3,2,1,0:T(8,128)(2,1)S(1)}, u32[]{:S(2)}, u32[]{:S(2)}) async-start(bf16[8,3,16,1152]{3,2,1,0:T(8,128)(2,1)} %core_temporal.1), calls=%async_computation.1 | async-start | bytes 1769472 | tf_op jit(solution)/shard_map/all_to_all | solution.py:255
  38.1 0.7 %collective-permute-start.5 = (bf16[432,128]{1,0:T(8,128)(2,1)S(1)}, bf16[432,128]{1,0:T(8,128)(2,1)S(1)}, u32[]{:S(2)}, u32[]{:S(2)}) collective-permute-start(bf16[432,128]{1,0:T(8,128)(2,1)S(1)} %get-tuple-element.31), channel_id=1, source_target_pairs={{0,1},{1,0},{2,3},{3,2},{4,5},{5,4},{6,7},{7,6},{8,9},{9,8},{10,11... | collective-permute-start | bytes 331784 | tf_op jit(solution)/shard_map/ppermute | solution.py:51
  38.9 2.2 %core_spatial1.1 = (bf16[432,128]{1,0:T(8,128)(2,1)S(1)}, bf16[432,128]{1,0:T(8,128)(2,1)S(1)}, bf16[432,128]{1,0:T(8,128)(2,1)S(1)}, bf16[432,128]{1,0:T(8,128)(2,1)S(1)}) custom-call(bf16[576,128]{1,0:T(8,128)(2,1)S(1)} %get-tuple-element.34.refs_0_, bf16[576,128]{1,0:T(8,128)(2,1)S(1)} %collective-permute-done.6.refs_1_, ...), custom_call_target="tpu_custom_call" | custom-call | flops 15000000512 | bytes 1024 | tf_op jit(solution)/shard_map/core_spatial1/pallas_call | solution.py:236
  41.0 3.6 %collective-permute-start.9 = (bf16[432,128]{1,0:T(8,128)(2,1)S(1)}, bf16[432,128]{1,0:T(8,128)(2,1)S(1)}, u32[]{:S(2)}, u32[]{:S(2)}) collective-permute-start(bf16[432,128]{1,0:T(8,128)(2,1)S(1)} %get-tuple-element.39), channel_id=1, source_target_pairs={{0,2},{1,3},{2,0},{3,1},{4,6},{5,7},{6,4},{7,5},{8,10},{9,11},{10,... | collective-permute-start | bytes 331784 | tf_op jit(solution)/shard_map/ppermute | solution.py:51
  44.6 0.2 collective-permute-start.10
  44.8 0.4 collective-permute-start.11
  45.2 7.4 %collective-permute-done.9.refs_5_ = bf16[432,128]{1,0:T(8,128)(2,1)S(1)} collective-permute-done((bf16[432,128]{1,0:T(8,128)(2,1)S(1)}, bf16[432,128]{1,0:T(8,128)(2,1)S(1)}, u32[]{:S(2)}, u32[]{:S(2)}) %collective-permute-start.9) | collective-permute-done | bytes 110624 | tf_op jit(solution)/shard_map/ppermute | solution.py:51
  52.6 1.3 %collective-permute-done.11.refs_7_ = bf16[432,128]{1,0:T(8,128)(2,1)S(1)} collective-permute-done((bf16[432,128]{1,0:T(8,128)(2,1)S(1)}, bf16[432,128]{1,0:T(8,128)(2,1)S(1)}, u32[]{:S(2)}, u32[]{:S(2)}) %collective-permute-start.11) | collective-permute-done | bytes 110624 | tf_op jit(solution)/shard_map/ppermute | solution.py:51
  54.0 1.7 %unpack.1 = (bf16[1,128,1152]{2,1,0:T(8,128)(2,1)}, bf16[1,128,1152]{2,1,0:T(8,128)(2,1)}, bf16[1,128,1152]{2,1,0:T(8,128)(2,1)}, bf16[1,128,1152]{2,1,0:T(8,128...) custom-call(bf16[432,128]{1,0:T(8,128)(2,1)S(1)} %get-tuple-element.28.token.refs_0_, ...), custom_call_target="tpu_custom_call" | custom-call | flops 3000000000 | bytes 1024 | tf_op jit(solution)/shard_map/unpack/pallas_call | solution.py:257
  (25 shorter events, 0.1 us)
Async XLA Ops:
  0.6 8.6 %copy-start.3 = (bf16[1,128,1152]{2,1,0:T(8,128)(2,1)S(1)}, bf16[1,128,1152]{2,1,0:T(8,128)(2,1)}, u32[]{:S(2)}) copy-start(bf16[1,128,1152]{2,1,0:T(8,128)(2,1)} %g.1) | copy-start | bytes 884740
  0.6 8.6 %copy-start.2 = (bf16[1,128,1152]{2,1,0:T(8,128)(2,1)S(1)}, bf16[1,128,1152]{2,1,0:T(8,128)(2,1)}, u32[]{:S(2)}) copy-start(bf16[1,128,1152]{2,1,0:T(8,128)(2,1)} %v.1) | copy-start | bytes 884740
  0.7 8.6 %copy-start.1 = (bf16[1,128,1152]{2,1,0:T(8,128)(2,1)S(1)}, bf16[1,128,1152]{2,1,0:T(8,128)(2,1)}, u32[]{:S(2)}) copy-start(bf16[1,128,1152]{2,1,0:T(8,128)(2,1)} %k.1) | copy-start | bytes 884740
  0.7 8.6 %copy-start = (bf16[1,128,1152]{2,1,0:T(8,128)(2,1)S(1)}, bf16[1,128,1152]{2,1,0:T(8,128)(2,1)}, u32[]{:S(2)}) copy-start(bf16[1,128,1152]{2,1,0:T(8,128)(2,1)} %q.1) | copy-start | bytes 884740
  3.5 17.2 %collective-permute-start = (bf16[576,128]{1,0:T(8,128)(2,1)}, bf16[576,128]{1,0:T(8,128)(2,1)S(1)}, u32[]{:S(2)}, u32[]{:S(2)}) collective-permute-start(bf16[576,128]{1,0:T(8,128)(2,1)} %get-tuple-element.25), channel_id=1, source_target_pairs={{0,2},{1,3},{2,0},{3,1},{4,6},{5,7},{6,4},{7,5},{8,10},{9,11},{10,... | collective-permute-start | bytes 442376 | tf_op jit(solution)/shard_map/ppermute | solution.py:51
  7.6 13.3 %collective-permute-start.1 = (bf16[576,128]{1,0:T(8,128)(2,1)}, bf16[576,128]{1,0:T(8,128)(2,1)S(1)}, u32[]{:S(2)}, u32[]{:S(2)}) collective-permute-start(bf16[576,128]{1,0:T(8,128)(2,1)} %get-tuple-element.26), channel_id=1, source_target_pairs={{0,1},{1,0},{2,3},{3,2},{4,5},{5,4},{6,7},{7,6},{8,9},{9,8},{10,11... | collective-permute-start | bytes 442376 | tf_op jit(solution)/shard_map/ppermute | solution.py:51
  9.2 11.8 %collective-permute-start.2 = (bf16[576,128]{1,0:T(8,128)(2,1)}, bf16[576,128]{1,0:T(8,128)(2,1)S(1)}, u32[]{:S(2)}, u32[]{:S(2)}) collective-permute-start(bf16[576,128]{1,0:T(8,128)(2,1)} %get-tuple-element.27), channel_id=1, source_target_pairs={{0,3},{1,2},{2,1},{3,0},{4,7},{5,6},{6,5},{7,4},{8,11},{9,10},{10,... | collective-permute-start | bytes 442376 | tf_op jit(solution)/shard_map/ppermute | solution.py:51
  9.2 0.9 %copy-start.5 = (bf16[576,128]{1,0:T(8,128)(2,1)S(1)}, bf16[576,128]{1,0:T(8,128)(2,1)}, u32[]{:S(2)}) copy-start(bf16[576,128]{1,0:T(8,128)(2,1)} %get-tuple-element.24.refs_0_.token) | copy-start | bytes 442372
  11.3 20.7 %all-to-all-start = ((bf16[8,4,16,1152]{3,2,1,0:T(8,128)(2,1)}), bf16[8,4,16,1152]{3,2,1,0:T(8,128)(2,1)S(1)}, u32[]{:S(2)}, u32[]{:S(2)}) async-start(bf16[8,4,16,1152]{3,2,1,0:T(8,128)(2,1)} %pack_temporal.1.token), calls=%async_computation | async-start | bytes 2359296 | tf_op jit(solution)/shard_map/all_to_all | solution.py:213
  15.2 1.3 %copy-start.4 = (bf16[4,4,288,128]{3,2,1,0:T(8,128)(2,1)S(1)}, bf16[4,4,288,128]{3,2,1,0:T(8,128)(2,1)}, u32[]{:S(2)}) copy-start(bf16[4,4,288,128]{3,2,1,0:T(8,128)(2,1)} %get-tuple-element.32.turned) | copy-start | bytes 3538948
  16.5 4.5 %copy-start.6 = (bf16[576,128]{1,0:T(8,128)(2,1)S(1)}, bf16[576,128]{1,0:T(8,128)(2,1)}, u32[]{:S(2)}) copy-start(bf16[576,128]{1,0:T(8,128)(2,1)} %get-tuple-element.24.refs_0_.token) | copy-start | bytes 442372
  16.5 21.6 %collective-permute-start.6 = (bf16[576,128]{1,0:T(8,128)(2,1)S(1)}, bf16[576,128]{1,0:T(8,128)(2,1)S(1)}, u32[]{:S(2)}, u32[]{:S(2)}) collective-permute-start(bf16[576,128]{1,0:T(8,128)(2,1)S(1)} %get-tuple-element.35), channel_id=1, source_target_pairs={{0,2},{1,3},{2,0},{3,1},{4,6},{5,7},{6,4},{7,5},{8,10},{9,11},{10,... | collective-permute-start | bytes 442376 | tf_op jit(solution)/shard_map/ppermute | solution.py:51
  18.3 20.6 %collective-permute-start.7 = (bf16[576,128]{1,0:T(8,128)(2,1)S(1)}, bf16[576,128]{1,0:T(8,128)(2,1)S(1)}, u32[]{:S(2)}, u32[]{:S(2)}) collective-permute-start(bf16[576,128]{1,0:T(8,128)(2,1)S(1)} %get-tuple-element.36), channel_id=1, source_target_pairs={{0,1},{1,0},{2,3},{3,2},{4,5},{5,4},{6,7},{7,6},{8,9},{9,8},{10,11... | collective-permute-start | bytes 442376 | tf_op jit(solution)/shard_map/ppermute | solution.py:51
  20.7 18.1 %collective-permute-start.8 = (bf16[576,128]{1,0:T(8,128)(2,1)S(1)}, bf16[576,128]{1,0:T(8,128)(2,1)S(1)}, u32[]{:S(2)}, u32[]{:S(2)}) collective-permute-start(bf16[576,128]{1,0:T(8,128)(2,1)S(1)} %get-tuple-element.37), channel_id=1, source_target_pairs={{0,3},{1,2},{2,1},{3,0},{4,7},{5,6},{6,5},{7,4},{8,11},{9,10},{10,... | collective-permute-start | bytes 442376 | tf_op jit(solution)/shard_map/ppermute | solution.py:51
  23.2 21.7 %collective-permute-start.3 = (bf16[432,128]{1,0:T(8,128)(2,1)S(1)}, bf16[432,128]{1,0:T(8,128)(2,1)S(1)}, u32[]{:S(2)}, u32[]{:S(2)}) collective-permute-start(bf16[432,128]{1,0:T(8,128)(2,1)S(1)} %get-tuple-element.29), channel_id=1, source_target_pairs={{0,2},{1,3},{2,0},{3,1},{4,6},{5,7},{6,4},{7,5},{8,10},{9,11},{10,... | collective-permute-start | bytes 331784 | tf_op jit(solution)/shard_map/ppermute | solution.py:51
  29.3 15.9 %collective-permute-start.4 = (bf16[432,128]{1,0:T(8,128)(2,1)S(1)}, bf16[432,128]{1,0:T(8,128)(2,1)S(1)}, u32[]{:S(2)}, u32[]{:S(2)}) collective-permute-start(bf16[432,128]{1,0:T(8,128)(2,1)S(1)} %get-tuple-element.30), channel_id=1, source_target_pairs={{0,3},{1,2},{2,1},{3,0},{4,7},{5,6},{6,5},{7,4},{8,11},{9,10},{10,... | collective-permute-start | bytes 331784 | tf_op jit(solution)/shard_map/ppermute | solution.py:51
  34.5 19.4 %all-to-all-start.1 = ((bf16[8,3,16,1152]{3,2,1,0:T(8,128)(2,1)}), bf16[8,3,16,1152]{3,2,1,0:T(8,128)(2,1)S(1)}, u32[]{:S(2)}, u32[]{:S(2)}) async-start(bf16[8,3,16,1152]{3,2,1,0:T(8,128)(2,1)} %core_temporal.1), calls=%async_computation.1 | async-start | bytes 1769472 | tf_op jit(solution)/shard_map/all_to_all | solution.py:255
  38.1 7.1 %collective-permute-start.5 = (bf16[432,128]{1,0:T(8,128)(2,1)S(1)}, bf16[432,128]{1,0:T(8,128)(2,1)S(1)}, u32[]{:S(2)}, u32[]{:S(2)}) collective-permute-start(bf16[432,128]{1,0:T(8,128)(2,1)S(1)} %get-tuple-element.31), channel_id=1, source_target_pairs={{0,1},{1,0},{2,3},{3,2},{4,5},{5,4},{6,7},{7,6},{8,9},{9,8},{10,11... | collective-permute-start | bytes 331784 | tf_op jit(solution)/shard_map/ppermute | solution.py:51
  41.0 11.6 %collective-permute-start.9 = (bf16[432,128]{1,0:T(8,128)(2,1)S(1)}, bf16[432,128]{1,0:T(8,128)(2,1)S(1)}, u32[]{:S(2)}, u32[]{:S(2)}) collective-permute-start(bf16[432,128]{1,0:T(8,128)(2,1)S(1)} %get-tuple-element.39), channel_id=1, source_target_pairs={{0,2},{1,3},{2,0},{3,1},{4,6},{5,7},{6,4},{7,5},{8,10},{9,11},{10,... | collective-permute-start | bytes 331784 | tf_op jit(solution)/shard_map/ppermute | solution.py:51
  44.6 8.1 %collective-permute-start.10 = (bf16[432,128]{1,0:T(8,128)(2,1)S(1)}, bf16[432,128]{1,0:T(8,128)(2,1)S(1)}, u32[]{:S(2)}, u32[]{:S(2)}) collective-permute-start(bf16[432,128]{1,0:T(8,128)(2,1)S(1)} %get-tuple-element.40), channel_id=1, source_target_pairs={{0,3},{1,2},{2,1},{3,0},{4,7},{5,6},{6,5},{7,4},{8,11},{9,10},{10,... | collective-permute-start | bytes 331784 | tf_op jit(solution)/shard_map/ppermute | solution.py:51
  44.8 9.2 %collective-permute-start.11 = (bf16[432,128]{1,0:T(8,128)(2,1)S(1)}, bf16[432,128]{1,0:T(8,128)(2,1)S(1)}, u32[]{:S(2)}, u32[]{:S(2)}) collective-permute-start(bf16[432,128]{1,0:T(8,128)(2,1)S(1)} %get-tuple-element.41), channel_id=1, source_target_pairs={{0,1},{1,0},{2,3},{3,2},{4,5},{5,4},{6,7},{7,6},{8,9},{9,8},{10,11... | collective-permute-start | bytes 331784 | tf_op jit(solution)/shard_map/ppermute | solution.py:51

commit v3 on v2

--- a/solution.py
+++ b/solution.py
@@ -12,23 +12,21 @@
 SCALE = 1.0 / math.sqrt(HEAD_DIM)
 EXP2_SCALE = SCALE * math.log2(math.e)
 LANES = 128
-CHUNKS = 2
-REST_AFTER = True
-HOLD = True
-HEAD_GROUP = 8
-IN_ORDER = "213"
-OUT_ORDER = "231"
-SEND_ORDER = "desc"
+SPLIT = (2, 2)
+AHEAD = 1
+GATE = (1,)
+IN_ORDER = (3, 1, 2)
+OUT_ORDER = (2, 1, 3)
+HEAD_GROUP = 16
 COST = {"core_spatial0": 40, "core_spatial1": 15, "core_temporal": 3, "unpack": 3}
-AFTER = 1
-VM = {"pack_spatial": 62}
+VM = {"pack_spatial0": 62}
 
 NT = (((1,), (1,)), ((), ()))
 TN = (((0,), (0,)), ((), ()))
 VMEM_LIMIT = 48 * 1024 * 1024
 
 
-def call(name, kernel, out_shape, *, us=1.0, scratch=(), **specs):
+def call(name, kernel, out_shape, *, cost=1.0, scratch=(), **specs):
     return pl.pallas_call(
         kernel,
         out_shape=out_shape,
@@ -37,7 +35,7 @@
         name=name,
         compiler_params=pltpu.CompilerParams(vmem_limit_bytes=VM.get(name, 48) * 1024 * 1024),
         cost_estimate=pl.CostEstimate(
-            flops=int(COST.get(name, us) * 1e9), bytes_accessed=1024, transcendentals=0
+            flops=int(COST.get(name, cost) * 1e9), bytes_accessed=1024, transcendentals=0
         ),
     )
 
@@ -51,35 +49,28 @@
     return lax.ppermute(array, axis, [(i, i ^ distance) for i in range(size)])
 
 
-def cut_messages(turned, outs, group, chunks, wanted):
-    me = lax.axis_index("space")
-    rows = turned.shape[2] // chunks
-    for n, c in enumerate(wanted):
-        for d in range(group):
-            for a in range(4):
-                block = turned[a, me ^ d]
-                outs[n * group + d][a * rows : (a + 1) * rows] = block[c * rows : (c + 1) * rows]
-
-
-def spatial_pack_kernel(group, chunks, *refs):
-    sources, outs, turned = refs[:4], refs[4 : 4 + group], refs[-3]
-    staged, sems = refs[-2:]
+def spatial_pack_kernel(first, last, group, *refs):
+    sources, outs = refs[:4], refs[-3 - group : -3]
+    staged, turned, sems = refs[-3:]
+    start = first // LANES * LANES
     share = turned.shape[2]
     copies = [
-        pltpu.make_async_copy(sources[a].at[0], staged.at[a], sems.at[a]) for a in range(4)
+        pltpu.make_async_copy(
+            sources[a].at[0, :, start : start + staged.shape[2]], staged.at[a], sems.at[a]
+        )
+        for a in range(4)
     ]
     for copy in copies:
         copy.start()
     for a in range(4):
         copies[a].wait()
-        block = staged[a].T
+        block = staged[a].T[first - start : last - start]
         for d in range(group):
             turned[a, d] = block[d * share : (d + 1) * share]
-    cut_messages(turned, outs, group, chunks, [0])
-
-
-def spatial_pack_rest_kernel(group, chunks, turned, token, *outs):
-    cut_messages(turned, outs, group, chunks, range(1, chunks))
+    me = lax.axis_index("space")
+    for d in range(group):
+        for a in range(4):
+            outs[d][a * share : (a + 1) * share] = turned[a, me ^ d]
 
 
 def temporal_pack_kernel(q, k, v, g, token, out):
@@ -136,90 +127,93 @@
                 outs[k][row : row + HEAD_DIM] = low[:, k * per : (k + 1) * per]
 
 
-def unpack_kernel(places, chunks, *refs):
-    group = len(places)
-    messages, others = refs[: group * chunks], refs[group * chunks : -4]
-    scratch, turned, sems, other_sems = refs[-4:]
-    outs, slices = others[-3:], []
-    if len(others) > 3:
-        arrived, outs = others[0], others[1:4]
-        parts, _, rows, _ = arrived.shape
-        slices = [
-            pltpu.make_async_copy(
-                arrived.at[t, i], others[4 + i].at[0, t * rows : (t + 1) * rows], other_sems.at[t, i]
-            )
-            for i in range(3)
-            for t in range(parts)
-        ]
-    for copy in slices:
+def temporal_unpack_kernel(arrived, *refs):
+    outs, token, sems = refs[:3], refs[3], refs[4]
+    parts, _, rows, _ = arrived.shape
+    copies = [
+        pltpu.make_async_copy(
+            arrived.at[t, i], outs[i].at[0, t * rows : (t + 1) * rows], sems.at[t, i]
+        )
+        for i in range(3)
+        for t in range(parts)
+    ]
+    for copy in copies:
         copy.start()
-    share, tokens = scratch.shape[2:]
-    rows = share // chunks
+    token[...] = jnp.zeros_like(token)
+    for copy in copies:
+        copy.wait()
+
+
+def spatial_unpack_kernel(first, last, group, count, *refs):
+    messages, outs = refs[: group * count], refs[-5 - count : -2 - count]
+    scratch, turned, sems = refs[-2 - count : -2], refs[-2], refs[-1]
     me = lax.axis_index("space")
+    places = order(OUT_ORDER, group)
     copies = []
     for i in range(3):
-        for k, d in enumerate(places):
-            parts = [
-                messages[c * group + k][i * rows : (i + 1) * rows] for c in range(chunks)
-            ]
-            scratch[i, me ^ d] = jnp.concatenate(parts, axis=0)
-        turned[i] = scratch[i].reshape(group * share, tokens).T
-        copies.append(pltpu.make_async_copy(turned.at[i], outs[i].at[0], sems.at[i]))
+        blocks = []
+        for c in range(count):
+            rows = scratch[c].shape[2]
+            for k, d in enumerate(places):
+                scratch[c][i, me ^ d] = messages[c * group + k][i * rows : (i + 1) * rows]
+            blocks.append(scratch[c][i].reshape(group * rows, scratch[c].shape[3]))
+        turned[i] = jnp.concatenate(blocks, axis=0)[first:last].T
+        copies.append(
+            pltpu.make_async_copy(turned.at[i], outs[i].at[0, :, first:last], sems.at[i])
+        )
         copies[i].start()
-    for copy in copies + slices:
+    for copy in copies:
         copy.wait()
 
 
 def send(arrays):
     _, tokens, width = arrays[0].shape
     group, parts = lax.axis_size("space"), lax.axis_size("tm")
-    share = width // group
-    heads_here = share // HEAD_DIM
-    chunks = math.gcd(CHUNKS, heads_here)
+    heads_here = width // HEAD_DIM // group
+    split = SPLIT if sum(SPLIT) == heads_here else (heads_here,)
+    chunks = len(split)
     rows = tokens // parts
     hbm, vmem = pl.BlockSpec(memory_space=pltpu.HBM), pl.BlockSpec(memory_space=pltpu.VMEM)
-    message = bf16(4 * share // chunks, tokens)
-    *messages, turned = call(
-        "pack_spatial",
-        functools.partial(spatial_pack_kernel, group, chunks),
-        [message] * group + [bf16(4, group, share, tokens)],
-        in_specs=[hbm] * 4,
-        scratch=[
-            pltpu.VMEM((4, tokens, width), jnp.bfloat16),
-            pltpu.SemaphoreType.DMA((4,)),
-        ],
-    )(*arrays[:4])
+    later = pl.BlockSpec(memory_space=pl.ANY)
+
+    def pack(c, *after):
+        share = split[c] * HEAD_DIM
+        first = group * HEAD_DIM * sum(split[:c])
+        last = first + group * share
+        span = -(-last // LANES) * LANES - first // LANES * LANES
+        return call(
+            f"pack_spatial{c}",
+            functools.partial(spatial_pack_kernel, first, last, group),
+            [bf16(4 * share, tokens)] * group,
+            in_specs=[hbm] * 4 + [later] * len(after),
+            scratch=[
+                pltpu.VMEM((4, tokens, span), jnp.bfloat16),
+                pltpu.VMEM((4, group, share, tokens), jnp.bfloat16),
+                pltpu.SemaphoreType.DMA((4,)),
+            ],
+        )(*arrays[:4], *after)
+
+    messages = pack(0)
     if rows % 16 == 0:
         slices = call(
             "pack_temporal",
             temporal_pack_kernel,
             bf16(parts, 4, rows, width),
-            in_specs=[vmem] * 4 + [pl.BlockSpec(memory_space=pl.ANY)],
+            in_specs=[vmem] * 4 + [later],
         )(*arrays[4:], messages[0])
     else:
         slices = jnp.stack([x.reshape(parts, rows, width) for x in arrays[4:]], axis=1)
-    if chunks > 1:
-        messages += call(
-            "pack_rest",
-            functools.partial(spatial_pack_rest_kernel, group, chunks),
-            [message] * (group * (chunks - 1)),
-            in_specs=[vmem, pl.BlockSpec(memory_space=pl.ANY)],
-        )(turned, slices if REST_AFTER else messages[0])
+    for c in range(1, chunks):
+        messages += pack(c, slices)
     spatial = []
     for c in range(chunks):
         mine = messages[c * group : (c + 1) * group]
-        far = {d: swap(mine[d], "space", d) for d in order(SEND_ORDER, group)[1:]}
-        spatial.append([mine[0]] + [far[d] for d in range(1, group)])
+        spatial.append([mine[0]] + [swap(mine[d], "space", d) for d in range(1, group)])
     return spatial, lax.all_to_all(slices, "tm", 0, 0, tiled=True)
 
 
-def order(kind, group):
-    far = list(range(1, group))
-    if kind == "desc":
-        far = far[::-1]
-    elif kind != "asc" and len(kind) == group - 1:
-        far = [int(c) for c in kind]
-    return [0] + far
+def order(far, group):
+    return [0, *(far if len(far) == group - 1 else range(1, group))]
 
 
 def spatial_core(arrived, first):
@@ -237,7 +231,7 @@
             f"core_spatial{first + c}",
             functools.partial(spatial_core_kernel, heads),
             [bf16(3 * heads * HEAD_DIM, tokens)] * group,
-            us=1.2 * heads * (length / 512) ** 2,
+            cost=1.2 * heads * (length / 512) ** 2,
         )(*[messages[d] for d in places])
         )
     return [[chunk[places.index(d)] for d in range(group)] for chunk in results]
@@ -247,32 +241,56 @@
     chunks, group = len(spatial), len(spatial[0])
     tokens = spatial[0][0].shape[1]
     parts, _, rows, _ = temporal.shape
-    aligned = rows % 16 == 0
     places = order(OUT_ORDER, group)
     messages = [
-        mine[d] if d == 0 else swap(mine[d], "space", d) for mine in spatial for d in places
+        [mine[d] if d == 0 else swap(mine[d], "space", d) for d in places] for mine in spatial
     ]
     arrived = lax.all_to_all(temporal, "tm", 0, 0, tiled=True)
     hbm, vmem = pl.BlockSpec(memory_space=pltpu.HBM), pl.BlockSpec(memory_space=pltpu.VMEM)
-    outs = call(
-        "unpack",
-        functools.partial(unpack_kernel, places, chunks),
-        [bf16(1, tokens, width)] * (6 if aligned else 3),
-        in_specs=[vmem] * len(messages) + [pl.BlockSpec(memory_space=pl.ANY)] * aligned,
-        out_specs=[hbm] * (6 if aligned else 3),
-        scratch=[
-            pltpu.VMEM((3, group, width // group, tokens), jnp.bfloat16),
-            pltpu.VMEM((3, tokens, width), jnp.bfloat16),
-            pltpu.SemaphoreType.DMA((3,)),
-            pltpu.SemaphoreType.DMA((parts, 3)),
-        ],
-    )(*messages, *[arrived] * aligned)
-    if aligned:
-        return outs
-    return list(outs) + [arrived[:, i].reshape(1, tokens, width) for i in range(3)]
-
-
-def temporal_core_kernel(messages, token, out):
+    later = pl.BlockSpec(memory_space=pl.ANY)
+    whole = [bf16(1, tokens, width)] * 3
+
+    def unpack(name, first, last, mine, into, *after):
+        n = len(mine) * group
+        return call(
+            name,
+            functools.partial(spatial_unpack_kernel, first, last, group, len(mine)),
+            whole,
+            in_specs=[vmem] * n + [hbm] * len(into) + [later] * len(after),
+            out_specs=[hbm] * 3,
+            input_output_aliases={n + i: i for i in range(len(into))},
+            scratch=[
+                pltpu.VMEM((3, group, row[0].shape[0] // 3, tokens), jnp.bfloat16) for row in mine
+            ]
+            + [
+                pltpu.VMEM((3, tokens, last - first), jnp.bfloat16),
+                pltpu.SemaphoreType.DMA((3,)),
+            ],
+        )(*[m for row in mine for m in row], *into, *after)
+
+    edge, begun = 0, []
+    if chunks > 1:
+        edge = (width - group * spatial[-1][0].shape[0] // 3) // LANES * LANES
+        begun = unpack("unpack_early", 0, edge, messages[:-1], [])
+    if rows % 16 == 0:
+        *others, token = call(
+            "unpack_temporal",
+            temporal_unpack_kernel,
+            whole + [bf16(16, LANES)],
+            in_specs=[later],
+            out_specs=[hbm] * 3 + [vmem],
+            scratch=[pltpu.SemaphoreType.DMA((parts, 3))],
+        )(arrived)
+        after = [token]
+    else:
+        others = [arrived[:, i].reshape(1, tokens, width) for i in range(3)]
+        after = []
+    done = unpack("unpack", edge, width, messages, begun, *after)
+    return list(done) + list(others)
+
+
+def temporal_core_kernel(messages, *refs):
+    out = refs[-1]
     group, _, tok, width = messages.shape
     total = group * tok
     arrays = [
@@ -345,26 +363,29 @@
                     flush(t)
 
 
-def temporal_core(arrived, token):
+def temporal_core(arrived, after):
     group, _, rows, width = arrived.shape
     return call(
         "core_temporal",
         temporal_core_kernel,
         bf16(group, 3, rows, width),
-        us=3.4,
-        in_specs=[pl.BlockSpec(memory_space=pltpu.VMEM), pl.BlockSpec(memory_space=pl.ANY)],
-    )(arrived, token)
+        cost=3.4,
+        in_specs=[pl.BlockSpec(memory_space=pltpu.VMEM)]
+        + [pl.BlockSpec(memory_space=pl.ANY)] * len(after),
+    )(arrived, *after)
 
 
 def shards(*arrays):
     width = arrays[0].shape[2]
     spatial, temporal = send(arrays)
-    cut = min(AFTER, len(spatial))
+    cut = min(AHEAD, len(spatial))
     done = spatial_core(spatial[:cut], 0)
-    results = temporal_core(temporal, done[-1][0])
+    after = [done[-1][0]]
     if cut < len(spatial):
-        if HOLD:
-            spatial[cut][0], _ = lax.optimization_barrier((spatial[cut][0], results))
+        after += [spatial[cut][d] for d in GATE]
+    results = temporal_core(temporal, after)
+    if cut < len(spatial):
+        spatial[cut][0], _ = lax.optimization_barrier((spatial[cut][0], results))
         done += spatial_core(spatial[cut:], cut)
     return tuple(give_back(done, results, width))
 

time: 56 us -> 53.5 us (0.955)
  starting transfers between devices: 29.4 us -> 27.7 us
  local copies, waits for them, and re-layouts: 2.19 us -> 0.94 us
  Pallas kernels: 12.6 us -> 13.6 us
  waiting for transfers between devices: 10.8 us -> 10.1 us
    ppermute x12, waiting for transfers between devices: 8.75 us -> 3.16 us  [swap(): return lax.ppermute(array, axis, [(i, i ^ distance) for i in range(size)])]
    all_to_all x1, waiting for transfers between devices: 0.01 us -> 5.06 us  [give_back(): arrived = lax.all_to_all(temporal, 'tm', 0, 0, tiled=True)]
    ppermute x12, starting transfers between devices: 21.9 us -> 20.1 us  [swap(): return lax.ppermute(array, axis, [(i, i ^ distance) for i in range(size)])]
    unnamed x14 -> x20, local copies, waits for them, and re-layouts: 2.19 us -> 0.94 us
    pallas_call x3 -> x5, Pallas kernels: 4.59 us -> 5.79 us  [the longest x2 2.82 us: pack(): call(f'pack_spatial{c}', functools.partial(spatial_pack_kernel, first, la...]
  transfers between devices with their start and end apart: 14 -> 14, of which waited for: 3 -> 5; matrix products, arithmetic and copies ran while one was open for 0% -> 0% of each run, Pallas kernels for 14% -> 20%
where the time goes in v3:
time: 53.5 us; the launch traced here: 53.2 us
  starting transfers between devices  27.7 us (52%)
  Pallas kernels  13.6 us (25%)
  waiting for transfers between devices  10.1 us (19%)
  local copies, waits for them, and re-layouts  0.94 us (2%)
  between operations  0.8 us (1%)
    ppermute x12, starting transfers between devices, swap(): return lax.ppermute(array, axis, [(i, i ^ distance) for i in range(size)])  20.1 us
    all_to_all x1, waiting for transfers between devices, give_back(): arrived = lax.all_to_all(temporal, 'tm', 0, 0, tiled=True)  5.06 us
    pallas_call x2, Pallas kernels, spatial_core(): call(f'core_spatial{first + c}', functools.partial(spatial_core_kernel, h...  4.35 us
    all_to_all x1, starting transfers between devices, send(): return (spatial, lax.all_to_all(slices, 'tm', 0, 0, tiled=True))  4 us
    all_to_all x1, starting transfers between devices, give_back(): arrived = lax.all_to_all(temporal, 'tm', 0, 0, tiled=True)  3.55 us
    ppermute x12, waiting for transfers between devices, swap(): return lax.ppermute(array, axis, [(i, i ^ distance) for i in range(size)])  3.16 us
    pallas_call x2, Pallas kernels, pack(): call(f'pack_spatial{c}', functools.partial(spatial_pack_kernel, first, la...  2.82 us
    pallas_call x1, Pallas kernels, temporal_core(): call('core_temporal', temporal_core_kernel, bf16(group, 3, rows, width),...  2.36 us
  transfers between devices with their start and end apart: 14, of which 5 were waited for; matrix products, arithmetic and copies ran while one was open for 0% of the time, Pallas kernels for 20%

profile of v3, /device:TPU:0, one launch (start us, length us, event | category | flops | bytes accessed | tf_op | source)
XLA Modules:
  0.0 53.2 jit_solution(5112767097166725169)
XLA Ops:
  0.7 2.3 %pack_spatial0.1 = (bf16[576,128]{1,0:T(8,128)(2,1)}, bf16[576,128]{1,0:T(8,128)(2,1)}, bf16[576,128]{1,0:T(8,128)(2,1)}, bf16[576,128]{1,0:T(8,128)(2,1)}) custom-call(bf16[1,128,1152]{2,1,0:T(8,128)(2,1)} %refs_0_.3, bf16[1,128,1152]{2,1,0:T(8,128)(2,1)} %refs_1_.3, bf16[1,128,1152]{2,1,0:T(8,128)(2,1)} %refs_2_.3, bf16[1,128,1152]{2,1,0:T(8,128)(2,1)} %refs_3_.3), custom_call_target="tpu_custom_call" | custom-call | flops 1000000000 | bytes 1024 | tf_op jit(solution)/shard_map/pack_spatial0/pallas_call | solution.py:184
  2.9 5.1 %collective-permute-start = (bf16[576,128]{1,0:T(8,128)(2,1)}, bf16[576,128]{1,0:T(8,128)(2,1)S(1)}, u32[]{:S(2)}, u32[]{:S(2)}) collective-permute-start(bf16[576,128]{1,0:T(8,128)(2,1)} %get-tuple-element.34), channel_id=1, source_target_pairs={{0,3},{1,2},{2,1},{3,0},{4,7},{5,6},{6,5},{7,4},{8,11},{9,10},{10,... | collective-permute-start | bytes 442376 | tf_op jit(solution)/shard_map/ppermute | solution.py:49
  8.7 0.9 %copy-done.8 = bf16[576,128]{1,0:T(8,128)(2,1)S(1)} copy-done((bf16[576,128]{1,0:T(8,128)(2,1)S(1)}, bf16[576,128]{1,0:T(8,128)(2,1)}, u32[]{:S(2)}) %copy-start.8) | copy-done | bytes 147480
  9.6 1.1 %pack_temporal.1.refs_4_ = bf16[8,4,16,1152]{3,2,1,0:T(8,128)(2,1)} custom-call(bf16[1,128,1152]{2,1,0:T(8,128)(2,1)S(1)} %copy-done, bf16[1,128,1152]{2,1,0:T(8,128)(2,1)S(1)} %copy-done.1, bf16[1,128,1152]{2,1,0:T(8,128)(2,1)S(1)} %copy-done.2, bf16[1,128,1152]{2,1,0:T(8,128)(2,1)S(1)} %copy-done.3, bf16[576,128]{1,0:T(8,128)(2,1)S(1)} %copy-done.8), custom_call_target="tpu_custom_call" | custom-call | flops 1000000000 | bytes 1024 | tf_op jit(solution)/shard_map/pack_temporal/pallas_call | solution.py:198
  10.7 4.0 %all-to-all-start = ((bf16[8,4,16,1152]{3,2,1,0:T(8,128)(2,1)}), bf16[8,4,16,1152]{3,2,1,0:T(8,128)(2,1)S(1)}, u32[]{:S(2)}, u32[]{:S(2)}) async-start(bf16[8,4,16,1152]{3,2,1,0:T(8,128)(2,1)} %pack_temporal.1.refs_4_), calls=%async_computation | async-start | bytes 2359296 | tf_op jit(solution)/shard_map/all_to_all | solution.py:212
  15.4 1.3 %collective-permute-start.6 = (bf16[576,128]{1,0:T(8,128)(2,1)S(1)}, bf16[576,128]{1,0:T(8,128)(2,1)S(1)}, u32[]{:S(2)}, u32[]{:S(2)}) collective-permute-start(bf16[576,128]{1,0:T(8,128)(2,1)S(1)} %get-tuple-element.42), channel_id=1, source_target_pairs={{0,1},{1,0},{2,3},{3,2},{4,5},{5,4},{6,7},{7,6},{8,9},{9,8},{10,11... | collective-permute-start | bytes 442376 | tf_op jit(solution)/shard_map/ppermute | solution.py:49
  16.7 2.4 %collective-permute-start.7 = (bf16[576,128]{1,0:T(8,128)(2,1)S(1)}, bf16[576,128]{1,0:T(8,128)(2,1)S(1)}, u32[]{:S(2)}, u32[]{:S(2)}) collective-permute-start(bf16[576,128]{1,0:T(8,128)(2,1)S(1)} %get-tuple-element.44), channel_id=1, source_target_pairs={{0,3},{1,2},{2,1},{3,0},{4,7},{5,6},{6,5},{7,4},{8,11},{9,10},{10,... | collective-permute-start | bytes 442376 | tf_op jit(solution)/shard_map/ppermute | solution.py:49
  19.6 1.2 %collective-permute-done.2.refs_3_ = bf16[576,128]{1,0:T(8,128)(2,1)S(1)} collective-permute-done((bf16[576,128]{1,0:T(8,128)(2,1)}, bf16[576,128]{1,0:T(8,128)(2,1)S(1)}, u32[]{:S(2)}, u32[]{:S(2)}) %collective-permute-start.2) | collective-permute-done | bytes 147488 | tf_op jit(solution)/shard_map/ppermute | solution.py:49
  20.9 2.2 %core_spatial0.1 = (bf16[432,128]{1,0:T(8,128)(2,1)S(1)}, bf16[432,128]{1,0:T(8,128)(2,1)S(1)}, bf16[432,128]{1,0:T(8,128)(2,1)S(1)}, bf16[432,128]{1,0:T(8,128)(2,1)S(1)}) custom-call(bf16[576,128]{1,0:T(8,128)(2,1)S(1)} %copy-done.9, bf16[576,128]{1,0:T(8,128)(2,1)S(1)} %collective-permute-done.refs_1_, ...), custom_call_target="tpu_custom_call" | custom-call | flops 40000000000 | bytes 1024 | tf_op jit(solution)/shard_map/core_spatial0/pallas_call | solution.py:230
  23.0 1.3 %collective-permute-start.3 = (bf16[432,128]{1,0:T(8,128)(2,1)S(1)}, bf16[432,128]{1,0:T(8,128)(2,1)S(1)}, u32[]{:S(2)}, u32[]{:S(2)}) collective-permute-start(bf16[432,128]{1,0:T(8,128)(2,1)S(1)} %get-tuple-element.38), channel_id=1, source_target_pairs={{0,2},{1,3},{2,0},{3,1},{4,6},{5,7},{6,4},{7,5},{8,10},{9,11},{10,... | collective-permute-start | bytes 331784 | tf_op jit(solution)/shard_map/ppermute | solution.py:49
  24.3 1.8 %collective-permute-start.4 = (bf16[432,128]{1,0:T(8,128)(2,1)S(1)}, bf16[432,128]{1,0:T(8,128)(2,1)S(1)}, u32[]{:S(2)}, u32[]{:S(2)}) collective-permute-start(bf16[432,128]{1,0:T(8,128)(2,1)S(1)} %get-tuple-element.39), channel_id=1, source_target_pairs={{0,1},{1,0},{2,3},{3,2},{4,5},{5,4},{6,7},{7,6},{8,9},{9,8},{10,11... | collective-permute-start | bytes 331784 | tf_op jit(solution)/shard_map/ppermute | solution.py:49
  26.1 0.9 %collective-permute-done.6.refs_1_.refs_2_ = bf16[576,128]{1,0:T(8,128)(2,1)S(1)} collective-permute-done((bf16[576,128]{1,0:T(8,128)(2,1)S(1)}, bf16[576,128]{1,0:T(8,128)(2,1)S(1)}, u32[]{:S(2)}, u32[]{:S(2)}) %collective-permute-start.6) | collective-permute-done | bytes 147488 | tf_op jit(solution)/shard_map/ppermute | solution.py:49
  27.1 2.6 %collective-permute-start.5 = (bf16[432,128]{1,0:T(8,128)(2,1)S(1)}, bf16[432,128]{1,0:T(8,128)(2,1)S(1)}, u32[]{:S(2)}, u32[]{:S(2)}) collective-permute-start(bf16[432,128]{1,0:T(8,128)(2,1)S(1)} %get-tuple-element.40), channel_id=1, source_target_pairs={{0,3},{1,2},{2,1},{3,0},{4,7},{5,6},{6,5},{7,4},{8,11},{9,10},{10,... | collective-permute-start | bytes 331784 | tf_op jit(solution)/shard_map/ppermute | solution.py:49
  29.6 1.9 %all-to-all-done.messages = bf16[8,4,16,1152]{3,2,1,0:T(8,128)(2,1)S(1)} async-done(((bf16[8,4,16,1152]{3,2,1,0:T(8,128)(2,1)}), bf16[8,4,16,1152]{3,2,1,0:T(8,128)(2,1)S(1)}, u32[]{:S(2)}, u32[]{:S(2)}) %all-to-all-start) | async-done | bytes 1179680 | tf_op jit(solution)/shard_map/all_to_all | solution.py:212
  31.6 2.4 %core_temporal.1 = bf16[8,3,16,1152]{3,2,1,0:T(8,128)(2,1)} custom-call(bf16[8,4,16,1152]{3,2,1,0:T(8,128)(2,1)S(1)} %all-to-all-done.messages, bf16[432,128]{1,0:T(8,128)(2,1)S(1)} %get-tuple-element.37.refs_0_, bf16[576,128]{1,0:T(8,128)(2,1)S(1)} %collective-permute-done.6.refs_1_.refs_2_), custom_call_target="tpu_custom_call" | custom-call | flops 3000000000 | bytes 1024 | tf_op jit(solution)/shard_map/core_temporal/pallas_call | solution.py:368
  33.9 3.5 %all-to-all-start.1 = ((bf16[8,3,16,1152]{3,2,1,0:T(8,128)(2,1)}), bf16[8,3,16,1152]{3,2,1,0:T(8,128)(2,1)S(1)}, u32[]{:S(2)}, u32[]{:S(2)}) async-start(bf16[8,3,16,1152]{3,2,1,0:T(8,128)(2,1)} %core_temporal.1), calls=%async_computation.1 | async-start | bytes 1769472 | tf_op jit(solution)/shard_map/all_to_all | solution.py:248
  37.5 1.0 %collective-permute-done.8.refs_3_ = bf16[576,128]{1,0:T(8,128)(2,1)S(1)} collective-permute-done((bf16[576,128]{1,0:T(8,128)(2,1)S(1)}, bf16[576,128]{1,0:T(8,128)(2,1)S(1)}, u32[]{:S(2)}, u32[]{:S(2)}) %collective-permute-start.8) | collective-permute-done | bytes 147488 | tf_op jit(solution)/shard_map/ppermute | solution.py:49
  38.5 2.2 %core_spatial1.1 = (bf16[432,128]{1,0:T(8,128)(2,1)S(1)}, bf16[432,128]{1,0:T(8,128)(2,1)S(1)}, bf16[432,128]{1,0:T(8,128)(2,1)S(1)}, bf16[432,128]{1,0:T(8,128)(2,1)S(1)}) custom-call(bf16[576,128]{1,0:T(8,128)(2,1)S(1)} %get-tuple-element.43.refs_0_, bf16[576,128]{1,0:T(8,128)(2,1)S(1)} %collective-permute-done.7.refs_1_, ...), custom_call_target="tpu_custom_call" | custom-call | flops 15000000512 | bytes 1024 | tf_op jit(solution)/shard_map/core_spatial1/pallas_call | solution.py:230
  40.6 1.3 %collective-permute-start.9 = (bf16[432,128]{1,0:T(8,128)(2,1)S(1)}, bf16[432,128]{1,0:T(8,128)(2,1)S(1)}, u32[]{:S(2)}, u32[]{:S(2)}) collective-permute-start(bf16[432,128]{1,0:T(8,128)(2,1)S(1)} %get-tuple-element.47), channel_id=1, source_target_pairs={{0,2},{1,3},{2,0},{3,1},{4,6},{5,7},{6,4},{7,5},{8,10},{9,11},{10,... | collective-permute-start | bytes 331784 | tf_op jit(solution)/shard_map/ppermute | solution.py:49
  41.9 2.3 %collective-permute-start.10 = (bf16[432,128]{1,0:T(8,128)(2,1)S(1)}, bf16[432,128]{1,0:T(8,128)(2,1)S(1)}, u32[]{:S(2)}, u32[]{:S(2)}) collective-permute-start(bf16[432,128]{1,0:T(8,128)(2,1)S(1)} %get-tuple-element.48), channel_id=1, source_target_pairs={{0,1},{1,0},{2,3},{3,2},{4,5},{5,4},{6,7},{7,6},{8,9},{9,8},{10,11... | collective-permute-start | bytes 331784 | tf_op jit(solution)/shard_map/ppermute | solution.py:49
  45.1 0.9 %unpack_early.1 = (bf16[1,128,1152]{2,1,0:T(8,128)(2,1)}, bf16[1,128,1152]{2,1,0:T(8,128)(2,1)}, bf16[1,128,1152]{2,1,0:T(8,128)(2,1)}) custom-call(bf16[432,128]{1,0:T(8,128)(2,1)S(1)} %get-tuple-element.37.refs_0_, bf16[432,128]{1,0:T(8,128)(2,1)S(1)} %collective-permute-done.3.refs_1_, bf16[432,128]{1,0:T(8,128)(2,1)S(1)} %collective-permute-done.4.refs_2_, ...), custom_call_target="tpu_custom_call" | custom-call | flops 1000000000 | bytes 1024 | tf_op jit(solution)/shard_map/unpack_early/pallas_call | solution.py:255
  46.0 5.1 %all-to-all-done.1.arrived = bf16[8,3,16,1152]{3,2,1,0:T(8,128)(2,1)S(1)} async-done(((bf16[8,3,16,1152]{3,2,1,0:T(8,128)(2,1)}), bf16[8,3,16,1152]{3,2,1,0:T(8,128)(2,1)S(1)}, u32[]{:S(2)}, u32[]{:S(2)}) %all-to-all-start.1) | async-done | bytes 884768 | tf_op jit(solution)/shard_map/all_to_all | solution.py:248
  51.1 1.1 %unpack_temporal.1 = (bf16[1,128,1152]{2,1,0:T(8,128)(2,1)}, bf16[1,128,1152]{2,1,0:T(8,128)(2,1)}, bf16[1,128,1152]{2,1,0:T(8,128)(2,1)}, bf16[16,128]{1,0:T(8,128)(2,1)S(1)}) custom-call(bf16[8,3,16,1152]{3,2,1,0:T(8,128)(2,1)S(1)} %all-to-all-done.1.arrived), custom_call_target="tpu_custom_call" | custom-call | flops 1000000000 | bytes 1024 | tf_op jit(solution)/shard_map/unpack_temporal/pallas_call | solution.py:276
  52.2 1.0 %unpack.1 = (bf16[1,128,1152]{2,1,0:T(8,128)(2,1)}, bf16[1,128,1152]{2,1,0:T(8,128)(2,1)}, bf16[1,128,1152]{2,1,0:T(8,128)(2,1)}) custom-call(bf16[432,128]{1,0:T(8,128)(2,1)S(1)} %get-tuple-element.37.refs_0_, bf16[432,128]{1,0:T(8,128)(2,1)S(1)} %collective-permute-done.3.refs_1_, ...), custom_call_target="tpu_custom_call", output_to_operand_aliasing={{0}: (8, {}), {1}: (9, {}), {2}: (10, {})} | custom-call | flops 3000000000 | bytes 1024 | tf_op jit(solution)/shard_map/unpack/pallas_call | solution.py:255
  (33 shorter events, 2.6 us)
Async XLA Ops:
  0.6 8.1 %copy-start = (bf16[1,128,1152]{2,1,0:T(8,128)(2,1)S(1)}, bf16[1,128,1152]{2,1,0:T(8,128)(2,1)}, u32[]{:S(2)}) copy-start(bf16[1,128,1152]{2,1,0:T(8,128)(2,1)} %q.1) | copy-start | bytes 884740
  0.6 8.1 %copy-start.1 = (bf16[1,128,1152]{2,1,0:T(8,128)(2,1)S(1)}, bf16[1,128,1152]{2,1,0:T(8,128)(2,1)}, u32[]{:S(2)}) copy-start(bf16[1,128,1152]{2,1,0:T(8,128)(2,1)} %k.1) | copy-start | bytes 884740
  0.7 8.1 %copy-start.2 = (bf16[1,128,1152]{2,1,0:T(8,128)(2,1)S(1)}, bf16[1,128,1152]{2,1,0:T(8,128)(2,1)}, u32[]{:S(2)}) copy-start(bf16[1,128,1152]{2,1,0:T(8,128)(2,1)} %v.1) | copy-start | bytes 884740
  0.7 8.0 %copy-start.3 = (bf16[1,128,1152]{2,1,0:T(8,128)(2,1)S(1)}, bf16[1,128,1152]{2,1,0:T(8,128)(2,1)}, u32[]{:S(2)}) copy-start(bf16[1,128,1152]{2,1,0:T(8,128)(2,1)} %g.1) | copy-start | bytes 884740
  2.9 16.2 %collective-permute-start = (bf16[576,128]{1,0:T(8,128)(2,1)}, bf16[576,128]{1,0:T(8,128)(2,1)S(1)}, u32[]{:S(2)}, u32[]{:S(2)}) collective-permute-start(bf16[576,128]{1,0:T(8,128)(2,1)} %get-tuple-element.34), channel_id=1, source_target_pairs={{0,3},{1,2},{2,1},{3,0},{4,7},{5,6},{6,5},{7,4},{8,11},{9,10},{10,... | collective-permute-start | bytes 442376 | tf_op jit(solution)/shard_map/ppermute | solution.py:49
  8.1 11.6 %collective-permute-start.1 = (bf16[576,128]{1,0:T(8,128)(2,1)}, bf16[576,128]{1,0:T(8,128)(2,1)S(1)}, u32[]{:S(2)}, u32[]{:S(2)}) collective-permute-start(bf16[576,128]{1,0:T(8,128)(2,1)} %get-tuple-element.35), channel_id=1, source_target_pairs={{0,1},{1,0},{2,3},{3,2},{4,5},{5,4},{6,7},{7,6},{8,9},{9,8},{10,11... | collective-permute-start | bytes 442376 | tf_op jit(solution)/shard_map/ppermute | solution.py:49
  8.1 12.8 %collective-permute-start.2 = (bf16[576,128]{1,0:T(8,128)(2,1)}, bf16[576,128]{1,0:T(8,128)(2,1)S(1)}, u32[]{:S(2)}, u32[]{:S(2)}) collective-permute-start(bf16[576,128]{1,0:T(8,128)(2,1)} %get-tuple-element.36), channel_id=1, source_target_pairs={{0,2},{1,3},{2,0},{3,1},{4,6},{5,7},{6,4},{7,5},{8,10},{9,11},{10,... | collective-permute-start | bytes 442376 | tf_op jit(solution)/shard_map/ppermute | solution.py:49
  8.7 0.9 %copy-start.8 = (bf16[576,128]{1,0:T(8,128)(2,1)S(1)}, bf16[576,128]{1,0:T(8,128)(2,1)}, u32[]{:S(2)}) copy-start(bf16[576,128]{1,0:T(8,128)(2,1)} %get-tuple-element.33.refs_0_.token) | copy-start | bytes 442372
  10.7 4.0 %copy-start.4 = (bf16[1,128,1152]{2,1,0:T(8,128)(2,1)S(1)}, bf16[1,128,1152]{2,1,0:T(8,128)(2,1)}, u32[]{:S(2)}) copy-start(bf16[1,128,1152]{2,1,0:T(8,128)(2,1)} %refs_0_.3) | copy-start | bytes 884740
  10.7 4.0 %copy-start.5 = (bf16[1,128,1152]{2,1,0:T(8,128)(2,1)S(1)}, bf16[1,128,1152]{2,1,0:T(8,128)(2,1)}, u32[]{:S(2)}) copy-start(bf16[1,128,1152]{2,1,0:T(8,128)(2,1)} %refs_1_.3) | copy-start | bytes 884740
  10.7 4.0 %copy-start.6 = (bf16[1,128,1152]{2,1,0:T(8,128)(2,1)S(1)}, bf16[1,128,1152]{2,1,0:T(8,128)(2,1)}, u32[]{:S(2)}) copy-start(bf16[1,128,1152]{2,1,0:T(8,128)(2,1)} %refs_2_.3) | copy-start | bytes 884740
  10.7 4.0 %copy-start.7 = (bf16[1,128,1152]{2,1,0:T(8,128)(2,1)S(1)}, bf16[1,128,1152]{2,1,0:T(8,128)(2,1)}, u32[]{:S(2)}) copy-start(bf16[1,128,1152]{2,1,0:T(8,128)(2,1)} %refs_3_.3) | copy-start | bytes 884740
  10.7 20.8 %all-to-all-start = ((bf16[8,4,16,1152]{3,2,1,0:T(8,128)(2,1)}), bf16[8,4,16,1152]{3,2,1,0:T(8,128)(2,1)S(1)}, u32[]{:S(2)}, u32[]{:S(2)}) async-start(bf16[8,4,16,1152]{3,2,1,0:T(8,128)(2,1)} %pack_temporal.1.refs_4_), calls=%async_computation | async-start | bytes 2359296 | tf_op jit(solution)/shard_map/all_to_all | solution.py:212
  14.8 6.1 %copy-start.9 = (bf16[576,128]{1,0:T(8,128)(2,1)S(1)}, bf16[576,128]{1,0:T(8,128)(2,1)}, u32[]{:S(2)}) copy-start(bf16[576,128]{1,0:T(8,128)(2,1)} %get-tuple-element.33.refs_0_.token) | copy-start | bytes 442372
  15.4 11.7 %collective-permute-start.6 = (bf16[576,128]{1,0:T(8,128)(2,1)S(1)}, bf16[576,128]{1,0:T(8,128)(2,1)S(1)}, u32[]{:S(2)}, u32[]{:S(2)}) collective-permute-start(bf16[576,128]{1,0:T(8,128)(2,1)S(1)} %get-tuple-element.42), channel_id=1, source_target_pairs={{0,1},{1,0},{2,3},{3,2},{4,5},{5,4},{6,7},{7,6},{8,9},{9,8},{10,11... | collective-permute-start | bytes 442376 | tf_op jit(solution)/shard_map/ppermute | solution.py:49
  16.7 20.8 %collective-permute-start.7 = (bf16[576,128]{1,0:T(8,128)(2,1)S(1)}, bf16[576,128]{1,0:T(8,128)(2,1)S(1)}, u32[]{:S(2)}, u32[]{:S(2)}) collective-permute-start(bf16[576,128]{1,0:T(8,128)(2,1)S(1)} %get-tuple-element.44), channel_id=1, source_target_pairs={{0,3},{1,2},{2,1},{3,0},{4,7},{5,6},{6,5},{7,4},{8,11},{9,10},{10,... | collective-permute-start | bytes 442376 | tf_op jit(solution)/shard_map/ppermute | solution.py:49
  19.1 19.3 %collective-permute-start.8 = (bf16[576,128]{1,0:T(8,128)(2,1)S(1)}, bf16[576,128]{1,0:T(8,128)(2,1)S(1)}, u32[]{:S(2)}, u32[]{:S(2)}) collective-permute-start(bf16[576,128]{1,0:T(8,128)(2,1)S(1)} %get-tuple-element.45), channel_id=1, source_target_pairs={{0,2},{1,3},{2,0},{3,1},{4,6},{5,7},{6,4},{7,5},{8,10},{9,11},{10,... | collective-permute-start | bytes 442376 | tf_op jit(solution)/shard_map/ppermute | solution.py:49
  23.0 21.2 %collective-permute-start.3 = (bf16[432,128]{1,0:T(8,128)(2,1)S(1)}, bf16[432,128]{1,0:T(8,128)(2,1)S(1)}, u32[]{:S(2)}, u32[]{:S(2)}) collective-permute-start(bf16[432,128]{1,0:T(8,128)(2,1)S(1)} %get-tuple-element.38), channel_id=1, source_target_pairs={{0,2},{1,3},{2,0},{3,1},{4,6},{5,7},{6,4},{7,5},{8,10},{9,11},{10,... | collective-permute-start | bytes 331784 | tf_op jit(solution)/shard_map/ppermute | solution.py:49
  24.3 20.8 %collective-permute-start.4 = (bf16[432,128]{1,0:T(8,128)(2,1)S(1)}, bf16[432,128]{1,0:T(8,128)(2,1)S(1)}, u32[]{:S(2)}, u32[]{:S(2)}) collective-permute-start(bf16[432,128]{1,0:T(8,128)(2,1)S(1)} %get-tuple-element.39), channel_id=1, source_target_pairs={{0,1},{1,0},{2,3},{3,2},{4,5},{5,4},{6,7},{7,6},{8,9},{9,8},{10,11... | collective-permute-start | bytes 331784 | tf_op jit(solution)/shard_map/ppermute | solution.py:49
  27.1 18.0 %collective-permute-start.5 = (bf16[432,128]{1,0:T(8,128)(2,1)S(1)}, bf16[432,128]{1,0:T(8,128)(2,1)S(1)}, u32[]{:S(2)}, u32[]{:S(2)}) collective-permute-start(bf16[432,128]{1,0:T(8,128)(2,1)S(1)} %get-tuple-element.40), channel_id=1, source_target_pairs={{0,3},{1,2},{2,1},{3,0},{4,7},{5,6},{6,5},{7,4},{8,11},{9,10},{10,... | collective-permute-start | bytes 331784 | tf_op jit(solution)/shard_map/ppermute | solution.py:49
  33.9 17.1 %all-to-all-start.1 = ((bf16[8,3,16,1152]{3,2,1,0:T(8,128)(2,1)}), bf16[8,3,16,1152]{3,2,1,0:T(8,128)(2,1)S(1)}, u32[]{:S(2)}, u32[]{:S(2)}) async-start(bf16[8,3,16,1152]{3,2,1,0:T(8,128)(2,1)} %core_temporal.1), calls=%async_computation.1 | async-start | bytes 1769472 | tf_op jit(solution)/shard_map/all_to_all | solution.py:248
  40.6 11.6 %collective-permute-start.9 = (bf16[432,128]{1,0:T(8,128)(2,1)S(1)}, bf16[432,128]{1,0:T(8,128)(2,1)S(1)}, u32[]{:S(2)}, u32[]{:S(2)}) collective-permute-start(bf16[432,128]{1,0:T(8,128)(2,1)S(1)} %get-tuple-element.47), channel_id=1, source_target_pairs={{0,2},{1,3},{2,0},{3,1},{4,6},{5,7},{6,4},{7,5},{8,10},{9,11},{10,... | collective-permute-start | bytes 331784 | tf_op jit(solution)/shard_map/ppermute | solution.py:49
  41.9 10.3 %collective-permute-start.10 = (bf16[432,128]{1,0:T(8,128)(2,1)S(1)}, bf16[432,128]{1,0:T(8,128)(2,1)S(1)}, u32[]{:S(2)}, u32[]{:S(2)}) collective-permute-start(bf16[432,128]{1,0:T(8,128)(2,1)S(1)} %get-tuple-element.48), channel_id=1, source_target_pairs={{0,1},{1,0},{2,3},{3,2},{4,5},{5,4},{6,7},{7,6},{8,9},{9,8},{10,11... | collective-permute-start | bytes 331784 | tf_op jit(solution)/shard_map/ppermute | solution.py:49
  44.2 8.0 %collective-permute-start.11 = (bf16[432,128]{1,0:T(8,128)(2,1)S(1)}, bf16[432,128]{1,0:T(8,128)(2,1)S(1)}, u32[]{:S(2)}, u32[]{:S(2)}) collective-permute-start(bf16[432,128]{1,0:T(8,128)(2,1)S(1)} %get-tuple-element.49), channel_id=1, source_target_pairs={{0,3},{1,2},{2,1},{3,0},{4,7},{5,6},{6,5},{7,4},{8,11},{9,10},{10,... | collective-permute-start | bytes 331784 | tf_op jit(solution)/shard_map/ppermute | solution.py:49

commit v4 on v3

--- a/solution.py
+++ b/solution.py
@@ -118,13 +118,11 @@
             dqs[h].append(mm(ks[h], ds))
             dk[h] += nt(q[h], ds)
             dv[h] += nt(g[h], w)
-    for h in every:
-        dq = jnp.concatenate(dqs[h], axis=1)
-        for i, result in enumerate((dq * SCALE, dk[h] * SCALE, dv[h])):
-            low = result.astype(jnp.bfloat16)
-            row = (i * heads + h) * HEAD_DIM
-            for k in range(group):
-                outs[k][row : row + HEAD_DIM] = low[:, k * per : (k + 1) * per]
+    dq = [jnp.concatenate(x, axis=1) * SCALE for x in dqs]
+    dk = [x * SCALE for x in dk]
+    low = jnp.concatenate(dq + dk + dv, axis=0).astype(jnp.bfloat16)
+    for k in range(group):
+        outs[k][...] = low[:, k * per : (k + 1) * per]
 
 
 def temporal_unpack_kernel(arrived, *refs):

time: 53.5 us -> 53.5 us (level)
  transfers between devices with their start and end apart: 14 -> 14, of which waited for: 5 -> 5; matrix products, arithmetic and copies ran while one was open for 0% -> 0% of each run, Pallas kernels for 20% -> 19%
where the time goes in v4:
time: 53.5 us; the launch traced here: 53.2 us
  starting transfers between devices  27.7 us (52%)
  Pallas kernels  13.6 us (25%)
  waiting for transfers between devices  10.2 us (19%)
  local copies, waits for them, and re-layouts  0.94 us (2%)
  between operations  0.8 us (1%)
    ppermute x12, starting transfers between devices, swap(): return lax.ppermute(array, axis, [(i, i ^ distance) for i in range(size)])  20.1 us
    all_to_all x1, waiting for transfers between devices, give_back(): arrived = lax.all_to_all(temporal, 'tm', 0, 0, tiled=True)  5.07 us
    pallas_call x2, Pallas kernels, spatial_core(): call(f'core_spatial{first + c}', functools.partial(spatial_core_kernel, h...  4.33 us
    all_to_all x1, starting transfers between devices, send(): return (spatial, lax.all_to_all(slices, 'tm', 0, 0, tiled=True))  4 us
    all_to_all x1, starting transfers between devices, give_back(): arrived = lax.all_to_all(temporal, 'tm', 0, 0, tiled=True)  3.55 us
    ppermute x12, waiting for transfers between devices, swap(): return lax.ppermute(array, axis, [(i, i ^ distance) for i in range(size)])  3.16 us
    pallas_call x2, Pallas kernels, pack(): call(f'pack_spatial{c}', functools.partial(spatial_pack_kernel, first, la...  2.82 us
    pallas_call x1, Pallas kernels, temporal_core(): call('core_temporal', temporal_core_kernel, bf16(group, 3, rows, width),...  2.36 us
  transfers between devices with their start and end apart: 14, of which 5 were waited for; matrix products, arithmetic and copies ran while one was open for 0% of the time, Pallas kernels for 19%

profile of v4, /device:TPU:0, one launch (start us, length us, event | category | flops | bytes accessed | tf_op | source)
XLA Modules:
  0.0 53.2 jit_solution(728668407714994282)
XLA Ops:
  0.7 2.3 %pack_spatial0.1 = (bf16[576,128]{1,0:T(8,128)(2,1)}, bf16[576,128]{1,0:T(8,128)(2,1)}, bf16[576,128]{1,0:T(8,128)(2,1)}, bf16[576,128]{1,0:T(8,128)(2,1)}) custom-call(bf16[1,128,1152]{2,1,0:T(8,128)(2,1)} %refs_0_.3, bf16[1,128,1152]{2,1,0:T(8,128)(2,1)} %refs_1_.3, bf16[1,128,1152]{2,1,0:T(8,128)(2,1)} %refs_2_.3, bf16[1,128,1152]{2,1,0:T(8,128)(2,1)} %refs_3_.3), custom_call_target="tpu_custom_call" | custom-call | flops 1000000000 | bytes 1024 | tf_op jit(solution)/shard_map/pack_spatial0/pallas_call | solution.py:182
  2.9 5.1 %collective-permute-start = (bf16[576,128]{1,0:T(8,128)(2,1)}, bf16[576,128]{1,0:T(8,128)(2,1)S(1)}, u32[]{:S(2)}, u32[]{:S(2)}) collective-permute-start(bf16[576,128]{1,0:T(8,128)(2,1)} %get-tuple-element.34), channel_id=1, source_target_pairs={{0,3},{1,2},{2,1},{3,0},{4,7},{5,6},{6,5},{7,4},{8,11},{9,10},{10,... | collective-permute-start | bytes 442376 | tf_op jit(solution)/shard_map/ppermute | solution.py:49
  8.7 0.9 %copy-done.8 = bf16[576,128]{1,0:T(8,128)(2,1)S(1)} copy-done((bf16[576,128]{1,0:T(8,128)(2,1)S(1)}, bf16[576,128]{1,0:T(8,128)(2,1)}, u32[]{:S(2)}) %copy-start.8) | copy-done | bytes 147480
  9.6 1.1 %pack_temporal.1.refs_4_ = bf16[8,4,16,1152]{3,2,1,0:T(8,128)(2,1)} custom-call(bf16[1,128,1152]{2,1,0:T(8,128)(2,1)S(1)} %copy-done, bf16[1,128,1152]{2,1,0:T(8,128)(2,1)S(1)} %copy-done.1, bf16[1,128,1152]{2,1,0:T(8,128)(2,1)S(1)} %copy-done.2, bf16[1,128,1152]{2,1,0:T(8,128)(2,1)S(1)} %copy-done.3, bf16[576,128]{1,0:T(8,128)(2,1)S(1)} %copy-done.8), custom_call_target="tpu_custom_call" | custom-call | flops 1000000000 | bytes 1024 | tf_op jit(solution)/shard_map/pack_temporal/pallas_call | solution.py:196
  10.7 4.0 %all-to-all-start = ((bf16[8,4,16,1152]{3,2,1,0:T(8,128)(2,1)}), bf16[8,4,16,1152]{3,2,1,0:T(8,128)(2,1)S(1)}, u32[]{:S(2)}, u32[]{:S(2)}) async-start(bf16[8,4,16,1152]{3,2,1,0:T(8,128)(2,1)} %pack_temporal.1.refs_4_), calls=%async_computation | async-start | bytes 2359296 | tf_op jit(solution)/shard_map/all_to_all | solution.py:210
  15.4 1.3 %collective-permute-start.6 = (bf16[576,128]{1,0:T(8,128)(2,1)S(1)}, bf16[576,128]{1,0:T(8,128)(2,1)S(1)}, u32[]{:S(2)}, u32[]{:S(2)}) collective-permute-start(bf16[576,128]{1,0:T(8,128)(2,1)S(1)} %get-tuple-element.42), channel_id=1, source_target_pairs={{0,1},{1,0},{2,3},{3,2},{4,5},{5,4},{6,7},{7,6},{8,9},{9,8},{10,11... | collective-permute-start | bytes 442376 | tf_op jit(solution)/shard_map/ppermute | solution.py:49
  16.7 2.4 %collective-permute-start.7 = (bf16[576,128]{1,0:T(8,128)(2,1)S(1)}, bf16[576,128]{1,0:T(8,128)(2,1)S(1)}, u32[]{:S(2)}, u32[]{:S(2)}) collective-permute-start(bf16[576,128]{1,0:T(8,128)(2,1)S(1)} %get-tuple-element.44), channel_id=1, source_target_pairs={{0,3},{1,2},{2,1},{3,0},{4,7},{5,6},{6,5},{7,4},{8,11},{9,10},{10,... | collective-permute-start | bytes 442376 | tf_op jit(solution)/shard_map/ppermute | solution.py:49
  19.6 1.2 %collective-permute-done.2.refs_3_ = bf16[576,128]{1,0:T(8,128)(2,1)S(1)} collective-permute-done((bf16[576,128]{1,0:T(8,128)(2,1)}, bf16[576,128]{1,0:T(8,128)(2,1)S(1)}, u32[]{:S(2)}, u32[]{:S(2)}) %collective-permute-start.2) | collective-permute-done | bytes 147488 | tf_op jit(solution)/shard_map/ppermute | solution.py:49
  20.9 2.2 %core_spatial0.1 = (bf16[432,128]{1,0:T(8,128)(2,1)S(1)}, bf16[432,128]{1,0:T(8,128)(2,1)S(1)}, bf16[432,128]{1,0:T(8,128)(2,1)S(1)}, bf16[432,128]{1,0:T(8,128)(2,1)S(1)}) custom-call(bf16[576,128]{1,0:T(8,128)(2,1)S(1)} %copy-done.9, bf16[576,128]{1,0:T(8,128)(2,1)S(1)} %collective-permute-done.refs_1_, ...), custom_call_target="tpu_custom_call" | custom-call | flops 40000000000 | bytes 1024 | tf_op jit(solution)/shard_map/core_spatial0/pallas_call | solution.py:228
  23.0 1.3 %collective-permute-start.3 = (bf16[432,128]{1,0:T(8,128)(2,1)S(1)}, bf16[432,128]{1,0:T(8,128)(2,1)S(1)}, u32[]{:S(2)}, u32[]{:S(2)}) collective-permute-start(bf16[432,128]{1,0:T(8,128)(2,1)S(1)} %get-tuple-element.38), channel_id=1, source_target_pairs={{0,2},{1,3},{2,0},{3,1},{4,6},{5,7},{6,4},{7,5},{8,10},{9,11},{10,... | collective-permute-start | bytes 331784 | tf_op jit(solution)/shard_map/ppermute | solution.py:49
  24.3 1.8 %collective-permute-start.4 = (bf16[432,128]{1,0:T(8,128)(2,1)S(1)}, bf16[432,128]{1,0:T(8,128)(2,1)S(1)}, u32[]{:S(2)}, u32[]{:S(2)}) collective-permute-start(bf16[432,128]{1,0:T(8,128)(2,1)S(1)} %get-tuple-element.39), channel_id=1, source_target_pairs={{0,1},{1,0},{2,3},{3,2},{4,5},{5,4},{6,7},{7,6},{8,9},{9,8},{10,11... | collective-permute-start | bytes 331784 | tf_op jit(solution)/shard_map/ppermute | solution.py:49
  26.1 0.9 %collective-permute-done.6.refs_1_.refs_2_ = bf16[576,128]{1,0:T(8,128)(2,1)S(1)} collective-permute-done((bf16[576,128]{1,0:T(8,128)(2,1)S(1)}, bf16[576,128]{1,0:T(8,128)(2,1)S(1)}, u32[]{:S(2)}, u32[]{:S(2)}) %collective-permute-start.6) | collective-permute-done | bytes 147488 | tf_op jit(solution)/shard_map/ppermute | solution.py:49
  27.1 2.6 %collective-permute-start.5 = (bf16[432,128]{1,0:T(8,128)(2,1)S(1)}, bf16[432,128]{1,0:T(8,128)(2,1)S(1)}, u32[]{:S(2)}, u32[]{:S(2)}) collective-permute-start(bf16[432,128]{1,0:T(8,128)(2,1)S(1)} %get-tuple-element.40), channel_id=1, source_target_pairs={{0,3},{1,2},{2,1},{3,0},{4,7},{5,6},{6,5},{7,4},{8,11},{9,10},{10,... | collective-permute-start | bytes 331784 | tf_op jit(solution)/shard_map/ppermute | solution.py:49
  29.6 1.9 %all-to-all-done.messages = bf16[8,4,16,1152]{3,2,1,0:T(8,128)(2,1)S(1)} async-done(((bf16[8,4,16,1152]{3,2,1,0:T(8,128)(2,1)}), bf16[8,4,16,1152]{3,2,1,0:T(8,128)(2,1)S(1)}, u32[]{:S(2)}, u32[]{:S(2)}) %all-to-all-start) | async-done | bytes 1179680 | tf_op jit(solution)/shard_map/all_to_all | solution.py:210
  31.6 2.4 %core_temporal.1 = bf16[8,3,16,1152]{3,2,1,0:T(8,128)(2,1)} custom-call(bf16[8,4,16,1152]{3,2,1,0:T(8,128)(2,1)S(1)} %all-to-all-done.messages, bf16[432,128]{1,0:T(8,128)(2,1)S(1)} %get-tuple-element.37.refs_0_, bf16[576,128]{1,0:T(8,128)(2,1)S(1)} %collective-permute-done.6.refs_1_.refs_2_), custom_call_target="tpu_custom_call" | custom-call | flops 3000000000 | bytes 1024 | tf_op jit(solution)/shard_map/core_temporal/pallas_call | solution.py:366
  33.9 3.5 %all-to-all-start.1 = ((bf16[8,3,16,1152]{3,2,1,0:T(8,128)(2,1)}), bf16[8,3,16,1152]{3,2,1,0:T(8,128)(2,1)S(1)}, u32[]{:S(2)}, u32[]{:S(2)}) async-start(bf16[8,3,16,1152]{3,2,1,0:T(8,128)(2,1)} %core_temporal.1), calls=%async_computation.1 | async-start | bytes 1769472 | tf_op jit(solution)/shard_map/all_to_all | solution.py:246
  37.5 1.0 %collective-permute-done.8.refs_3_ = bf16[576,128]{1,0:T(8,128)(2,1)S(1)} collective-permute-done((bf16[576,128]{1,0:T(8,128)(2,1)S(1)}, bf16[576,128]{1,0:T(8,128)(2,1)S(1)}, u32[]{:S(2)}, u32[]{:S(2)}) %collective-permute-start.8) | collective-permute-done | bytes 147488 | tf_op jit(solution)/shard_map/ppermute | solution.py:49
  38.5 2.2 %core_spatial1.1 = (bf16[432,128]{1,0:T(8,128)(2,1)S(1)}, bf16[432,128]{1,0:T(8,128)(2,1)S(1)}, bf16[432,128]{1,0:T(8,128)(2,1)S(1)}, bf16[432,128]{1,0:T(8,128)(2,1)S(1)}) custom-call(bf16[576,128]{1,0:T(8,128)(2,1)S(1)} %get-tuple-element.43.refs_0_, bf16[576,128]{1,0:T(8,128)(2,1)S(1)} %collective-permute-done.7.refs_1_, ...), custom_call_target="tpu_custom_call" | custom-call | flops 15000000512 | bytes 1024 | tf_op jit(solution)/shard_map/core_spatial1/pallas_call | solution.py:228
  40.6 1.3 %collective-permute-start.9 = (bf16[432,128]{1,0:T(8,128)(2,1)S(1)}, bf16[432,128]{1,0:T(8,128)(2,1)S(1)}, u32[]{:S(2)}, u32[]{:S(2)}) collective-permute-start(bf16[432,128]{1,0:T(8,128)(2,1)S(1)} %get-tuple-element.47), channel_id=1, source_target_pairs={{0,2},{1,3},{2,0},{3,1},{4,6},{5,7},{6,4},{7,5},{8,10},{9,11},{10,... | collective-permute-start | bytes 331784 | tf_op jit(solution)/shard_map/ppermute | solution.py:49
  41.9 2.3 %collective-permute-start.10 = (bf16[432,128]{1,0:T(8,128)(2,1)S(1)}, bf16[432,128]{1,0:T(8,128)(2,1)S(1)}, u32[]{:S(2)}, u32[]{:S(2)}) collective-permute-start(bf16[432,128]{1,0:T(8,128)(2,1)S(1)} %get-tuple-element.48), channel_id=1, source_target_pairs={{0,1},{1,0},{2,3},{3,2},{4,5},{5,4},{6,7},{7,6},{8,9},{9,8},{10,11... | collective-permute-start | bytes 331784 | tf_op jit(solution)/shard_map/ppermute | solution.py:49
  45.1 0.9 %unpack_early.1 = (bf16[1,128,1152]{2,1,0:T(8,128)(2,1)}, bf16[1,128,1152]{2,1,0:T(8,128)(2,1)}, bf16[1,128,1152]{2,1,0:T(8,128)(2,1)}) custom-call(bf16[432,128]{1,0:T(8,128)(2,1)S(1)} %get-tuple-element.37.refs_0_, bf16[432,128]{1,0:T(8,128)(2,1)S(1)} %collective-permute-done.3.refs_1_, bf16[432,128]{1,0:T(8,128)(2,1)S(1)} %collective-permute-done.4.refs_2_, ...), custom_call_target="tpu_custom_call" | custom-call | flops 1000000000 | bytes 1024 | tf_op jit(solution)/shard_map/unpack_early/pallas_call | solution.py:253
  46.0 5.1 %all-to-all-done.1.arrived = bf16[8,3,16,1152]{3,2,1,0:T(8,128)(2,1)S(1)} async-done(((bf16[8,3,16,1152]{3,2,1,0:T(8,128)(2,1)}), bf16[8,3,16,1152]{3,2,1,0:T(8,128)(2,1)S(1)}, u32[]{:S(2)}, u32[]{:S(2)}) %all-to-all-start.1) | async-done | bytes 884768 | tf_op jit(solution)/shard_map/all_to_all | solution.py:246
  51.1 1.1 %unpack_temporal.1 = (bf16[1,128,1152]{2,1,0:T(8,128)(2,1)}, bf16[1,128,1152]{2,1,0:T(8,128)(2,1)}, bf16[1,128,1152]{2,1,0:T(8,128)(2,1)}, bf16[16,128]{1,0:T(8,128)(2,1)S(1)}) custom-call(bf16[8,3,16,1152]{3,2,1,0:T(8,128)(2,1)S(1)} %all-to-all-done.1.arrived), custom_call_target="tpu_custom_call" | custom-call | flops 1000000000 | bytes 1024 | tf_op jit(solution)/shard_map/unpack_temporal/pallas_call | solution.py:274
  52.2 1.0 %unpack.1 = (bf16[1,128,1152]{2,1,0:T(8,128)(2,1)}, bf16[1,128,1152]{2,1,0:T(8,128)(2,1)}, bf16[1,128,1152]{2,1,0:T(8,128)(2,1)}) custom-call(bf16[432,128]{1,0:T(8,128)(2,1)S(1)} %get-tuple-element.37.refs_0_, bf16[432,128]{1,0:T(8,128)(2,1)S(1)} %collective-permute-done.3.refs_1_, ...), custom_call_target="tpu_custom_call", output_to_operand_aliasing={{0}: (8, {}), {1}: (9, {}), {2}: (10, {})} | custom-call | flops 3000000000 | bytes 1024 | tf_op jit(solution)/shard_map/unpack/pallas_call | solution.py:253
  (33 shorter events, 2.6 us)
Async XLA Ops:
  0.6 8.1 %copy-start = (bf16[1,128,1152]{2,1,0:T(8,128)(2,1)S(1)}, bf16[1,128,1152]{2,1,0:T(8,128)(2,1)}, u32[]{:S(2)}) copy-start(bf16[1,128,1152]{2,1,0:T(8,128)(2,1)} %q.1) | copy-start | bytes 884740
  0.6 8.1 %copy-start.1 = (bf16[1,128,1152]{2,1,0:T(8,128)(2,1)S(1)}, bf16[1,128,1152]{2,1,0:T(8,128)(2,1)}, u32[]{:S(2)}) copy-start(bf16[1,128,1152]{2,1,0:T(8,128)(2,1)} %k.1) | copy-start | bytes 884740
  0.7 8.1 %copy-start.2 = (bf16[1,128,1152]{2,1,0:T(8,128)(2,1)S(1)}, bf16[1,128,1152]{2,1,0:T(8,128)(2,1)}, u32[]{:S(2)}) copy-start(bf16[1,128,1152]{2,1,0:T(8,128)(2,1)} %v.1) | copy-start | bytes 884740
  0.7 8.0 %copy-start.3 = (bf16[1,128,1152]{2,1,0:T(8,128)(2,1)S(1)}, bf16[1,128,1152]{2,1,0:T(8,128)(2,1)}, u32[]{:S(2)}) copy-start(bf16[1,128,1152]{2,1,0:T(8,128)(2,1)} %g.1) | copy-start | bytes 884740
  2.9 16.2 %collective-permute-start = (bf16[576,128]{1,0:T(8,128)(2,1)}, bf16[576,128]{1,0:T(8,128)(2,1)S(1)}, u32[]{:S(2)}, u32[]{:S(2)}) collective-permute-start(bf16[576,128]{1,0:T(8,128)(2,1)} %get-tuple-element.34), channel_id=1, source_target_pairs={{0,3},{1,2},{2,1},{3,0},{4,7},{5,6},{6,5},{7,4},{8,11},{9,10},{10,... | collective-permute-start | bytes 442376 | tf_op jit(solution)/shard_map/ppermute | solution.py:49
  8.1 11.6 %collective-permute-start.1 = (bf16[576,128]{1,0:T(8,128)(2,1)}, bf16[576,128]{1,0:T(8,128)(2,1)S(1)}, u32[]{:S(2)}, u32[]{:S(2)}) collective-permute-start(bf16[576,128]{1,0:T(8,128)(2,1)} %get-tuple-element.35), channel_id=1, source_target_pairs={{0,1},{1,0},{2,3},{3,2},{4,5},{5,4},{6,7},{7,6},{8,9},{9,8},{10,11... | collective-permute-start | bytes 442376 | tf_op jit(solution)/shard_map/ppermute | solution.py:49
  8.1 12.8 %collective-permute-start.2 = (bf16[576,128]{1,0:T(8,128)(2,1)}, bf16[576,128]{1,0:T(8,128)(2,1)S(1)}, u32[]{:S(2)}, u32[]{:S(2)}) collective-permute-start(bf16[576,128]{1,0:T(8,128)(2,1)} %get-tuple-element.36), channel_id=1, source_target_pairs={{0,2},{1,3},{2,0},{3,1},{4,6},{5,7},{6,4},{7,5},{8,10},{9,11},{10,... | collective-permute-start | bytes 442376 | tf_op jit(solution)/shard_map/ppermute | solution.py:49
  8.7 0.9 %copy-start.8 = (bf16[576,128]{1,0:T(8,128)(2,1)S(1)}, bf16[576,128]{1,0:T(8,128)(2,1)}, u32[]{:S(2)}) copy-start(bf16[576,128]{1,0:T(8,128)(2,1)} %get-tuple-element.33.refs_0_.token) | copy-start | bytes 442372
  10.7 4.0 %copy-start.4 = (bf16[1,128,1152]{2,1,0:T(8,128)(2,1)S(1)}, bf16[1,128,1152]{2,1,0:T(8,128)(2,1)}, u32[]{:S(2)}) copy-start(bf16[1,128,1152]{2,1,0:T(8,128)(2,1)} %refs_0_.3) | copy-start | bytes 884740
  10.7 4.0 %copy-start.5 = (bf16[1,128,1152]{2,1,0:T(8,128)(2,1)S(1)}, bf16[1,128,1152]{2,1,0:T(8,128)(2,1)}, u32[]{:S(2)}) copy-start(bf16[1,128,1152]{2,1,0:T(8,128)(2,1)} %refs_1_.3) | copy-start | bytes 884740
  10.7 4.0 %copy-start.6 = (bf16[1,128,1152]{2,1,0:T(8,128)(2,1)S(1)}, bf16[1,128,1152]{2,1,0:T(8,128)(2,1)}, u32[]{:S(2)}) copy-start(bf16[1,128,1152]{2,1,0:T(8,128)(2,1)} %refs_2_.3) | copy-start | bytes 884740
  10.7 4.0 %copy-start.7 = (bf16[1,128,1152]{2,1,0:T(8,128)(2,1)S(1)}, bf16[1,128,1152]{2,1,0:T(8,128)(2,1)}, u32[]{:S(2)}) copy-start(bf16[1,128,1152]{2,1,0:T(8,128)(2,1)} %refs_3_.3) | copy-start | bytes 884740
  10.7 20.8 %all-to-all-start = ((bf16[8,4,16,1152]{3,2,1,0:T(8,128)(2,1)}), bf16[8,4,16,1152]{3,2,1,0:T(8,128)(2,1)S(1)}, u32[]{:S(2)}, u32[]{:S(2)}) async-start(bf16[8,4,16,1152]{3,2,1,0:T(8,128)(2,1)} %pack_temporal.1.refs_4_), calls=%async_computation | async-start | bytes 2359296 | tf_op jit(solution)/shard_map/all_to_all | solution.py:210
  14.8 6.1 %copy-start.9 = (bf16[576,128]{1,0:T(8,128)(2,1)S(1)}, bf16[576,128]{1,0:T(8,128)(2,1)}, u32[]{:S(2)}) copy-start(bf16[576,128]{1,0:T(8,128)(2,1)} %get-tuple-element.33.refs_0_.token) | copy-start | bytes 442372
  15.4 11.7 %collective-permute-start.6 = (bf16[576,128]{1,0:T(8,128)(2,1)S(1)}, bf16[576,128]{1,0:T(8,128)(2,1)S(1)}, u32[]{:S(2)}, u32[]{:S(2)}) collective-permute-start(bf16[576,128]{1,0:T(8,128)(2,1)S(1)} %get-tuple-element.42), channel_id=1, source_target_pairs={{0,1},{1,0},{2,3},{3,2},{4,5},{5,4},{6,7},{7,6},{8,9},{9,8},{10,11... | collective-permute-start | bytes 442376 | tf_op jit(solution)/shard_map/ppermute | solution.py:49
  16.7 20.8 %collective-permute-start.7 = (bf16[576,128]{1,0:T(8,128)(2,1)S(1)}, bf16[576,128]{1,0:T(8,128)(2,1)S(1)}, u32[]{:S(2)}, u32[]{:S(2)}) collective-permute-start(bf16[576,128]{1,0:T(8,128)(2,1)S(1)} %get-tuple-element.44), channel_id=1, source_target_pairs={{0,3},{1,2},{2,1},{3,0},{4,7},{5,6},{6,5},{7,4},{8,11},{9,10},{10,... | collective-permute-start | bytes 442376 | tf_op jit(solution)/shard_map/ppermute | solution.py:49
  19.1 19.3 %collective-permute-start.8 = (bf16[576,128]{1,0:T(8,128)(2,1)S(1)}, bf16[576,128]{1,0:T(8,128)(2,1)S(1)}, u32[]{:S(2)}, u32[]{:S(2)}) collective-permute-start(bf16[576,128]{1,0:T(8,128)(2,1)S(1)} %get-tuple-element.45), channel_id=1, source_target_pairs={{0,2},{1,3},{2,0},{3,1},{4,6},{5,7},{6,4},{7,5},{8,10},{9,11},{10,... | collective-permute-start | bytes 442376 | tf_op jit(solution)/shard_map/ppermute | solution.py:49
  23.0 21.2 %collective-permute-start.3 = (bf16[432,128]{1,0:T(8,128)(2,1)S(1)}, bf16[432,128]{1,0:T(8,128)(2,1)S(1)}, u32[]{:S(2)}, u32[]{:S(2)}) collective-permute-start(bf16[432,128]{1,0:T(8,128)(2,1)S(1)} %get-tuple-element.38), channel_id=1, source_target_pairs={{0,2},{1,3},{2,0},{3,1},{4,6},{5,7},{6,4},{7,5},{8,10},{9,11},{10,... | collective-permute-start | bytes 331784 | tf_op jit(solution)/shard_map/ppermute | solution.py:49
  24.3 20.8 %collective-permute-start.4 = (bf16[432,128]{1,0:T(8,128)(2,1)S(1)}, bf16[432,128]{1,0:T(8,128)(2,1)S(1)}, u32[]{:S(2)}, u32[]{:S(2)}) collective-permute-start(bf16[432,128]{1,0:T(8,128)(2,1)S(1)} %get-tuple-element.39), channel_id=1, source_target_pairs={{0,1},{1,0},{2,3},{3,2},{4,5},{5,4},{6,7},{7,6},{8,9},{9,8},{10,11... | collective-permute-start | bytes 331784 | tf_op jit(solution)/shard_map/ppermute | solution.py:49
  27.1 18.0 %collective-permute-start.5 = (bf16[432,128]{1,0:T(8,128)(2,1)S(1)}, bf16[432,128]{1,0:T(8,128)(2,1)S(1)}, u32[]{:S(2)}, u32[]{:S(2)}) collective-permute-start(bf16[432,128]{1,0:T(8,128)(2,1)S(1)} %get-tuple-element.40), channel_id=1, source_target_pairs={{0,3},{1,2},{2,1},{3,0},{4,7},{5,6},{6,5},{7,4},{8,11},{9,10},{10,... | collective-permute-start | bytes 331784 | tf_op jit(solution)/shard_map/ppermute | solution.py:49
  33.9 17.1 %all-to-all-start.1 = ((bf16[8,3,16,1152]{3,2,1,0:T(8,128)(2,1)}), bf16[8,3,16,1152]{3,2,1,0:T(8,128)(2,1)S(1)}, u32[]{:S(2)}, u32[]{:S(2)}) async-start(bf16[8,3,16,1152]{3,2,1,0:T(8,128)(2,1)} %core_temporal.1), calls=%async_computation.1 | async-start | bytes 1769472 | tf_op jit(solution)/shard_map/all_to_all | solution.py:246
  40.6 11.6 %collective-permute-start.9 = (bf16[432,128]{1,0:T(8,128)(2,1)S(1)}, bf16[432,128]{1,0:T(8,128)(2,1)S(1)}, u32[]{:S(2)}, u32[]{:S(2)}) collective-permute-start(bf16[432,128]{1,0:T(8,128)(2,1)S(1)} %get-tuple-element.47), channel_id=1, source_target_pairs={{0,2},{1,3},{2,0},{3,1},{4,6},{5,7},{6,4},{7,5},{8,10},{9,11},{10,... | collective-permute-start | bytes 331784 | tf_op jit(solution)/shard_map/ppermute | solution.py:49
  41.9 10.3 %collective-permute-start.10 = (bf16[432,128]{1,0:T(8,128)(2,1)S(1)}, bf16[432,128]{1,0:T(8,128)(2,1)S(1)}, u32[]{:S(2)}, u32[]{:S(2)}) collective-permute-start(bf16[432,128]{1,0:T(8,128)(2,1)S(1)} %get-tuple-element.48), channel_id=1, source_target_pairs={{0,1},{1,0},{2,3},{3,2},{4,5},{5,4},{6,7},{7,6},{8,9},{9,8},{10,11... | collective-permute-start | bytes 331784 | tf_op jit(solution)/shard_map/ppermute | solution.py:49
  44.2 8.0 %collective-permute-start.11 = (bf16[432,128]{1,0:T(8,128)(2,1)S(1)}, bf16[432,128]{1,0:T(8,128)(2,1)S(1)}, u32[]{:S(2)}, u32[]{:S(2)}) collective-permute-start(bf16[432,128]{1,0:T(8,128)(2,1)S(1)} %get-tuple-element.49), channel_id=1, source_target_pairs={{0,3},{1,2},{2,1},{3,0},{4,7},{5,6},{6,5},{7,4},{8,11},{9,10},{10,... | collective-permute-start | bytes 331784 | tf_op jit(solution)/shard_map/ppermute | solution.py:49
